TPU v7x, 32 devices: a whole 2x2x4 slice. The times are simulated.
32 devices in a mesh: group: 2 (over x), cell: 16 (over z, y, core).
Axes of the slice: x: 2, y: 2, z: 4, core: 2. Of those that a mesh axis runs over, the one named last changes fastest.
Arguments:
- cell_factor: bfloat16 [32768, 128], P(('group', 'cell')), parts along dimension 0, may hold values from -6 to 6
- sched_factor: bfloat16 [16384, 128], P('group'), parts along dimension 0, may hold values from -6 to 6
- core_matrix: float32 [256, 128], P('group'), parts along dimension 0, may hold values from -0.03125 to 0.03125
- rate_table: bfloat16 [64, 128], replicated, may hold values from 0.5 to 2
- cell_well: int32 [32768], P(('group', 'cell')), parts along dimension 0, may hold values from 0 to 63
- sched_profile: int32 [16384], P('group'), parts along dimension 0, may hold values from 0 to 127
Outputs:
- basis_cells: float32 [32768, 256], P(('group', 'cell')), parts along dimension 0
- basis_sched: float32 [16384, 256], P(('group', 'cell')), parts along dimension 0
- core_out: float32 [512, 256], P('group'), parts along dimension 0
There are 2 independent parts, one for each index of `group`. A program takes and returns all parts, laid end to end along the dimension named above; an argument that names none is the same for every part. Nothing has to cross between parts.
All inputs are finite; a program needn't handle non-finite values.
Results may differ from a plain program's by a relative error of at most 0.02.
Values may be sent and summed in bfloat16 or wider, within the bound.
No kernel may reach another device: no remote copies, remote signals or barrier semaphores. Data moves between devices by JAX's collectives and lax.ppermute only.
A program may use at most 128 MiB of HBM per device.

v0:
```python
import jax
import jax.numpy as jnp
from jax import lax
from jax.experimental import pallas as pl
from jax.experimental.pallas import tpu as pltpu
from jax.sharding import PartitionSpec as P

TIME_STEP = 0.25
PANEL_SCALE = 8.0
HI = lax.Precision.HIGHEST
f32, bf16, i32 = jnp.float32, jnp.bfloat16, jnp.int32


def dot(a, b, ca, cb, precision=None):
    return lax.dot_general(
        a, b, (((ca,), (cb,)), ((), ())), precision=precision, preferred_element_type=f32
    )


def split(x):
    hi = x.astype(bf16)
    return hi, (x - hi.astype(f32)).astype(bf16)


def swap(x, mask, n):
    return lax.ppermute(x, "cell", [(i, i ^ mask) for i in range(n)])


def all_sum(x, n):
    me = lax.axis_index("cell")
    bits = n.bit_length() - 1
    half = x.shape[0] // 2
    odd = (me & 1) == 1
    lo, hi = x[:half], x[half:]
    mine = jnp.where(odd, hi, lo) + swap(jnp.where(odd, lo, hi), 1, n)
    for bit in range(1, bits):
        mine = mine + swap(mine, 1 << bit, n)
    other = swap(mine, 1, n)
    return jnp.concatenate([jnp.where(odd, other, mine), jnp.where(odd, mine, other)], axis=0)


def state_kernel(ck, cl, block_ref, slot_ref, c_hbm, s_hbm, core_hbm, table_hbm, well_hbm, prof_hbm,
                 k_ref, gram_ref, send_l, send_m, hold_l, hold_m,
                 c_ref, s_ref, core_ref, table_ref, well_ref, prof_ref,
                 g_ref, ft_ref, ps_ref, kt_ref, both_ref, inj_ref, l_ref, m_ref, sems, out_sems):
    n, blk, rank = s_ref.shape
    cells = c_ref.shape[0]
    half = n // 2
    wells, profiles = table_ref.shape
    copies = [
        pltpu.make_async_copy(src, dst, sems.at[i])
        for i, (src, dst) in enumerate(
            [(c_hbm, c_ref), (core_hbm, core_ref), (s_hbm, s_ref), (prof_hbm, prof_ref),
             (table_hbm, table_ref), (well_hbm, well_ref)]
        )
    ]
    for copy in copies:
        copy.start()
    kt_ref[...] = jnp.zeros_like(kt_ref)
    ps_ref[...] = jnp.zeros_like(ps_ref)
    copies[0].wait()
    copies[1].wait()
    c = c_ref[...]
    core = core_ref[...]
    c1 = core.astype(bf16)
    c2, c3 = split(core - c1.astype(f32))
    ft_ref[...] = (dot(c, c1, 1, 0) + dot(c, c2, 1, 0) + dot(c, c3, 1, 0)).T.astype(bf16)
    for copy in copies[2:]:
        copy.wait()

    def first(b, carry):
        s = s_ref[b]
        r = dot(s, ft_ref[...], 1, 0)
        g = (r * ((1.0 + TIME_STEP) - TIME_STEP * (r * r))).astype(bf16)
        g_ref[b] = g
        kt_ref[...] += dot(s, g, 0, 0)
        ps_ref[...] += dot(onehot(prof_ref[b], profiles, blk), s, 1, 0)
        return carry

    lax.fori_loop(0, n, first, 0, unroll=2)

    table = table_ref[...]
    wt = onehot(well_ref[...], wells, cells)
    ps_hi, ps_lo = split(ps_ref[...])
    tp_hi, tp_lo = split(dot(table, ps_hi, 1, 0) + dot(table, ps_lo, 1, 0))
    kt = (kt_ref[...] + TIME_STEP * (dot(tp_hi, wt, 0, 0) + dot(tp_lo, wt, 0, 0))) * ck
    k = kt.T
    k_ref[...] = k
    ct = c.astype(f32).T.astype(bf16)
    kt_hi, kt_lo = split(kt)
    k_hi, k_lo = split(k)
    both_ref[:, :rank] = c
    both_ref[:, rank:] = k_hi
    w_hi, w_lo = split(dot(wt, both_ref[...], 1, 0))
    a_hi, a_lo = split(TIME_STEP * (dot(table, w_hi, 0, 0) + dot(table, w_lo, 0, 0)))
    inj_ref[:profiles, :] = a_hi
    inj_ref[profiles:, :] = a_lo
    gram_ref[:rank, :] = dot(ct, c, 1, 0)
    gram_ref[rank : 2 * rank, :] = dot(ct, k_hi, 1, 0) + dot(ct, k_lo, 1, 0)
    gram_ref[2 * rank :, :] = dot(kt_hi, k_hi, 1, 0) + (dot(kt_hi, k_lo, 1, 0) + dot(kt_lo, k_hi, 1, 0))

    def outgoing(j, at, dst_l, dst_m):
        return (
            pltpu.make_async_copy(l_ref.at[j], dst_l.at[at], out_sems.at[0, j]),
            pltpu.make_async_copy(m_ref.at[j], dst_m.at[slot_ref[at]], out_sems.at[1, j]),
        )

    def second(first_slot, dst_l, dst_m):
        def body(at, carry):
            j = first_slot + at
            b = block_ref[j]
            hot = onehot(prof_ref[b], profiles, blk)
            out = dot(g_ref[b], both_ref[...], 1, 0) + dot(
                jnp.concatenate([hot, hot], axis=0), inj_ref[...], 0, 0
            )
            l_ref[j] = (out[:, :rank] * cl).astype(bf16)
            m_ref[j] = out[:, rank:].astype(bf16)
            for copy in outgoing(j, at, dst_l, dst_m):
                copy.start()
            return carry

        lax.fori_loop(0, half, body, 0)

    def finish(first_slot, dst_l, dst_m):
        def body(at, carry):
            for copy in outgoing(first_slot + at, at, dst_l, dst_m):
                copy.wait()
            return carry

        lax.fori_loop(0, half, body, 0)

    second(half, send_l, send_m)
    second(0, hold_l, hold_m)
    finish(half, send_l, send_m)
    finish(0, hold_l, hold_m)


def onehot(ids, size, count):
    return jnp.where(lax.broadcasted_iota(i32, (size, count), 0) == ids, 1.0, 0.0).astype(bf16)


def fold_kernel(keep_l, came_l, keep_m, came_m, after, send_l, hold_l, send_m, hold_m):
    half = hold_l.shape[0]
    for keep, came, send, hold in ((keep_l, came_l, send_l, hold_l), (keep_m, came_m, send_m, hold_m)):
        for j in range(half):
            hold[j] = (keep[j].astype(f32) + came[j].astype(f32)).astype(bf16)
            send[j] = (keep[half + j].astype(f32) + came[half + j].astype(f32)).astype(bf16)


def pair_kernel(keep_l, came_l, keep_m, came_m, after, l_ref, sums_ref):
    rank = l_ref.shape[1]
    l = keep_l[0].astype(f32) + came_l[0].astype(f32)
    m2 = keep_m[0].astype(f32) + came_m[0].astype(f32)
    l_ref[...] = l
    sums_ref[:rank, :] = dot(l, l, 0, 0, HI)
    sums_ref[rank:, :] = dot(m2, l, 0, 0, HI)


def spread(row, col, m):
    return jnp.broadcast_to(row[:, col : col + 1], (8, m))


def eliminate(w_refs):
    m = w_refs[0].shape[0]

    def take(w, base):
        left = [jnp.broadcast_to(w[base + i : base + i + 1, :m], (8, m)) for i in range(8)]
        right = [jnp.broadcast_to(w[base + i : base + i + 1, m:], (8, m)) for i in range(8)]
        cell = [[spread(left[r], base + i, m) for i in range(r + 1)] for r in range(8)]
        return left, right, cell

    held = [take(w, 0) for w in w_refs]
    for base in range(0, m, 8):
        after = base + 8
        for at, w in enumerate(w_refs):
            left, right, cell = held[at]
            if after < m:
                next_left, next_right, next_cell = take(w, after)
            for i in range(8):
                inv = lax.rsqrt(cell[i][i])
                left[i] = left[i] * inv
                right[i] = right[i] * inv
                mult = [None] * 8
                for r in range(i + 1, 8):
                    mult[r] = cell[r][i] * inv
                for r in range(i + 1, 8):
                    for q in range(i + 1, r + 1):
                        cell[r][q] = cell[r][q] - mult[r] * mult[q]
                    left[r] = left[r] - mult[r] * left[i]
                    right[r] = right[r] - mult[r] * right[i]
                w[base + i : base + i + 1, :m] = left[i][:1, :]
                w[base + i : base + i + 1, m:] = right[i][:1, :]
                if after < m:
                    ahead = [spread(left[i], after + r, m) for r in range(8)]
                    for r in range(8):
                        for q in range(r + 1):
                            next_cell[r][q] = next_cell[r][q] - ahead[r] * ahead[q]
                        next_left[r] = next_left[r] - ahead[r] * left[i]
                        next_right[r] = next_right[r] - ahead[r] * right[i]
            if after + 8 < m:
                u = w[base:after, :]
                w[after + 8 :, :] -= dot(u[:, after + 8 : m], u, 0, 0, HI)
            if after < m:
                held[at] = (next_left, next_right, next_cell)


def load_gram(w, gram):
    m = gram.shape[0]
    row = lax.broadcasted_iota(i32, (m, m), 0)
    col = lax.broadcasted_iota(i32, (m, m), 1)
    w[:, :m] = gram
    w[:, m:] = jnp.where(row == col, 1.0, 0.0)


def upper(w):
    m = w.shape[0]
    row = lax.broadcasted_iota(i32, (m, m), 0)
    col = lax.broadcasted_iota(i32, (m, m), 1)
    return jnp.where(col >= row, w[:, :m], 0.0), jnp.where(col <= row, w[:, m:], 0.0)


def plans_lead_kernel(ss_ref, av_ref, w):
    load_gram(w, ss_ref[...])
    eliminate([w])
    av_ref[...] = upper(w)[1]


def lead_kernel(ratio, gram_ref, av_ref, lead_ref, w):
    m = av_ref.shape[0]
    load_gram(w, gram_ref[:m, :])
    av = av_ref[...]
    ck = gram_ref[m : 2 * m, :]
    l21v = dot(ck * ratio, av, 1, 1, HI)
    lead_ref[4] = av
    lead_ref[5] = l21v
    lead_ref[6] = dot(av, l21v, 0, 1, HI)
    lead_ref[7] = dot(l21v, l21v, 1, 1, HI)
    eliminate([w])
    a = upper(w)[1]
    l21u = dot(ck, a, 0, 1, HI)
    lead_ref[0] = a
    lead_ref[1] = l21u
    lead_ref[2] = dot(a, l21u, 0, 1, HI)
    lead_ref[3] = gram_ref[2 * m :, :] - dot(l21u, l21u, 1, 1, HI)


def cells_kernel(root, lead_ref, c_ref, k_ref, basis_ref, lt_ref, inv_ref, w):
    m = w.shape[0]
    load_gram(w, lead_ref[3])
    eliminate([w])
    lt, d = upper(w)
    lt_ref[...] = lt
    inv_ref[...] = d
    c = c_ref[...].astype(f32)
    basis_ref[:, :m] = dot(c, lead_ref[0], 1, 1, HI) * root
    basis_ref[:, m:] = dot(k_ref[...] - dot(c, lead_ref[2], 1, 0, HI), d, 1, 1, HI) * root


def plans_kernel(root, ck, cl, scale, sums_ref, lead_ref, ltu_ref, d_ref, s_ref, l_ref,
                 basis_ref, core_ref, w):
    m = w.shape[0]
    ll = sums_ref[:m, :]
    n22 = sums_ref[m:, :]
    load_gram(w, ll - lead_ref[7])
    eliminate([w])
    ltv, dv = upper(w)
    a, l21u, av, l21v, xv = (lead_ref[i] for i in (0, 1, 4, 5, 6))
    d = d_ref[...]
    own = s_ref[...].astype(f32)
    basis_ref[:, :m] = dot(own, av, 1, 1, HI) * root
    basis_ref[:, m:] = dot(l_ref[...] - dot(own, xv, 1, 0, HI), dv, 1, 1, HI) * root
    b = -dot(dot(d, l21u, 1, 0, HI), a, 1, 0, HI)
    e = dot(b, ll, 1, 0, HI) * (1.0 / cl) + dot(d, n22, 1, 0, HI) - dot(ltu_ref[...], xv, 1, 0, HI) * (1.0 / ck)
    core_ref[:m, :m] = dot(a, l21v, 1, 0, HI) * (scale / cl)
    core_ref[:m, m:] = dot(a, ltv, 1, 1, HI) * (scale / cl)
    core_ref[m:, :m] = dot(ltu_ref[...], av, 1, 1, HI) * (scale / ck)
    core_ref[m:, m:] = dot(e, dv, 1, 1, HI) * scale


def params(mib):
    return pltpu.CompilerParams(vmem_limit_bytes=mib << 20)


def local(cell_factor, sched_factor, core_matrix, rate_table, cell_well, sched_profile):
    cells_dev, rank = cell_factor.shape
    n_sched = sched_factor.shape[0]
    n = lax.axis_size("cell")
    n_cells = cells_dev * n
    profiles = rate_table.shape[1]
    me = lax.axis_index("cell")
    blk = n_sched // n
    bits = n.bit_length() - 1
    half = n // 2
    ck = PANEL_SCALE / n_sched
    cl = PANEL_SCALE / n_cells
    order_a = list(range(bits))
    order_b = [0, 2, 1] + order_a[3:] if bits > 2 else order_a
    rel = [sum(((j >> (bits - 1 - i)) & 1) << bit for i, bit in enumerate(order_a)) for j in range(n)]
    slots = [
        sum(((p >> bit) & 1) << (bits - 1 - i) for i, bit in enumerate(order_b)) % half for p in rel[:half]
    ]
    perm = jnp.array(rel, i32) ^ me
    vmem = pl.BlockSpec(memory_space=pltpu.VMEM)
    smem = pl.BlockSpec(memory_space=pltpu.SMEM)
    hbm = pl.BlockSpec(memory_space=pltpu.HBM)
    anywhere = pl.BlockSpec(memory_space=pl.ANY)

    def shape(dtype, *dims):
        return jax.ShapeDtypeStruct(dims, dtype)

    part = shape(bf16, half, blk, rank)
    k, gram, send_l, send_m, hold_l, hold_m = pl.pallas_call(
        lambda *refs: state_kernel(ck, cl, *refs),
        out_shape=(shape(f32, cells_dev, rank), shape(f32, 3 * rank, rank), part, part, part, part),
        in_specs=[smem] * 2 + [hbm] * 6,
        out_specs=(vmem,) * 2 + (hbm,) * 4,
        scratch_shapes=[
            pltpu.VMEM((cells_dev, rank), bf16),
            pltpu.VMEM((n, blk, rank), bf16),
            pltpu.VMEM((rank, rank), f32),
            pltpu.VMEM(rate_table.shape, bf16),
            pltpu.VMEM((1, cells_dev), i32),
            pltpu.VMEM((n, 1, blk), i32),
            pltpu.VMEM((n, blk, cells_dev), bf16),
            pltpu.VMEM((rank, cells_dev), bf16),
            pltpu.VMEM((profiles, rank), f32),
            pltpu.VMEM((rank, cells_dev), f32),
            pltpu.VMEM((cells_dev, 2 * rank), bf16),
            pltpu.VMEM((2 * profiles, 2 * rank), bf16),
            pltpu.VMEM((n, blk, rank), bf16),
            pltpu.VMEM((n, blk, rank), bf16),
            pltpu.SemaphoreType.DMA((6,)),
            pltpu.SemaphoreType.DMA((2, n)),
        ],
        compiler_params=params(60),
        name="state",
    )(
        perm, jnp.array(slots, i32), cell_factor, sched_factor.reshape(n, blk, rank), core_matrix,
        rate_table, cell_well.reshape(1, cells_dev), sched_profile.reshape(n, 1, blk),
    )
    sums = all_sum(gram, n)
    ss = dot(sched_factor, sched_factor, 0, 0)
    pair = pltpu.VMEM((rank, 2 * rank), f32)
    square = jax.ShapeDtypeStruct((rank, rank), f32)
    av = pl.pallas_call(
        plans_lead_kernel, out_shape=square, in_specs=[vmem], out_specs=vmem, scratch_shapes=[pair],
        compiler_params=params(16), name="plans_lead",
    )(ss)
    lead = pl.pallas_call(
        lambda *refs: lead_kernel(cl / ck, *refs),
        out_shape=jax.ShapeDtypeStruct((8, rank, rank), f32),
        in_specs=[vmem] * 2, out_specs=vmem, scratch_shapes=[pair],
        compiler_params=params(16), name="lead",
    )(sums, av)
    basis_cells, ltu, d = pl.pallas_call(
        lambda *refs: cells_kernel(float(n_cells) ** 0.5, *refs),
        out_shape=(shape(f32, cells_dev, 2 * rank), square, square),
        in_specs=[vmem] * 3, out_specs=(vmem,) * 3, scratch_shapes=[pair],
        compiler_params=params(16), name="cells",
    )(lead, cell_factor, k)
    waits = [gram, av] + [lead] * (bits - 3) + [d]
    for step in range(bits):
        came_l = swap(send_l, 1 << order_a[step], n)
        came_m = swap(send_m, 1 << order_b[step], n)
        args = (hold_l, came_l, hold_m, came_m, waits[step])
        specs = [vmem] * 4 + [anywhere]
        if step < bits - 1:
            part = shape(bf16, half >> (step + 1), blk, rank)
            send_l, hold_l, send_m, hold_m = pl.pallas_call(
                fold_kernel, out_shape=(part,) * 4, in_specs=specs, out_specs=(vmem,) * 4,
                compiler_params=params(16), name="fold",
            )(*args)
        else:
            lt, sums2 = pl.pallas_call(
                pair_kernel, out_shape=(shape(f32, blk, rank), shape(f32, 2 * rank, rank)),
                in_specs=specs, out_specs=(vmem,) * 2, compiler_params=params(16), name="pair",
            )(*args)
    sums2 = all_sum(sums2, n)
    own = lax.dynamic_slice_in_dim(sched_factor, me * blk, blk, 0)
    scale = rank / (float(n_cells) * float(n_sched)) ** 0.5
    basis_sched, core_out = pl.pallas_call(
        lambda *refs: plans_kernel(float(n_sched) ** 0.5, ck, cl, scale, *refs),
        out_shape=(
            jax.ShapeDtypeStruct((blk, 2 * rank), f32),
            jax.ShapeDtypeStruct((2 * rank, 2 * rank), f32),
        ),
        in_specs=[vmem] * 6, out_specs=(vmem,) * 2, scratch_shapes=[pair],
        compiler_params=params(16), name="plans",
    )(sums2, lead, ltu, d, own, lt)
    return (basis_cells, basis_sched, core_out)


def solution(mesh):
    return jax.shard_map(
        local,
        mesh=mesh,
        in_specs=(
            P(("group", "cell"), None),
            P("group", None),
            P("group", None),
            P(),
            P(("group", "cell")),
            P("group"),
        ),
        out_specs=(P(("group", "cell"), None), P(("group", "cell"), None), P("group", None)),
        check_vma=False,
    )
```

profile of v0, /device:TPU:0, one launch (start us, length us, event | category | flops | bytes accessed | tf_op | source)
XLA Modules:
  0.0 115.6 jit_solution(7293091163596310692)
XLA Ops:
  0.6 1.3 %broadcast_xor_fusion.refs_0_ = s32[16]{0:T(128)} fusion(s32[16]{0:T(128)} %constant.16.clone, s32[]{:T(128)S(6)} %axis_index.8), kind=kLoop, calls=%fused_computation.11 | loop fusion | flops 16 | bytes 132 | tf_op jit(solution)/shard_map/xor | solution.py:302
  1.9 24.9 %state.1 = (f32[1024,128]{1,0:T(8,128)}, f32[384,128]{1,0:T(8,128)}, bf16[8,512,128]{2,1,0:T(8,128)(2,1)}, bf16[8,512,128]{2,1,0:T(8,128)(2,1)}, bf16[8,512,128]...) custom-call(s32[16]{0:T(128)} %broadcast_xor_fusion.refs_0_, s32[8]{0:T(128)} %constant.17.clone.refs_1_, ...), custom_call_target="tpu_custom_call" | custom-call | tf_op jit(solution)/shard_map/state/pallas_call | solution.py:312
  27.4 1.0 slice_select_fusion
  28.8 2.4 %collective-permute-done = f32[192,128]{1,0:T(8,128)S(1)} collective-permute-done((f32[192,128]{1,0:T(8,128)S(1)}, f32[192,128]{1,0:T(8,128)S(1)}, u32[]{:S(2)}, u32[]{:S(2)}) %collective-permute-start) | collective-permute-done | bytes 98336 | tf_op jit(solution)/shard_map/ppermute | solution.py:26
  31.2 1.0 select_add_fusion
  32.2 2.9 %collective-permute-start.1 = (f32[192,128]{1,0:T(8,128)S(1)}, f32[192,128]{1,0:T(8,128)S(1)}, u32[]{:S(2)}, u32[]{:S(2)}) collective-permute-start(f32[192,128]{1,0:T(8,128)S(1)} %select_add_fusion), channel_id=1, source_target_pairs={{0,2},{1,3},{2,0},{3,1},{4,6},{5,7},{6,4},{7,5},{8,10},{9,11},{10,... | collective-permute-start | bytes 294920 | tf_op jit(solution)/shard_map/ppermute | solution.py:26
  35.1 3.1 %collective-permute-done.1 = f32[192,128]{1,0:T(8,128)S(1)} collective-permute-done((f32[192,128]{1,0:T(8,128)S(1)}, f32[192,128]{1,0:T(8,128)S(1)}, u32[]{:S(2)}, u32[]{:S(2)}) %collective-permute-start.1) | collective-permute-done | bytes 98336 | tf_op jit(solution)/shard_map/ppermute | solution.py:26
  38.2 1.9 %collective-permute-start.2 = (f32[192,128]{1,0:T(8,128)S(1)}, f32[192,128]{1,0:T(8,128)S(1)}, u32[]{:S(2)}, u32[]{:S(2)}) collective-permute-start(f32[192,128]{1,0:T(8,128)S(1)} %add.28), channel_id=1, source_target_pairs={{0,4},{1,5},{2,6},{3,7},{4,0},{5,1},{6,2},{7,3},{8,12},{9,13},{10,... | collective-permute-start | bytes 294920 | tf_op jit(solution)/shard_map/ppermute | solution.py:26
  40.1 0.9 copy-done
  41.1 1.2 %copy-done.2 = bf16[8,512,128]{2,1,0:T(8,128)(2,1)S(1)} copy-done((bf16[8,512,128]{2,1,0:T(8,128)(2,1)S(1)}, bf16[8,512,128]{2,1,0:T(8,128)(2,1)}, u32[]{:S(2)}) %copy-start.2) | copy-done | bytes 1048600
  42.3 1.2 %copy-done.3 = bf16[8,512,128]{2,1,0:T(8,128)(2,1)S(1)} copy-done((bf16[8,512,128]{2,1,0:T(8,128)(2,1)S(1)}, bf16[8,512,128]{2,1,0:T(8,128)(2,1)}, u32[]{:S(2)}) %copy-start.3) | copy-done | bytes 1048600
  44.0 1.6 %collective-permute-start.7 = (bf16[4,512,128]{2,1,0:T(8,128)(2,1)S(1)}, bf16[4,512,128]{2,1,0:T(8,128)(2,1)S(1)}, u32[]{:S(2)}, u32[]{:S(2)}) collective-permute-start(bf16[4,512,128]{2,1,0:T(8,128)(2,1)S(1)} %get-tuple-element.36), channel_id=1, source_target_pairs={{0,2},{1,3},{2,0},{3,1},{4,6},{5,7},{6,4},{7,5},{8,10},{9,11},{10,... | collective-permute-start | bytes 1572872 | tf_op jit(solution)/shard_map/ppermute | solution.py:26
  46.0 2.7 %collective-permute-start.3 = (f32[192,128]{1,0:T(8,128)S(1)}, f32[192,128]{1,0:T(8,128)S(1)}, u32[]{:S(2)}, u32[]{:S(2)}) collective-permute-start(f32[192,128]{1,0:T(8,128)S(1)} %add.29), channel_id=1, source_target_pairs={{0,8},{1,9},{2,10},{3,11},{4,12},{5,13},{6,14},{7,15},{8,0},{9,1},... | collective-permute-start | bytes 294920 | tf_op jit(solution)/shard_map/ppermute | solution.py:26
  48.7 9.5 %collective-permute-done.3 = f32[192,128]{1,0:T(8,128)S(1)} collective-permute-done((f32[192,128]{1,0:T(8,128)S(1)}, f32[192,128]{1,0:T(8,128)S(1)}, u32[]{:S(2)}, u32[]{:S(2)}) %collective-permute-start.3) | collective-permute-done | bytes 98336 | tf_op jit(solution)/shard_map/ppermute | solution.py:26
  58.3 0.8 fusion.ss_ref
  59.1 5.2 %plans_lead.1.refs_1_.after = f32[128,128]{1,0:T(8,128)S(1)} custom-call(f32[128,128]{1,0:T(8,128)S(1)} %fusion.ss_ref), custom_call_target="tpu_custom_call" | custom-call | tf_op jit(solution)/shard_map/plans_lead/pallas_call | solution.py:345
  64.5 0.7 collective-permute-start.10
  65.2 4.5 %collective-permute-start.9 = (bf16[2,512,128]{2,1,0:T(8,128)(2,1)S(1)}, bf16[2,512,128]{2,1,0:T(8,128)(2,1)S(1)}, u32[]{:S(2)}, u32[]{:S(2)}) collective-permute-start(bf16[2,512,128]{2,1,0:T(8,128)(2,1)S(1)} %get-tuple-element.40), channel_id=1, source_target_pairs={{0,4},{1,5},{2,6},{3,7},{4,0},{5,1},{6,2},{7,3},{8,12},{9,13},{10,... | collective-permute-start | bytes 786440 | tf_op jit(solution)/shard_map/ppermute | solution.py:26
  69.8 5.8 %lead.1.refs_0_.after.refs_1_ = f32[8,128,128]{2,1,0:T(8,128)S(1)} custom-call(f32[384,128]{1,0:T(8,128)S(1)} %pad_maximum_fusion.refs_0_, f32[128,128]{1,0:T(8,128)S(1)} %plans_lead.1.refs_1_.after), custom_call_target="tpu_custom_call" | custom-call | tf_op jit(solution)/shard_map/lead/pallas_call | solution.py:349
  75.6 0.8 collective-permute-done.9.came_l
  76.7 0.7 collective-permute-start.11
  77.4 2.3 %collective-permute-start.12 = (bf16[1,512,128]{2,1,0:T(8,128)(2,1)S(1)}, bf16[1,512,128]{2,1,0:T(8,128)(2,1)S(1)}, u32[]{:S(2)}, u32[]{:S(2)}) collective-permute-start(bf16[1,512,128]{2,1,0:T(8,128)(2,1)S(1)} %get-tuple-element.46), channel_id=1, source_target_pairs={{0,8},{1,9},{2,10},{3,11},{4,12},{5,13},{6,14},{7,15},{8,0},{9,1},... | collective-permute-start | bytes 393224 | tf_op jit(solution)/shard_map/ppermute | solution.py:26
  79.7 7.6 %cells.1 = (f32[1024,256]{1,0:T(8,128)}, f32[128,128]{1,0:T(8,128)S(1)}, f32[128,128]{1,0:T(8,128)S(1)}) custom-call(f32[8,128,128]{2,1,0:T(8,128)S(1)} %lead.1.refs_0_.after.refs_1_, bf16[1024,128]{1,0:T(8,128)(2,1)S(1)} %copy-done.1, f32[1024,128]{1,0:T(8,128)S(1)} %copy-done.4), custom_call_target="tpu_custom_call" | custom-call | tf_op jit(solution)/shard_map/cells/pallas_call | solution.py:355
  87.4 2.2 %collective-permute-done.11.came_l = bf16[1,512,128]{2,1,0:T(8,128)(2,1)S(1)} collective-permute-done((bf16[1,512,128]{2,1,0:T(8,128)(2,1)S(1)}, bf16[1,512,128]{2,1,0:T(8,128)(2,1)S(1)}, u32[]{:S(2)}, u32[]{:S(2)}) %collective-permute-start.11) | collective-permute-done | bytes 131104 | tf_op jit(solution)/shard_map/ppermute | solution.py:26
  89.5 1.7 %collective-permute-done.12.came_m = bf16[1,512,128]{2,1,0:T(8,128)(2,1)S(1)} collective-permute-done((bf16[1,512,128]{2,1,0:T(8,128)(2,1)S(1)}, bf16[1,512,128]{2,1,0:T(8,128)(2,1)S(1)}, u32[]{:S(2)}, u32[]{:S(2)}) %collective-permute-start.12) | collective-permute-done | bytes 131104 | tf_op jit(solution)/shard_map/ppermute | solution.py:26
  92.0 1.2 %collective-permute-done.13 = f32[128,128]{1,0:T(8,128)S(1)} collective-permute-done((f32[128,128]{1,0:T(8,128)S(1)}, f32[128,128]{1,0:T(8,128)S(1)}, u32[]{:S(2)}, u32[]{:S(2)}) %collective-permute-start.13) | collective-permute-done | bytes 65568 | tf_op jit(solution)/shard_map/ppermute | solution.py:26
  93.2 1.6 %collective-permute-start.14 = (f32[128,128]{1,0:T(8,128)S(1)}, f32[128,128]{1,0:T(8,128)S(1)}, u32[]{:S(2)}, u32[]{:S(2)}) collective-permute-start(f32[128,128]{1,0:T(8,128)S(1)} %select_add_fusion.1), channel_id=1, source_target_pairs={{0,2},{1,3},{2,0},{3,1},{4,6},{5,7},{6,4},{7,5},{8,10},{9,11},{10,... | collective-permute-start | bytes 196616 | tf_op jit(solution)/shard_map/ppermute | solution.py:26
  94.8 2.7 %collective-permute-done.14 = f32[128,128]{1,0:T(8,128)S(1)} collective-permute-done((f32[128,128]{1,0:T(8,128)S(1)}, f32[128,128]{1,0:T(8,128)S(1)}, u32[]{:S(2)}, u32[]{:S(2)}) %collective-permute-start.14) | collective-permute-done | bytes 65568 | tf_op jit(solution)/shard_map/ppermute | solution.py:26
  97.6 4.3 %collective-permute-done.15 = f32[128,128]{1,0:T(8,128)S(1)} collective-permute-done((f32[128,128]{1,0:T(8,128)S(1)}, f32[128,128]{1,0:T(8,128)S(1)}, u32[]{:S(2)}, u32[]{:S(2)}) %collective-permute-start.15) | collective-permute-done | bytes 65568 | tf_op jit(solution)/shard_map/ppermute | solution.py:26
  102.0 5.3 %collective-permute-done.16 = f32[128,128]{1,0:T(8,128)S(1)} collective-permute-done((f32[128,128]{1,0:T(8,128)S(1)}, f32[128,128]{1,0:T(8,128)S(1)}, u32[]{:S(2)}, u32[]{:S(2)}) %collective-permute-start.16) | collective-permute-done | bytes 65568 | tf_op jit(solution)/shard_map/ppermute | solution.py:26
  107.4 0.9 constant_dynamic-slice_fusion.refs_4_
  108.7 7.0 %plans.1 = (f32[512,256]{1,0:T(8,128)}, f32[256,256]{1,0:T(8,128)}) custom-call(f32[256,128]{1,0:T(8,128)S(1)} %pad_maximum_fusion.1.refs_0_, f32[8,128,128]{2,1,0:T(8,128)S(1)} %lead.1.refs_0_.after.refs_1_, f32[128,128]{1,0:T(8,128)S(1)} %get-tuple-element.49.refs_2_, f32[128,128]{1,0:T(8,128)S(1)} %get-tuple-element.47.after.refs_3_, ...), custom_call_target="tpu_custom_call" | custom-call | tf_op jit(solution)/shard_map/plans/pallas_call | solution.py:381
  (42 shorter events, 4.1 us)
Async XLA Ops:
  26.8 13.3 %collective-permute-start.5 = (bf16[8,512,128]{2,1,0:T(8,128)(2,1)}, bf16[8,512,128]{2,1,0:T(8,128)(2,1)S(1)}, u32[]{:S(2)}, u32[]{:S(2)}) collective-permute-start(bf16[8,512,128]{2,1,0:T(8,128)(2,1)} %get-tuple-element.32), channel_id=1, source_target_pairs={{0,1},{1,0},{2,3},{3,2},{4,5},{5,4},{6,7},{7,6},{8,9},{9,8},{10,11... | collective-permute-start | bytes 3145736 | tf_op jit(solution)/shard_map/ppermute | solution.py:26
  27.3 12.8 %collective-permute-start.6 = (bf16[8,512,128]{2,1,0:T(8,128)(2,1)}, bf16[8,512,128]{2,1,0:T(8,128)(2,1)S(1)}, u32[]{:S(2)}, u32[]{:S(2)}) collective-permute-start(bf16[8,512,128]{2,1,0:T(8,128)(2,1)} %get-tuple-element.34), channel_id=1, source_target_pairs={{0,1},{1,0},{2,3},{3,2},{4,5},{5,4},{6,7},{7,6},{8,9},{9,8},{10,11... | collective-permute-start | bytes 3145736 | tf_op jit(solution)/shard_map/ppermute | solution.py:26
  28.3 2.9 %collective-permute-start = (f32[192,128]{1,0:T(8,128)S(1)}, f32[192,128]{1,0:T(8,128)S(1)}, u32[]{:S(2)}, u32[]{:S(2)}) collective-permute-start(f32[192,128]{1,0:T(8,128)S(1)} %slice_select_fusion), channel_id=1, source_target_pairs={{0,1},{1,0},{2,3},{3,2},{4,5},{5,4},{6,7},{7,6},{8,9},{9,8},{10,11... | collective-permute-start | bytes 294920 | tf_op jit(solution)/shard_map/ppermute | solution.py:26
  32.2 6.0 %collective-permute-start.1 = (f32[192,128]{1,0:T(8,128)S(1)}, f32[192,128]{1,0:T(8,128)S(1)}, u32[]{:S(2)}, u32[]{:S(2)}) collective-permute-start(f32[192,128]{1,0:T(8,128)S(1)} %select_add_fusion), channel_id=1, source_target_pairs={{0,2},{1,3},{2,0},{3,1},{4,6},{5,7},{6,4},{7,5},{8,10},{9,11},{10,... | collective-permute-start | bytes 294920 | tf_op jit(solution)/shard_map/ppermute | solution.py:26
  38.2 7.8 %collective-permute-start.2 = (f32[192,128]{1,0:T(8,128)S(1)}, f32[192,128]{1,0:T(8,128)S(1)}, u32[]{:S(2)}, u32[]{:S(2)}) collective-permute-start(f32[192,128]{1,0:T(8,128)S(1)} %add.28), channel_id=1, source_target_pairs={{0,4},{1,5},{2,6},{3,7},{4,0},{5,1},{6,2},{7,3},{8,12},{9,13},{10,... | collective-permute-start | bytes 294920 | tf_op jit(solution)/shard_map/ppermute | solution.py:26
  40.1 0.9 copy-start
  41.0 1.2 %copy-start.2 = (bf16[8,512,128]{2,1,0:T(8,128)(2,1)S(1)}, bf16[8,512,128]{2,1,0:T(8,128)(2,1)}, u32[]{:S(2)}) copy-start(bf16[8,512,128]{2,1,0:T(8,128)(2,1)} %get-tuple-element.31.keep_l) | copy-start | bytes 3145732
  42.3 1.2 %copy-start.3 = (bf16[8,512,128]{2,1,0:T(8,128)(2,1)S(1)}, bf16[8,512,128]{2,1,0:T(8,128)(2,1)}, u32[]{:S(2)}) copy-start(bf16[8,512,128]{2,1,0:T(8,128)(2,1)} %get-tuple-element.33.keep_m) | copy-start | bytes 3145732
  43.5 14.8 %copy-start.5 = (bf16[8192,128]{1,0:T(8,128)(2,1)S(1)}, bf16[8192,128]{1,0:T(8,128)(2,1)}, u32[]{:S(2)}) copy-start(bf16[8192,128]{1,0:T(8,128)(2,1)} %param.9) | copy-start | bytes 6291460
  44.0 20.3 %collective-permute-start.7 = (bf16[4,512,128]{2,1,0:T(8,128)(2,1)S(1)}, bf16[4,512,128]{2,1,0:T(8,128)(2,1)S(1)}, u32[]{:S(2)}, u32[]{:S(2)}) collective-permute-start(bf16[4,512,128]{2,1,0:T(8,128)(2,1)S(1)} %get-tuple-element.36), channel_id=1, source_target_pairs={{0,2},{1,3},{2,0},{3,1},{4,6},{5,7},{6,4},{7,5},{8,10},{9,11},{10,... | collective-permute-start | bytes 1572872 | tf_op jit(solution)/shard_map/ppermute | solution.py:26
  45.6 18.7 %collective-permute-start.8 = (bf16[4,512,128]{2,1,0:T(8,128)(2,1)S(1)}, bf16[4,512,128]{2,1,0:T(8,128)(2,1)S(1)}, u32[]{:S(2)}, u32[]{:S(2)}) collective-permute-start(bf16[4,512,128]{2,1,0:T(8,128)(2,1)S(1)} %get-tuple-element.38), channel_id=1, source_target_pairs={{0,4},{1,5},{2,6},{3,7},{4,0},{5,1},{6,2},{7,3},{8,12},{9,13},{10,... | collective-permute-start | bytes 1572872 | tf_op jit(solution)/shard_map/ppermute | solution.py:26
  46.0 12.2 %collective-permute-start.3 = (f32[192,128]{1,0:T(8,128)S(1)}, f32[192,128]{1,0:T(8,128)S(1)}, u32[]{:S(2)}, u32[]{:S(2)}) collective-permute-start(f32[192,128]{1,0:T(8,128)S(1)} %add.29), channel_id=1, source_target_pairs={{0,8},{1,9},{2,10},{3,11},{4,12},{5,13},{6,14},{7,15},{8,0},{9,1},... | collective-permute-start | bytes 294920 | tf_op jit(solution)/shard_map/ppermute | solution.py:26
  58.2 11.5 %collective-permute-start.4 = (f32[192,128]{1,0:T(8,128)S(1)}, f32[192,128]{1,0:T(8,128)S(1)}, u32[]{:S(2)}, u32[]{:S(2)}) collective-permute-start(f32[192,128]{1,0:T(8,128)S(1)} %add.30), channel_id=1, source_target_pairs={{0,1},{1,0},{2,3},{3,2},{4,5},{5,4},{6,7},{7,6},{8,9},{9,8},{10,11... | collective-permute-start | bytes 294920 | tf_op jit(solution)/shard_map/ppermute | solution.py:26
  64.5 15.2 %copy-start.1 = (bf16[1024,128]{1,0:T(8,128)(2,1)S(1)}, bf16[1024,128]{1,0:T(8,128)(2,1)}, u32[]{:S(2)}) copy-start(bf16[1024,128]{1,0:T(8,128)(2,1)} %refs_1_.2) | copy-start | bytes 786436
  64.5 15.2 %copy-start.4 = (f32[1024,128]{1,0:T(8,128)S(1)}, f32[1024,128]{1,0:T(8,128)}, u32[]{:S(2)}) copy-start(f32[1024,128]{1,0:T(8,128)} %get-tuple-element.29.refs_2_) | copy-start | bytes 1572868
  64.5 11.0 %collective-permute-start.10 = (bf16[2,512,128]{2,1,0:T(8,128)(2,1)S(1)}, bf16[2,512,128]{2,1,0:T(8,128)(2,1)S(1)}, u32[]{:S(2)}, u32[]{:S(2)}) collective-permute-start(bf16[2,512,128]{2,1,0:T(8,128)(2,1)S(1)} %get-tuple-element.42), channel_id=1, source_target_pairs={{0,2},{1,3},{2,0},{3,1},{4,6},{5,7},{6,4},{7,5},{8,10},{9,11},{10,... | collective-permute-start | bytes 786440 | tf_op jit(solution)/shard_map/ppermute | solution.py:26
  65.2 11.2 %collective-permute-start.9 = (bf16[2,512,128]{2,1,0:T(8,128)(2,1)S(1)}, bf16[2,512,128]{2,1,0:T(8,128)(2,1)S(1)}, u32[]{:S(2)}, u32[]{:S(2)}) collective-permute-start(bf16[2,512,128]{2,1,0:T(8,128)(2,1)S(1)} %get-tuple-element.40), channel_id=1, source_target_pairs={{0,4},{1,5},{2,6},{3,7},{4,0},{5,1},{6,2},{7,3},{8,12},{9,13},{10,... | collective-permute-start | bytes 786440 | tf_op jit(solution)/shard_map/ppermute | solution.py:26
  76.7 12.8 %collective-permute-start.11 = (bf16[1,512,128]{2,1,0:T(8,128)(2,1)S(1)}, bf16[1,512,128]{2,1,0:T(8,128)(2,1)S(1)}, u32[]{:S(2)}, u32[]{:S(2)}) collective-permute-start(bf16[1,512,128]{2,1,0:T(8,128)(2,1)S(1)} %get-tuple-element.44), channel_id=1, source_target_pairs={{0,8},{1,9},{2,10},{3,11},{4,12},{5,13},{6,14},{7,15},{8,0},{9,1},... | collective-permute-start | bytes 393224 | tf_op jit(solution)/shard_map/ppermute | solution.py:26
  77.4 13.8 %collective-permute-start.12 = (bf16[1,512,128]{2,1,0:T(8,128)(2,1)S(1)}, bf16[1,512,128]{2,1,0:T(8,128)(2,1)S(1)}, u32[]{:S(2)}, u32[]{:S(2)}) collective-permute-start(bf16[1,512,128]{2,1,0:T(8,128)(2,1)S(1)} %get-tuple-element.46), channel_id=1, source_target_pairs={{0,8},{1,9},{2,10},{3,11},{4,12},{5,13},{6,14},{7,15},{8,0},{9,1},... | collective-permute-start | bytes 393224 | tf_op jit(solution)/shard_map/ppermute | solution.py:26
  91.9 1.3 %collective-permute-start.13 = (f32[128,128]{1,0:T(8,128)S(1)}, f32[128,128]{1,0:T(8,128)S(1)}, u32[]{:S(2)}, u32[]{:S(2)}) collective-permute-start(f32[128,128]{1,0:T(8,128)S(1)} %slice_select_fusion.1), channel_id=1, source_target_pairs={{0,1},{1,0},{2,3},{3,2},{4,5},{5,4},{6,7},{7,6},{8,9},{9,8},{10,11... | collective-permute-start | bytes 196616 | tf_op jit(solution)/shard_map/ppermute | solution.py:26
  93.2 4.3 %collective-permute-start.14 = (f32[128,128]{1,0:T(8,128)S(1)}, f32[128,128]{1,0:T(8,128)S(1)}, u32[]{:S(2)}, u32[]{:S(2)}) collective-permute-start(f32[128,128]{1,0:T(8,128)S(1)} %select_add_fusion.1), channel_id=1, source_target_pairs={{0,2},{1,3},{2,0},{3,1},{4,6},{5,7},{6,4},{7,5},{8,10},{9,11},{10,... | collective-permute-start | bytes 196616 | tf_op jit(solution)/shard_map/ppermute | solution.py:26
  97.6 4.3 %collective-permute-start.15 = (f32[128,128]{1,0:T(8,128)S(1)}, f32[128,128]{1,0:T(8,128)S(1)}, u32[]{:S(2)}, u32[]{:S(2)}) collective-permute-start(f32[128,128]{1,0:T(8,128)S(1)} %add.32), channel_id=1, source_target_pairs={{0,4},{1,5},{2,6},{3,7},{4,0},{5,1},{6,2},{7,3},{8,12},{9,13},{10,... | collective-permute-start | bytes 196616 | tf_op jit(solution)/shard_map/ppermute | solution.py:26
  101.9 5.4 %collective-permute-start.16 = (f32[128,128]{1,0:T(8,128)S(1)}, f32[128,128]{1,0:T(8,128)S(1)}, u32[]{:S(2)}, u32[]{:S(2)}) collective-permute-start(f32[128,128]{1,0:T(8,128)S(1)} %add.33), channel_id=1, source_target_pairs={{0,8},{1,9},{2,10},{3,11},{4,12},{5,13},{6,14},{7,15},{8,0},{9,1},... | collective-permute-start | bytes 196616 | tf_op jit(solution)/shard_map/ppermute | solution.py:26
  107.3 1.3 %collective-permute-start.17 = (f32[128,128]{1,0:T(8,128)S(1)}, f32[128,128]{1,0:T(8,128)S(1)}, u32[]{:S(2)}, u32[]{:S(2)}) collective-permute-start(f32[128,128]{1,0:T(8,128)S(1)} %add.34), channel_id=1, source_target_pairs={{0,1},{1,0},{2,3},{3,2},{4,5},{5,4},{6,7},{7,6},{8,9},{9,8},{10,11... | collective-permute-start | bytes 196616 | tf_op jit(solution)/shard_map/ppermute | solution.py:26
where the time goes:
time: 116 us
  Pallas kernels  52.1 us (45%)
  waiting for transfers between devices  33.6 us (29%)
  starting transfers between devices  20.7 us (18%)
  local copies, waits for them, and re-layouts  4.31 us (4%)
  other arithmetic  3.31 us (3%)
    ppermute x18, waiting for transfers between devices, swap(): return lax.ppermute(x, 'cell', [(i, i ^ mask) for i in range(n)])  33.6 us
    pallas_call x1, Pallas kernels, local(): pl.pallas_call(lambda *refs: state_kernel(ck, cl, *refs), out_shape=(shap...  24.9 us
    ppermute x18, starting transfers between devices, swap(): return lax.ppermute(x, 'cell', [(i, i ^ mask) for i in range(n)])  20.7 us
    pallas_call x1, Pallas kernels, local(): pl.pallas_call(lambda *refs: cells_kernel(float(n_cells) ** 0.5, *refs),...  7.63 us
    pallas_call x1, Pallas kernels, local(): pl.pallas_call(lambda *refs: plans_kernel(float(n_sched) ** 0.5, ck, cl,...  6.99 us
    pallas_call x1, Pallas kernels, local(): pl.pallas_call(lambda *refs: lead_kernel(cl / ck, *refs), out_shape=jax.S...  5.8 us
    pallas_call x1, Pallas kernels, local(): pl.pallas_call(plans_lead_kernel, out_shape=square, in_specs=[vmem], out_...  5.16 us
    unnamed x12, local copies, waits for them, and re-layouts  3.39 us
  transfers between devices with their start and end apart: 18, of which 11 were waited for; matrix products, arithmetic and copies ran while one was open for 3% of the time, Pallas kernels for 17%

commit v1 on v0

--- a/solution.py
+++ b/solution.py
@@ -26,23 +26,28 @@
     return lax.ppermute(x, "cell", [(i, i ^ mask) for i in range(n)])
 
 
-def all_sum(x, n):
-    me = lax.axis_index("cell")
-    bits = n.bit_length() - 1
-    half = x.shape[0] // 2
-    odd = (me & 1) == 1
-    lo, hi = x[:half], x[half:]
-    mine = jnp.where(odd, hi, lo) + swap(jnp.where(odd, lo, hi), 1, n)
-    for bit in range(1, bits):
-        mine = mine + swap(mine, 1 << bit, n)
-    other = swap(mine, 1, n)
-    return jnp.concatenate([jnp.where(odd, other, mine), jnp.where(odd, mine, other)], axis=0)
-
-
-def state_kernel(ck, cl, block_ref, slot_ref, c_hbm, s_hbm, core_hbm, table_hbm, well_hbm, prof_hbm,
-                 k_ref, gram_ref, send_l, send_m, hold_l, hold_m,
+def diagonal(m):
+    return lax.broadcasted_iota(i32, (m, m), 0) - lax.broadcasted_iota(i32, (m, m), 1)
+
+
+def cut(rows_ref, send_ref, keep_ref):
+    half = send_ref.shape[0]
+    odd = lax.rem(lax.axis_index("cell"), 2)
+    send_ref[...] = rows_ref[pl.ds(pl.multiple_of((1 - odd) * half, 8), half), :]
+    keep_ref[...] = rows_ref[pl.ds(pl.multiple_of(odd * half, 8), half), :]
+
+
+def joined(rows_ref, mine_ref, other_ref):
+    half = mine_ref.shape[0]
+    odd = lax.rem(lax.axis_index("cell"), 2)
+    rows_ref[pl.ds(pl.multiple_of(odd * half, 8), half), :] = mine_ref[...]
+    rows_ref[pl.ds(pl.multiple_of((1 - odd) * half, 8), half), :] = other_ref[...]
+
+
+def state_kernel(ck, cl, relative, slot_of, c_hbm, s_hbm, core_hbm, table_hbm, well_hbm, prof_hbm,
+                 k_ref, gsend_ref, gkeep_ref, send_l, send_m, hold_l, hold_m,
                  c_ref, s_ref, core_ref, table_ref, well_ref, prof_ref,
-                 g_ref, ft_ref, ps_ref, kt_ref, both_ref, inj_ref, l_ref, m_ref, sems, out_sems):
+                 g_ref, ft_ref, ps_ref, kt_ref, both_ref, inj_ref, l_ref, m_ref, gram_ref, sems, out_sems):
     n, blk, rank = s_ref.shape
     cells = c_ref.shape[0]
     half = n // 2
@@ -95,20 +100,27 @@
     a_hi, a_lo = split(TIME_STEP * (dot(table, w_hi, 0, 0) + dot(table, w_lo, 0, 0)))
     inj_ref[:profiles, :] = a_hi
     inj_ref[profiles:, :] = a_lo
-    gram_ref[:rank, :] = dot(ct, c, 1, 0)
-    gram_ref[rank : 2 * rank, :] = dot(ct, k_hi, 1, 0) + dot(ct, k_lo, 1, 0)
-    gram_ref[2 * rank :, :] = dot(kt_hi, k_hi, 1, 0) + (dot(kt_hi, k_lo, 1, 0) + dot(kt_lo, k_hi, 1, 0))
+    cc = dot(ct, c, 1, 0)
+    kk = dot(kt_hi, k_hi, 1, 0) + (dot(kt_hi, k_lo, 1, 0) + dot(kt_lo, k_hi, 1, 0))
+    below = diagonal(rank)
+    gram_ref[:rank, :] = dot(ct, k_hi, 1, 0) + dot(ct, k_lo, 1, 0)
+    gram_ref[rank : 2 * rank, :] = jnp.where(below > 0, cc, kk)
+    gram_ref[2 * rank :, :] = jnp.broadcast_to(
+        jnp.sum(jnp.where(below == 0, cc, 0.0), axis=0, keepdims=True), (16, rank)
+    )
+    cut(gram_ref, gsend_ref, gkeep_ref)
+    me = lax.axis_index("cell")
 
     def outgoing(j, at, dst_l, dst_m):
         return (
             pltpu.make_async_copy(l_ref.at[j], dst_l.at[at], out_sems.at[0, j]),
-            pltpu.make_async_copy(m_ref.at[j], dst_m.at[slot_ref[at]], out_sems.at[1, j]),
+            pltpu.make_async_copy(m_ref.at[j], dst_m.at[slot_of(at)], out_sems.at[1, j]),
         )
 
     def second(first_slot, dst_l, dst_m):
         def body(at, carry):
             j = first_slot + at
-            b = block_ref[j]
+            b = me ^ relative(j)
             hot = onehot(prof_ref[b], profiles, blk)
             out = dot(g_ref[b], both_ref[...], 1, 0) + dot(
                 jnp.concatenate([hot, hot], axis=0), inj_ref[...], 0, 0
@@ -147,13 +159,23 @@
             send[j] = (keep[half + j].astype(f32) + came[half + j].astype(f32)).astype(bf16)
 
 
-def pair_kernel(keep_l, came_l, keep_m, came_m, after, l_ref, sums_ref):
+def first_fold_kernel(keep_l0, keep_l1, came_l0, came_l1, keep_m0, keep_m1, came_m0, came_m1, after,
+                      send_l, hold_l, send_m, hold_m):
+    for keep, came, out in (
+        (keep_l0, came_l0, hold_l), (keep_l1, came_l1, send_l),
+        (keep_m0, came_m0, hold_m), (keep_m1, came_m1, send_m),
+    ):
+        out[...] = (keep[...].astype(f32) + came[...].astype(f32)).astype(bf16)
+
+
+def pair_kernel(keep_l, came_l, keep_m, came_m, after, l_ref, send_ref, keep_ref, sums_ref):
     rank = l_ref.shape[1]
     l = keep_l[0].astype(f32) + came_l[0].astype(f32)
     m2 = keep_m[0].astype(f32) + came_m[0].astype(f32)
     l_ref[...] = l
     sums_ref[:rank, :] = dot(l, l, 0, 0, HI)
     sums_ref[rank:, :] = dot(m2, l, 0, 0, HI)
+    cut(sums_ref, send_ref, keep_ref)
 
 
 def spread(row, col, m):
@@ -219,17 +241,23 @@
     return jnp.where(col >= row, w[:, :m], 0.0), jnp.where(col <= row, w[:, m:], 0.0)
 
 
-def plans_lead_kernel(ss_ref, av_ref, w):
+def plans_lead_kernel(ss_ref, after, av_ref, w):
     load_gram(w, ss_ref[...])
     eliminate([w])
     av_ref[...] = upper(w)[1]
 
 
-def lead_kernel(ratio, gram_ref, av_ref, lead_ref, w):
+def lead_kernel(ratio, mine_ref, other_ref, av_ref, after, lead_ref, w, gram_ref):
     m = av_ref.shape[0]
-    load_gram(w, gram_ref[:m, :])
+    joined(gram_ref, mine_ref, other_ref)
+    below = diagonal(m)
+    mixed = gram_ref[m : 2 * m, :]
+    low = jnp.where(below > 0, mixed, 0.0)
+    high = jnp.where(below <= 0, mixed, 0.0)
+    strict = jnp.where(below < 0, mixed, 0.0)
+    load_gram(w, low + low.T + jnp.where(below == 0, gram_ref[2 * m : 2 * m + 1, :], 0.0))
     av = av_ref[...]
-    ck = gram_ref[m : 2 * m, :]
+    ck = gram_ref[:m, :]
     l21v = dot(ck * ratio, av, 1, 1, HI)
     lead_ref[4] = av
     lead_ref[5] = l21v
@@ -241,7 +269,7 @@
     lead_ref[0] = a
     lead_ref[1] = l21u
     lead_ref[2] = dot(a, l21u, 0, 1, HI)
-    lead_ref[3] = gram_ref[2 * m :, :] - dot(l21u, l21u, 1, 1, HI)
+    lead_ref[3] = high + strict.T - dot(l21u, l21u, 1, 1, HI)
 
 
 def cells_kernel(root, lead_ref, c_ref, k_ref, basis_ref, lt_ref, inv_ref, w):
@@ -256,9 +284,10 @@
     basis_ref[:, m:] = dot(k_ref[...] - dot(c, lead_ref[2], 1, 0, HI), d, 1, 1, HI) * root
 
 
-def plans_kernel(root, ck, cl, scale, sums_ref, lead_ref, ltu_ref, d_ref, s_ref, l_ref,
-                 basis_ref, core_ref, w):
+def plans_kernel(root, ck, cl, scale, mine_ref, other_ref, lead_ref, ltu_ref, d_ref, s_ref, l_ref,
+                 basis_ref, core_ref, w, sums_ref):
     m = w.shape[0]
+    joined(sums_ref, mine_ref, other_ref)
     ll = sums_ref[:m, :]
     n22 = sums_ref[m:, :]
     load_gram(w, ll - lead_ref[7])
@@ -295,13 +324,15 @@
     cl = PANEL_SCALE / n_cells
     order_a = list(range(bits))
     order_b = [0, 2, 1] + order_a[3:] if bits > 2 else order_a
-    rel = [sum(((j >> (bits - 1 - i)) & 1) << bit for i, bit in enumerate(order_a)) for j in range(n)]
-    slots = [
-        sum(((p >> bit) & 1) << (bits - 1 - i) for i, bit in enumerate(order_b)) % half for p in rel[:half]
-    ]
-    perm = jnp.array(rel, i32) ^ me
+
+    def relative(j):
+        return sum(((j >> (bits - 1 - i)) & 1) << bit for i, bit in enumerate(order_a))
+
+    def slot_of(at):
+        p = relative(at)
+        return sum(((p >> bit) & 1) << (bits - 1 - i) for i, bit in enumerate(order_b) if i > 0)
+
     vmem = pl.BlockSpec(memory_space=pltpu.VMEM)
-    smem = pl.BlockSpec(memory_space=pltpu.SMEM)
     hbm = pl.BlockSpec(memory_space=pltpu.HBM)
     anywhere = pl.BlockSpec(memory_space=pl.ANY)
 
@@ -309,11 +340,12 @@
         return jax.ShapeDtypeStruct(dims, dtype)
 
     part = shape(bf16, half, blk, rank)
-    k, gram, send_l, send_m, hold_l, hold_m = pl.pallas_call(
-        lambda *refs: state_kernel(ck, cl, *refs),
-        out_shape=(shape(f32, cells_dev, rank), shape(f32, 3 * rank, rank), part, part, part, part),
-        in_specs=[smem] * 2 + [hbm] * 6,
-        out_specs=(vmem,) * 2 + (hbm,) * 4,
+    gram_half = shape(f32, rank + 8, rank)
+    k, gram_send, gram, send_l, send_m, hold_l, hold_m = pl.pallas_call(
+        lambda *refs: state_kernel(ck, cl, relative, slot_of, *refs),
+        out_shape=(shape(f32, cells_dev, rank), gram_half, gram_half, part, part, part, part),
+        in_specs=[hbm] * 6,
+        out_specs=(vmem,) * 3 + (hbm,) * 4,
         scratch_shapes=[
             pltpu.VMEM((cells_dev, rank), bf16),
             pltpu.VMEM((n, blk, rank), bf16),
@@ -329,53 +361,79 @@
             pltpu.VMEM((2 * profiles, 2 * rank), bf16),
             pltpu.VMEM((n, blk, rank), bf16),
             pltpu.VMEM((n, blk, rank), bf16),
+            pltpu.VMEM((2 * rank + 16, rank), f32),
             pltpu.SemaphoreType.DMA((6,)),
             pltpu.SemaphoreType.DMA((2, n)),
         ],
         compiler_params=params(60),
         name="state",
     )(
-        perm, jnp.array(slots, i32), cell_factor, sched_factor.reshape(n, blk, rank), core_matrix,
+        cell_factor, sched_factor.reshape(n, blk, rank), core_matrix,
         rate_table, cell_well.reshape(1, cells_dev), sched_profile.reshape(n, 1, blk),
     )
-    sums = all_sum(gram, n)
     ss = dot(sched_factor, sched_factor, 0, 0)
     pair = pltpu.VMEM((rank, 2 * rank), f32)
-    square = jax.ShapeDtypeStruct((rank, rank), f32)
+    square = shape(f32, rank, rank)
+
+    came_l, came_m = swap(send_l, 1, n), swap(send_m, 1, n)
+    gram = gram + swap(gram_send, 1, n)
+    quarter = half // 2
+    block = (1, blk, rank)
+    near = pl.BlockSpec(block, lambda j: (j, 0, 0))
+    far = pl.BlockSpec(block, lambda j: (quarter + j, 0, 0))
+    part = shape(bf16, quarter, blk, rank)
+    send_l, hold_l, send_m, hold_m = pl.pallas_call(
+        first_fold_kernel, grid=(quarter,), out_shape=(part,) * 4,
+        in_specs=[near, far] * 4 + [anywhere], out_specs=(near,) * 4, compiler_params=params(20), name="first_fold",
+    )(hold_l, hold_l, came_l, came_l, hold_m, hold_m, came_m, came_m, gram)
+
+    def fold(step, send_l, hold_l, send_m, hold_m, came_l, came_m, after):
+        part = shape(bf16, half >> (step + 1), blk, rank)
+        return pl.pallas_call(
+            fold_kernel, out_shape=(part,) * 4, in_specs=[vmem] * 4 + [anywhere], out_specs=(vmem,) * 4,
+            compiler_params=params(16), name="fold",
+        )(hold_l, came_l, hold_m, came_m, after)
+
+    gram = gram + swap(gram, 1 << order_a[1], n)
+    came_l, came_m = swap(send_l, 1 << order_a[1], n), swap(send_m, 1 << order_b[1], n)
+    gram_came = swap(gram, 1 << order_a[2], n)
     av = pl.pallas_call(
-        plans_lead_kernel, out_shape=square, in_specs=[vmem], out_specs=vmem, scratch_shapes=[pair],
-        compiler_params=params(16), name="plans_lead",
-    )(ss)
+        plans_lead_kernel, out_shape=square, in_specs=[vmem, anywhere], out_specs=vmem,
+        scratch_shapes=[pair], compiler_params=params(16), name="plans_lead",
+    )(ss, gram)
+    send_l, hold_l, send_m, hold_m = fold(1, send_l, hold_l, send_m, hold_m, came_l, came_m, av)
+    gram = gram + gram_came
+    for bit in range(3, bits):
+        gram = gram + swap(gram, 1 << bit, n)
+    gram_other = swap(gram, 1, n)
+    for step in range(2, bits - 1):
+        came_l = swap(send_l, 1 << order_a[step], n)
+        came_m = swap(send_m, 1 << order_b[step], n)
+        send_l, hold_l, send_m, hold_m = fold(step, send_l, hold_l, send_m, hold_m, came_l, came_m, gram_other)
+    came_l, came_m = swap(send_l, 1 << order_a[-1], n), swap(send_m, 1 << order_b[-1], n)
     lead = pl.pallas_call(
         lambda *refs: lead_kernel(cl / ck, *refs),
-        out_shape=jax.ShapeDtypeStruct((8, rank, rank), f32),
-        in_specs=[vmem] * 2, out_specs=vmem, scratch_shapes=[pair],
+        out_shape=shape(f32, 8, rank, rank),
+        in_specs=[vmem] * 3 + [anywhere], out_specs=vmem,
+        scratch_shapes=[pair, pltpu.VMEM((2 * rank + 16, rank), f32)],
         compiler_params=params(16), name="lead",
-    )(sums, av)
+    )(gram, gram_other, av, hold_l)
     basis_cells, ltu, d = pl.pallas_call(
         lambda *refs: cells_kernel(float(n_cells) ** 0.5, *refs),
         out_shape=(shape(f32, cells_dev, 2 * rank), square, square),
         in_specs=[vmem] * 3, out_specs=(vmem,) * 3, scratch_shapes=[pair],
         compiler_params=params(16), name="cells",
     )(lead, cell_factor, k)
-    waits = [gram, av] + [lead] * (bits - 3) + [d]
-    for step in range(bits):
-        came_l = swap(send_l, 1 << order_a[step], n)
-        came_m = swap(send_m, 1 << order_b[step], n)
-        args = (hold_l, came_l, hold_m, came_m, waits[step])
-        specs = [vmem] * 4 + [anywhere]
-        if step < bits - 1:
-            part = shape(bf16, half >> (step + 1), blk, rank)
-            send_l, hold_l, send_m, hold_m = pl.pallas_call(
-                fold_kernel, out_shape=(part,) * 4, in_specs=specs, out_specs=(vmem,) * 4,
-                compiler_params=params(16), name="fold",
-            )(*args)
-        else:
-            lt, sums2 = pl.pallas_call(
-                pair_kernel, out_shape=(shape(f32, blk, rank), shape(f32, 2 * rank, rank)),
-                in_specs=specs, out_specs=(vmem,) * 2, compiler_params=params(16), name="pair",
-            )(*args)
-    sums2 = all_sum(sums2, n)
+    lt, sums_send, sums = pl.pallas_call(
+        pair_kernel, out_shape=(shape(f32, blk, rank), square, square),
+        in_specs=[vmem] * 4 + [anywhere], out_specs=(vmem,) * 3,
+        scratch_shapes=[pltpu.VMEM((2 * rank, rank), f32)],
+        compiler_params=params(16), name="pair",
+    )(hold_l, came_l, hold_m, came_m, d)
+    sums = sums + swap(sums_send, 1, n)
+    for bit in range(1, bits):
+        sums = sums + swap(sums, 1 << bit, n)
+    sums_other = swap(sums, 1, n)
     own = lax.dynamic_slice_in_dim(sched_factor, me * blk, blk, 0)
     scale = rank / (float(n_cells) * float(n_sched)) ** 0.5
     basis_sched, core_out = pl.pallas_call(
@@ -384,9 +442,10 @@
             jax.ShapeDtypeStruct((blk, 2 * rank), f32),
             jax.ShapeDtypeStruct((2 * rank, 2 * rank), f32),
         ),
-        in_specs=[vmem] * 6, out_specs=(vmem,) * 2, scratch_shapes=[pair],
+        in_specs=[vmem] * 7, out_specs=(vmem,) * 2,
+        scratch_shapes=[pair, pltpu.VMEM((2 * rank, rank), f32)],
         compiler_params=params(16), name="plans",
-    )(sums2, lead, ltu, d, own, lt)
+    )(sums, sums_other, lead, ltu, d, own, lt)
     return (basis_cells, basis_sched, core_out)
 
 

time: 116 us -> 114 us (0.983)
  other arithmetic: 3.31 us -> 0.96 us
  waiting for transfers between devices: 33.6 us -> 35.9 us
  local copies, waits for them, and re-layouts: 4.31 us -> 2.48 us
    ppermute x18, waiting for transfers between devices: 33.6 us -> 35.9 us  [swap(): return lax.ppermute(x, 'cell', [(i, i ^ mask) for i in range(n)])]
    xor x1 -> x0, other arithmetic: 1.25 us -> none  [local(): perm = jnp.array(rel, i32) ^ me]
    unnamed x12 -> x10, local copies, waits for them, and re-layouts: 3.39 us -> 2.46 us
  transfers between devices with their start and end apart: 18 -> 18, of which waited for: 11 -> 10; matrix products, arithmetic and copies ran while one was open for 3% -> 1% of each run, Pallas kernels for 17% -> 17%
where the time goes in v1:
time: 114 us
  Pallas kernels  51.9 us (46%)
  waiting for transfers between devices  35.9 us (31%)
  starting transfers between devices  21.2 us (19%)
  local copies, waits for them, and re-layouts  2.48 us (2%)
    ppermute x18, waiting for transfers between devices, swap(): return lax.ppermute(x, 'cell', [(i, i ^ mask) for i in range(n)])  35.9 us
    pallas_call x1, Pallas kernels, local(): pl.pallas_call(lambda *refs: state_kernel(ck, cl, relative, slot_of, *ref...  24.3 us
    ppermute x18, starting transfers between devices, swap(): return lax.ppermute(x, 'cell', [(i, i ^ mask) for i in range(n)])  21.2 us
    pallas_call x1, Pallas kernels, local(): pl.pallas_call(lambda *refs: cells_kernel(float(n_cells) ** 0.5, *refs),...  7.85 us
    pallas_call x1, Pallas kernels, local(): pl.pallas_call(lambda *refs: plans_kernel(float(n_sched) ** 0.5, ck, cl,...  7 us
    pallas_call x1, Pallas kernels, local(): pl.pallas_call(lambda *refs: lead_kernel(cl / ck, *refs), out_shape=shape...  5.88 us
    pallas_call x1, Pallas kernels, local(): pl.pallas_call(plans_lead_kernel, out_shape=square, in_specs=[vmem, anywh...  5.16 us
    unnamed x10, local copies, waits for them, and re-layouts  2.46 us
  transfers between devices with their start and end apart: 18, of which 10 were waited for; matrix products, arithmetic and copies ran while one was open for 1% of the time, Pallas kernels for 17%

profile of v1, /device:TPU:0, one launch (start us, length us, event | category | flops | bytes accessed | tf_op | source)
XLA Modules:
  0.0 114.1 jit_solution(7152651783787151303)
XLA Ops:
  0.6 24.3 %state.1 = (f32[1024,128]{1,0:T(8,128)}, f32[136,128]{1,0:T(8,128)}, f32[136,128]{1,0:T(8,128)}, bf16[8,512,128]{2,1,0:T(8,128)(2,1)}, bf16[8,512,128]{2,1,0:T(8...) custom-call(bf16[1024,128]{1,0:T(8,128)(2,1)} %refs_1_.1, bf16[16,512,128]{2,1,0:T(8,128)(2,1)} %bitcast.5, ...), custom_call_target="tpu_custom_call" | custom-call | tf_op jit(solution)/shard_map/state/pallas_call | solution.py:344
  24.9 0.5 collective-permute-start.5
  26.0 3.6 %collective-permute-done = f32[136,128]{1,0:T(8,128)S(1)} collective-permute-done((f32[136,128]{1,0:T(8,128)}, f32[136,128]{1,0:T(8,128)S(1)}, u32[]{:S(2)}, u32[]{:S(2)}) %collective-permute-start) | collective-permute-done | bytes 69664 | tf_op jit(solution)/shard_map/ppermute | solution.py:26
  29.5 0.9 add.27.after
  30.5 1.2 %copy-done = bf16[8,512,128]{2,1,0:T(8,128)(2,1)S(1)} copy-done((bf16[8,512,128]{2,1,0:T(8,128)(2,1)S(1)}, bf16[8,512,128]{2,1,0:T(8,128)(2,1)}, u32[]{:S(2)}) %copy-start) | copy-done | bytes 1048600
  31.7 1.2 %copy-done.1 = bf16[8,512,128]{2,1,0:T(8,128)(2,1)S(1)} copy-done((bf16[8,512,128]{2,1,0:T(8,128)(2,1)S(1)}, bf16[8,512,128]{2,1,0:T(8,128)(2,1)}, u32[]{:S(2)}) %copy-start.1) | copy-done | bytes 1048600
  32.9 0.7 first_fold.1
  33.6 2.9 %collective-permute-start.7 = (bf16[4,512,128]{2,1,0:T(8,128)(2,1)S(1)}, bf16[4,512,128]{2,1,0:T(8,128)(2,1)S(1)}, u32[]{:S(2)}, u32[]{:S(2)}) collective-permute-start(bf16[4,512,128]{2,1,0:T(8,128)(2,1)S(1)} %get-tuple-element.37), channel_id=1, source_target_pairs={{0,2},{1,3},{2,0},{3,1},{4,6},{5,7},{6,4},{7,5},{8,10},{9,11},{10,... | collective-permute-start | bytes 1572872 | tf_op jit(solution)/shard_map/ppermute | solution.py:26
  36.6 1.6 %collective-permute-start.8 = (bf16[4,512,128]{2,1,0:T(8,128)(2,1)S(1)}, bf16[4,512,128]{2,1,0:T(8,128)(2,1)S(1)}, u32[]{:S(2)}, u32[]{:S(2)}) collective-permute-start(bf16[4,512,128]{2,1,0:T(8,128)(2,1)S(1)} %get-tuple-element.39), channel_id=1, source_target_pairs={{0,4},{1,5},{2,6},{3,7},{4,0},{5,1},{6,2},{7,3},{8,12},{9,13},{10,... | collective-permute-start | bytes 1572872 | tf_op jit(solution)/shard_map/ppermute | solution.py:26
  38.2 0.5 collective-permute-start.1
  38.7 0.8 fusion.ss_ref
  39.4 10.9 %collective-permute-done.1 = f32[136,128]{1,0:T(8,128)S(1)} collective-permute-done((f32[136,128]{1,0:T(8,128)S(1)}, f32[136,128]{1,0:T(8,128)S(1)}, u32[]{:S(2)}, u32[]{:S(2)}) %collective-permute-start.1) | collective-permute-done | bytes 69664 | tf_op jit(solution)/shard_map/ppermute | solution.py:26
  50.3 5.2 %plans_lead.1.after.refs_2_ = f32[128,128]{1,0:T(8,128)S(1)} custom-call(f32[128,128]{1,0:T(8,128)S(1)} %fusion.ss_ref, f32[136,128]{1,0:T(8,128)S(1)} %add.28.after), custom_call_target="tpu_custom_call" | custom-call | tf_op jit(solution)/shard_map/plans_lead/pallas_call | solution.py:400
  55.8 1.8 %collective-permute-start.10 = (bf16[2,512,128]{2,1,0:T(8,128)(2,1)S(1)}, bf16[2,512,128]{2,1,0:T(8,128)(2,1)S(1)}, u32[]{:S(2)}, u32[]{:S(2)}) collective-permute-start(bf16[2,512,128]{2,1,0:T(8,128)(2,1)S(1)} %get-tuple-element.43), channel_id=1, source_target_pairs={{0,2},{1,3},{2,0},{3,1},{4,6},{5,7},{6,4},{7,5},{8,10},{9,11},{10,... | collective-permute-start | bytes 786440 | tf_op jit(solution)/shard_map/ppermute | solution.py:26
  57.6 1.6 %collective-permute-start.9 = (bf16[2,512,128]{2,1,0:T(8,128)(2,1)S(1)}, bf16[2,512,128]{2,1,0:T(8,128)(2,1)S(1)}, u32[]{:S(2)}, u32[]{:S(2)}) collective-permute-start(bf16[2,512,128]{2,1,0:T(8,128)(2,1)S(1)} %get-tuple-element.41), channel_id=1, source_target_pairs={{0,4},{1,5},{2,6},{3,7},{4,0},{5,1},{6,2},{7,3},{8,12},{9,13},{10,... | collective-permute-start | bytes 786440 | tf_op jit(solution)/shard_map/ppermute | solution.py:26
  59.6 6.7 %collective-permute-done.2 = f32[136,128]{1,0:T(8,128)S(1)} collective-permute-done((f32[136,128]{1,0:T(8,128)S(1)}, f32[136,128]{1,0:T(8,128)S(1)}, u32[]{:S(2)}, u32[]{:S(2)}) %collective-permute-start.2) | collective-permute-done | bytes 69664 | tf_op jit(solution)/shard_map/ppermute | solution.py:26
  66.3 2.6 %collective-permute-start.3 = (f32[136,128]{1,0:T(8,128)S(1)}, f32[136,128]{1,0:T(8,128)S(1)}, u32[]{:S(2)}, u32[]{:S(2)}) collective-permute-start(f32[136,128]{1,0:T(8,128)S(1)} %add.29), channel_id=1, source_target_pairs={{0,8},{1,9},{2,10},{3,11},{4,12},{5,13},{6,14},{7,15},{8,0},{9,1},... | collective-permute-start | bytes 208904 | tf_op jit(solution)/shard_map/ppermute | solution.py:26
  69.0 2.6 %collective-permute-done.3 = f32[136,128]{1,0:T(8,128)S(1)} collective-permute-done((f32[136,128]{1,0:T(8,128)S(1)}, f32[136,128]{1,0:T(8,128)S(1)}, u32[]{:S(2)}, u32[]{:S(2)}) %collective-permute-start.3) | collective-permute-done | bytes 69664 | tf_op jit(solution)/shard_map/ppermute | solution.py:26
  71.7 1.2 %collective-permute-done.4.after.refs_1_ = f32[136,128]{1,0:T(8,128)S(1)} collective-permute-done((f32[136,128]{1,0:T(8,128)S(1)}, f32[136,128]{1,0:T(8,128)S(1)}, u32[]{:S(2)}, u32[]{:S(2)}) %collective-permute-start.4) | collective-permute-done | bytes 69664 | tf_op jit(solution)/shard_map/ppermute | solution.py:26
  73.1 2.7 %collective-permute-start.11 = (bf16[1,512,128]{2,1,0:T(8,128)(2,1)S(1)}, bf16[1,512,128]{2,1,0:T(8,128)(2,1)S(1)}, u32[]{:S(2)}, u32[]{:S(2)}) collective-permute-start(bf16[1,512,128]{2,1,0:T(8,128)(2,1)S(1)} %get-tuple-element.47), channel_id=1, source_target_pairs={{0,8},{1,9},{2,10},{3,11},{4,12},{5,13},{6,14},{7,15},{8,0},{9,1},... | collective-permute-start | bytes 393224 | tf_op jit(solution)/shard_map/ppermute | solution.py:26
  76.1 5.9 %lead.1.refs_0_.refs_2_ = f32[8,128,128]{2,1,0:T(8,128)S(1)} custom-call(f32[136,128]{1,0:T(8,128)S(1)} %add.30.refs_0_, f32[136,128]{1,0:T(8,128)S(1)} %collective-permute-done.4.after.refs_1_, f32[128,128]{1,0:T(8,128)S(1)} %plans_lead.1.after.refs_2_, bf16[1,512,128]{2,1,0:T(8,128)(2,1)S(1)} %get-tuple-element.44.refs_3_.keep_l), custom_call_target="tpu_custom_call" | custom-call | tf_op jit(solution)/shard_map/lead/pallas_call | solution.py:414
  82.0 7.9 %cells.1 = (f32[1024,256]{1,0:T(8,128)}, f32[128,128]{1,0:T(8,128)S(1)}, f32[128,128]{1,0:T(8,128)S(1)}) custom-call(f32[8,128,128]{2,1,0:T(8,128)S(1)} %lead.1.refs_0_.refs_2_, bf16[1024,128]{1,0:T(8,128)(2,1)S(1)} %copy-done.2, f32[1024,128]{1,0:T(8,128)S(1)} %copy-done.3), custom_call_target="tpu_custom_call" | custom-call | tf_op jit(solution)/shard_map/cells/pallas_call | solution.py:421
  89.8 0.7 pair.1
  90.6 1.2 %collective-permute-done.13 = f32[128,128]{1,0:T(8,128)S(1)} collective-permute-done((f32[128,128]{1,0:T(8,128)S(1)}, f32[128,128]{1,0:T(8,128)S(1)}, u32[]{:S(2)}, u32[]{:S(2)}) %collective-permute-start.13) | collective-permute-done | bytes 65568 | tf_op jit(solution)/shard_map/ppermute | solution.py:26
  91.8 0.7 collective-permute-start.14
  92.5 3.7 %collective-permute-done.14 = f32[128,128]{1,0:T(8,128)S(1)} collective-permute-done((f32[128,128]{1,0:T(8,128)S(1)}, f32[128,128]{1,0:T(8,128)S(1)}, u32[]{:S(2)}, u32[]{:S(2)}) %collective-permute-start.14) | collective-permute-done | bytes 65568 | tf_op jit(solution)/shard_map/ppermute | solution.py:26
  96.2 2.0 %collective-permute-start.15 = (f32[128,128]{1,0:T(8,128)S(1)}, f32[128,128]{1,0:T(8,128)S(1)}, u32[]{:S(2)}, u32[]{:S(2)}) collective-permute-start(f32[128,128]{1,0:T(8,128)S(1)} %add.32), channel_id=1, source_target_pairs={{0,4},{1,5},{2,6},{3,7},{4,0},{5,1},{6,2},{7,3},{8,12},{9,13},{10,... | collective-permute-start | bytes 196616 | tf_op jit(solution)/shard_map/ppermute | solution.py:26
  98.2 2.3 %collective-permute-done.15 = f32[128,128]{1,0:T(8,128)S(1)} collective-permute-done((f32[128,128]{1,0:T(8,128)S(1)}, f32[128,128]{1,0:T(8,128)S(1)}, u32[]{:S(2)}, u32[]{:S(2)}) %collective-permute-start.15) | collective-permute-done | bytes 65568 | tf_op jit(solution)/shard_map/ppermute | solution.py:26
  100.5 2.8 %collective-permute-start.16 = (f32[128,128]{1,0:T(8,128)S(1)}, f32[128,128]{1,0:T(8,128)S(1)}, u32[]{:S(2)}, u32[]{:S(2)}) collective-permute-start(f32[128,128]{1,0:T(8,128)S(1)} %add.33), channel_id=1, source_target_pairs={{0,8},{1,9},{2,10},{3,11},{4,12},{5,13},{6,14},{7,15},{8,0},{9,1},... | collective-permute-start | bytes 196616 | tf_op jit(solution)/shard_map/ppermute | solution.py:26
  103.4 2.4 %collective-permute-done.16 = f32[128,128]{1,0:T(8,128)S(1)} collective-permute-done((f32[128,128]{1,0:T(8,128)S(1)}, f32[128,128]{1,0:T(8,128)S(1)}, u32[]{:S(2)}, u32[]{:S(2)}) %collective-permute-start.16) | collective-permute-done | bytes 65568 | tf_op jit(solution)/shard_map/ppermute | solution.py:26
  105.9 1.2 %collective-permute-done.17.refs_1_ = f32[128,128]{1,0:T(8,128)S(1)} collective-permute-done((f32[128,128]{1,0:T(8,128)S(1)}, f32[128,128]{1,0:T(8,128)S(1)}, u32[]{:S(2)}, u32[]{:S(2)}) %collective-permute-start.17) | collective-permute-done | bytes 65568 | tf_op jit(solution)/shard_map/ppermute | solution.py:26
  107.1 7.0 %plans.1 = (f32[512,256]{1,0:T(8,128)}, f32[256,256]{1,0:T(8,128)}) custom-call(f32[128,128]{1,0:T(8,128)S(1)} %add.34.refs_0_, f32[128,128]{1,0:T(8,128)S(1)} %collective-permute-done.17.refs_1_, f32[8,128,128]{2,1,0:T(8,128)S(1)} %lead.1.refs_0_.refs_2_, f32[128,128]{1,0:T(8,128)S(1)} %get-tuple-element.53.refs_3_, ...), custom_call_target="tpu_custom_call" | custom-call | tf_op jit(solution)/shard_map/plans/pallas_call | solution.py:439
  (33 shorter events, 1.9 us)
Async XLA Ops:
  24.9 5.5 %collective-permute-start.5 = (bf16[8,512,128]{2,1,0:T(8,128)(2,1)}, bf16[8,512,128]{2,1,0:T(8,128)(2,1)S(1)}, u32[]{:S(2)}, u32[]{:S(2)}) collective-permute-start(bf16[8,512,128]{2,1,0:T(8,128)(2,1)} %get-tuple-element.33), channel_id=1, source_target_pairs={{0,1},{1,0},{2,3},{3,2},{4,5},{5,4},{6,7},{7,6},{8,9},{9,8},{10,11... | collective-permute-start | bytes 3145736 | tf_op jit(solution)/shard_map/ppermute | solution.py:26
  25.5 5.0 %collective-permute-start.6 = (bf16[8,512,128]{2,1,0:T(8,128)(2,1)}, bf16[8,512,128]{2,1,0:T(8,128)(2,1)S(1)}, u32[]{:S(2)}, u32[]{:S(2)}) collective-permute-start(bf16[8,512,128]{2,1,0:T(8,128)(2,1)} %get-tuple-element.35), channel_id=1, source_target_pairs={{0,1},{1,0},{2,3},{3,2},{4,5},{5,4},{6,7},{7,6},{8,9},{9,8},{10,11... | collective-permute-start | bytes 3145736 | tf_op jit(solution)/shard_map/ppermute | solution.py:26
  25.5 4.0 %collective-permute-start = (f32[136,128]{1,0:T(8,128)}, f32[136,128]{1,0:T(8,128)S(1)}, u32[]{:S(2)}, u32[]{:S(2)}) collective-permute-start(f32[136,128]{1,0:T(8,128)} %get-tuple-element.31), channel_id=1, source_target_pairs={{0,1},{1,0},{2,3},{3,2},{4,5},{5,4},{6,7},{7,6},{8,9},{9,8},{10,11... | collective-permute-start | bytes 208904 | tf_op jit(solution)/shard_map/ppermute | solution.py:26
  30.5 1.2 %copy-start = (bf16[8,512,128]{2,1,0:T(8,128)(2,1)S(1)}, bf16[8,512,128]{2,1,0:T(8,128)(2,1)}, u32[]{:S(2)}) copy-start(bf16[8,512,128]{2,1,0:T(8,128)(2,1)} %get-tuple-element.32.keep_l0.keep_l1) | copy-start | bytes 3145732
  31.7 1.2 %copy-start.1 = (bf16[8,512,128]{2,1,0:T(8,128)(2,1)S(1)}, bf16[8,512,128]{2,1,0:T(8,128)(2,1)}, u32[]{:S(2)}) copy-start(bf16[8,512,128]{2,1,0:T(8,128)(2,1)} %get-tuple-element.34.keep_m0.keep_m1) | copy-start | bytes 3145732
  32.9 5.8 %copy-start.4 = (bf16[8192,128]{1,0:T(8,128)(2,1)S(1)}, bf16[8192,128]{1,0:T(8,128)(2,1)}, u32[]{:S(2)}) copy-start(bf16[8192,128]{1,0:T(8,128)(2,1)} %param.7) | copy-start | bytes 6291460
  33.6 21.8 %collective-permute-start.7 = (bf16[4,512,128]{2,1,0:T(8,128)(2,1)S(1)}, bf16[4,512,128]{2,1,0:T(8,128)(2,1)S(1)}, u32[]{:S(2)}, u32[]{:S(2)}) collective-permute-start(bf16[4,512,128]{2,1,0:T(8,128)(2,1)S(1)} %get-tuple-element.37), channel_id=1, source_target_pairs={{0,2},{1,3},{2,0},{3,1},{4,6},{5,7},{6,4},{7,5},{8,10},{9,11},{10,... | collective-permute-start | bytes 1572872 | tf_op jit(solution)/shard_map/ppermute | solution.py:26
  36.6 18.9 %collective-permute-start.8 = (bf16[4,512,128]{2,1,0:T(8,128)(2,1)S(1)}, bf16[4,512,128]{2,1,0:T(8,128)(2,1)S(1)}, u32[]{:S(2)}, u32[]{:S(2)}) collective-permute-start(bf16[4,512,128]{2,1,0:T(8,128)(2,1)S(1)} %get-tuple-element.39), channel_id=1, source_target_pairs={{0,4},{1,5},{2,6},{3,7},{4,0},{5,1},{6,2},{7,3},{8,12},{9,13},{10,... | collective-permute-start | bytes 1572872 | tf_op jit(solution)/shard_map/ppermute | solution.py:26
  38.2 12.1 %collective-permute-start.1 = (f32[136,128]{1,0:T(8,128)S(1)}, f32[136,128]{1,0:T(8,128)S(1)}, u32[]{:S(2)}, u32[]{:S(2)}) collective-permute-start(f32[136,128]{1,0:T(8,128)S(1)} %add.27.after), channel_id=1, source_target_pairs={{0,2},{1,3},{2,0},{3,1},{4,6},{5,7},{6,4},{7,5},{8,10},{9,11},{10,... | collective-permute-start | bytes 208904 | tf_op jit(solution)/shard_map/ppermute | solution.py:26
  55.5 26.5 %copy-start.2 = (bf16[1024,128]{1,0:T(8,128)(2,1)S(1)}, bf16[1024,128]{1,0:T(8,128)(2,1)}, u32[]{:S(2)}) copy-start(bf16[1024,128]{1,0:T(8,128)(2,1)} %refs_1_.1) | copy-start | bytes 786436
  55.5 26.5 %copy-start.3 = (f32[1024,128]{1,0:T(8,128)S(1)}, f32[1024,128]{1,0:T(8,128)}, u32[]{:S(2)}) copy-start(f32[1024,128]{1,0:T(8,128)} %get-tuple-element.45.refs_2_) | copy-start | bytes 1572868
  55.8 17.2 %collective-permute-start.10 = (bf16[2,512,128]{2,1,0:T(8,128)(2,1)S(1)}, bf16[2,512,128]{2,1,0:T(8,128)(2,1)S(1)}, u32[]{:S(2)}, u32[]{:S(2)}) collective-permute-start(bf16[2,512,128]{2,1,0:T(8,128)(2,1)S(1)} %get-tuple-element.43), channel_id=1, source_target_pairs={{0,2},{1,3},{2,0},{3,1},{4,6},{5,7},{6,4},{7,5},{8,10},{9,11},{10,... | collective-permute-start | bytes 786440 | tf_op jit(solution)/shard_map/ppermute | solution.py:26
  57.6 15.4 %collective-permute-start.9 = (bf16[2,512,128]{2,1,0:T(8,128)(2,1)S(1)}, bf16[2,512,128]{2,1,0:T(8,128)(2,1)S(1)}, u32[]{:S(2)}, u32[]{:S(2)}) collective-permute-start(bf16[2,512,128]{2,1,0:T(8,128)(2,1)S(1)} %get-tuple-element.41), channel_id=1, source_target_pairs={{0,4},{1,5},{2,6},{3,7},{4,0},{5,1},{6,2},{7,3},{8,12},{9,13},{10,... | collective-permute-start | bytes 786440 | tf_op jit(solution)/shard_map/ppermute | solution.py:26
  59.2 7.2 %collective-permute-start.2 = (f32[136,128]{1,0:T(8,128)S(1)}, f32[136,128]{1,0:T(8,128)S(1)}, u32[]{:S(2)}, u32[]{:S(2)}) collective-permute-start(f32[136,128]{1,0:T(8,128)S(1)} %add.28.after), channel_id=1, source_target_pairs={{0,4},{1,5},{2,6},{3,7},{4,0},{5,1},{6,2},{7,3},{8,12},{9,13},{10,... | collective-permute-start | bytes 208904 | tf_op jit(solution)/shard_map/ppermute | solution.py:26
  66.3 5.3 %collective-permute-start.3 = (f32[136,128]{1,0:T(8,128)S(1)}, f32[136,128]{1,0:T(8,128)S(1)}, u32[]{:S(2)}, u32[]{:S(2)}) collective-permute-start(f32[136,128]{1,0:T(8,128)S(1)} %add.29), channel_id=1, source_target_pairs={{0,8},{1,9},{2,10},{3,11},{4,12},{5,13},{6,14},{7,15},{8,0},{9,1},... | collective-permute-start | bytes 208904 | tf_op jit(solution)/shard_map/ppermute | solution.py:26
  71.6 1.3 %collective-permute-start.4 = (f32[136,128]{1,0:T(8,128)S(1)}, f32[136,128]{1,0:T(8,128)S(1)}, u32[]{:S(2)}, u32[]{:S(2)}) collective-permute-start(f32[136,128]{1,0:T(8,128)S(1)} %add.30.refs_0_), channel_id=1, source_target_pairs={{0,1},{1,0},{2,3},{3,2},{4,5},{5,4},{6,7},{7,6},{8,9},{9,8},{10,11... | collective-permute-start | bytes 208904 | tf_op jit(solution)/shard_map/ppermute | solution.py:26
  73.1 16.8 %collective-permute-start.11 = (bf16[1,512,128]{2,1,0:T(8,128)(2,1)S(1)}, bf16[1,512,128]{2,1,0:T(8,128)(2,1)S(1)}, u32[]{:S(2)}, u32[]{:S(2)}) collective-permute-start(bf16[1,512,128]{2,1,0:T(8,128)(2,1)S(1)} %get-tuple-element.47), channel_id=1, source_target_pairs={{0,8},{1,9},{2,10},{3,11},{4,12},{5,13},{6,14},{7,15},{8,0},{9,1},... | collective-permute-start | bytes 393224 | tf_op jit(solution)/shard_map/ppermute | solution.py:26
  75.8 14.0 %collective-permute-start.12 = (bf16[1,512,128]{2,1,0:T(8,128)(2,1)S(1)}, bf16[1,512,128]{2,1,0:T(8,128)(2,1)S(1)}, u32[]{:S(2)}, u32[]{:S(2)}) collective-permute-start(bf16[1,512,128]{2,1,0:T(8,128)(2,1)S(1)} %get-tuple-element.49), channel_id=1, source_target_pairs={{0,8},{1,9},{2,10},{3,11},{4,12},{5,13},{6,14},{7,15},{8,0},{9,1},... | collective-permute-start | bytes 393224 | tf_op jit(solution)/shard_map/ppermute | solution.py:26
  90.5 1.3 %collective-permute-start.13 = (f32[128,128]{1,0:T(8,128)S(1)}, f32[128,128]{1,0:T(8,128)S(1)}, u32[]{:S(2)}, u32[]{:S(2)}) collective-permute-start(f32[128,128]{1,0:T(8,128)S(1)} %get-tuple-element.52), channel_id=1, source_target_pairs={{0,1},{1,0},{2,3},{3,2},{4,5},{5,4},{6,7},{7,6},{8,9},{9,8},{10,11... | collective-permute-start | bytes 196616 | tf_op jit(solution)/shard_map/ppermute | solution.py:26
  91.8 4.3 %collective-permute-start.14 = (f32[128,128]{1,0:T(8,128)S(1)}, f32[128,128]{1,0:T(8,128)S(1)}, u32[]{:S(2)}, u32[]{:S(2)}) collective-permute-start(f32[128,128]{1,0:T(8,128)S(1)} %add.31), channel_id=1, source_target_pairs={{0,2},{1,3},{2,0},{3,1},{4,6},{5,7},{6,4},{7,5},{8,10},{9,11},{10,... | collective-permute-start | bytes 196616 | tf_op jit(solution)/shard_map/ppermute | solution.py:26
  96.2 4.3 %collective-permute-start.15 = (f32[128,128]{1,0:T(8,128)S(1)}, f32[128,128]{1,0:T(8,128)S(1)}, u32[]{:S(2)}, u32[]{:S(2)}) collective-permute-start(f32[128,128]{1,0:T(8,128)S(1)} %add.32), channel_id=1, source_target_pairs={{0,4},{1,5},{2,6},{3,7},{4,0},{5,1},{6,2},{7,3},{8,12},{9,13},{10,... | collective-permute-start | bytes 196616 | tf_op jit(solution)/shard_map/ppermute | solution.py:26
  100.5 5.2 %collective-permute-start.16 = (f32[128,128]{1,0:T(8,128)S(1)}, f32[128,128]{1,0:T(8,128)S(1)}, u32[]{:S(2)}, u32[]{:S(2)}) collective-permute-start(f32[128,128]{1,0:T(8,128)S(1)} %add.33), channel_id=1, source_target_pairs={{0,8},{1,9},{2,10},{3,11},{4,12},{5,13},{6,14},{7,15},{8,0},{9,1},... | collective-permute-start | bytes 196616 | tf_op jit(solution)/shard_map/ppermute | solution.py:26
  105.8 1.3 %collective-permute-start.17 = (f32[128,128]{1,0:T(8,128)S(1)}, f32[128,128]{1,0:T(8,128)S(1)}, u32[]{:S(2)}, u32[]{:S(2)}) collective-permute-start(f32[128,128]{1,0:T(8,128)S(1)} %add.34.refs_0_), channel_id=1, source_target_pairs={{0,1},{1,0},{2,3},{3,2},{4,5},{5,4},{6,7},{7,6},{8,9},{9,8},{10,11... | collective-permute-start | bytes 196616 | tf_op jit(solution)/shard_map/ppermute | solution.py:26

commit v2 on v1

--- a/solution.py
+++ b/solution.py
@@ -131,7 +131,7 @@
                 copy.start()
             return carry
 
-        lax.fori_loop(0, half, body, 0)
+        lax.fori_loop(0, half, body, 0, unroll=2)
 
     def finish(first_slot, dst_l, dst_m):
         def body(at, carry):
@@ -151,7 +151,8 @@
     return jnp.where(lax.broadcasted_iota(i32, (size, count), 0) == ids, 1.0, 0.0).astype(bf16)
 
 
-def fold_kernel(keep_l, came_l, keep_m, came_m, after, send_l, hold_l, send_m, hold_m):
+def fold_kernel(keep_l, came_l, keep_m, came_m, *rest):
+    send_l, hold_l, send_m, hold_m = rest[-4:]
     half = hold_l.shape[0]
     for keep, came, send, hold in ((keep_l, came_l, send_l, hold_l), (keep_m, came_m, send_m, hold_m)):
         for j in range(half):
@@ -159,8 +160,12 @@
             send[j] = (keep[half + j].astype(f32) + came[half + j].astype(f32)).astype(bf16)
 
 
-def first_fold_kernel(keep_l0, keep_l1, came_l0, came_l1, keep_m0, keep_m1, came_m0, came_m1, after,
-                      send_l, hold_l, send_m, hold_m):
+def first_fold_kernel(keep_l0, keep_l1, came_l0, came_l1, keep_m0, keep_m1, came_m0, came_m1,
+                      gram_kept, gram_came, send_l, hold_l, send_m, hold_m, gram_ref):
+    @pl.when(pl.program_id(0) == 0)
+    def _():
+        gram_ref[...] = gram_kept[...] + gram_came[...]
+
     for keep, came, out in (
         (keep_l0, came_l0, hold_l), (keep_l1, came_l1, send_l),
         (keep_m0, came_m0, hold_m), (keep_m1, came_m1, send_m),
@@ -176,6 +181,10 @@
     sums_ref[:rank, :] = dot(l, l, 0, 0, HI)
     sums_ref[rank:, :] = dot(m2, l, 0, 0, HI)
     cut(sums_ref, send_ref, keep_ref)
+
+
+def add_kernel(a_ref, b_ref, after, out_ref):
+    out_ref[...] = a_ref[...] + b_ref[...]
 
 
 def spread(row, col, m):
@@ -247,7 +256,7 @@
     av_ref[...] = upper(w)[1]
 
 
-def lead_kernel(ratio, mine_ref, other_ref, av_ref, after, lead_ref, w, gram_ref):
+def lead_kernel(ratio, mine_ref, other_ref, av_ref, lead_ref, w, gram_ref):
     m = av_ref.shape[0]
     joined(gram_ref, mine_ref, other_ref)
     below = diagonal(m)
@@ -304,6 +313,10 @@
     core_ref[:m, m:] = dot(a, ltv, 1, 1, HI) * (scale / cl)
     core_ref[m:, :m] = dot(ltu_ref[...], av, 1, 1, HI) * (scale / ck)
     core_ref[m:, m:] = dot(e, dv, 1, 1, HI) * scale
+
+
+def cost(units):
+    return pl.CostEstimate(flops=0, bytes_accessed=units * 3_600_000, transcendentals=0)
 
 
 def params(mib):
@@ -376,63 +389,66 @@
     square = shape(f32, rank, rank)
 
     came_l, came_m = swap(send_l, 1, n), swap(send_m, 1, n)
-    gram = gram + swap(gram_send, 1, n)
+    gram_came = swap(gram_send, 1, n)
     quarter = half // 2
     block = (1, blk, rank)
     near = pl.BlockSpec(block, lambda j: (j, 0, 0))
     far = pl.BlockSpec(block, lambda j: (quarter + j, 0, 0))
     part = shape(bf16, quarter, blk, rank)
-    send_l, hold_l, send_m, hold_m = pl.pallas_call(
-        first_fold_kernel, grid=(quarter,), out_shape=(part,) * 4,
-        in_specs=[near, far] * 4 + [anywhere], out_specs=(near,) * 4, compiler_params=params(20), name="first_fold",
-    )(hold_l, hold_l, came_l, came_l, hold_m, hold_m, came_m, came_m, gram)
-
-    def fold(step, send_l, hold_l, send_m, hold_m, came_l, came_m, after):
+    whole = pl.BlockSpec(gram.shape, lambda j: (0, 0))
+    send_l, hold_l, send_m, hold_m, gram = pl.pallas_call(
+        first_fold_kernel, grid=(quarter,), out_shape=(part,) * 4 + (gram_half,),
+        in_specs=[near, far] * 4 + [whole] * 2, out_specs=(near,) * 4 + (whole,), compiler_params=params(20), name="first_fold",
+    )(hold_l, hold_l, came_l, came_l, hold_m, hold_m, came_m, came_m, gram, gram_came)
+
+    def fold(step, send_l, hold_l, send_m, hold_m, came_l, came_m, *due):
         part = shape(bf16, half >> (step + 1), blk, rank)
         return pl.pallas_call(
-            fold_kernel, out_shape=(part,) * 4, in_specs=[vmem] * 4 + [anywhere], out_specs=(vmem,) * 4,
+            fold_kernel, out_shape=(part,) * 4, in_specs=[vmem] * 4 + [anywhere] * len(due), out_specs=(vmem,) * 4,
             compiler_params=params(16), name="fold",
-        )(hold_l, came_l, hold_m, came_m, after)
-
+        )(hold_l, came_l, hold_m, came_m, *due)
+
+    came_l, came_m = swap(send_l, 1 << order_a[1], n), swap(send_m, 1 << order_b[1], n)
     gram = gram + swap(gram, 1 << order_a[1], n)
-    came_l, came_m = swap(send_l, 1 << order_a[1], n), swap(send_m, 1 << order_b[1], n)
-    gram_came = swap(gram, 1 << order_a[2], n)
     av = pl.pallas_call(
         plans_lead_kernel, out_shape=square, in_specs=[vmem, anywhere], out_specs=vmem,
-        scratch_shapes=[pair], compiler_params=params(16), name="plans_lead",
-    )(ss, gram)
-    send_l, hold_l, send_m, hold_m = fold(1, send_l, hold_l, send_m, hold_m, came_l, came_m, av)
-    gram = gram + gram_came
-    for bit in range(3, bits):
-        gram = gram + swap(gram, 1 << bit, n)
-    gram_other = swap(gram, 1, n)
+        scratch_shapes=[pair], compiler_params=params(16), cost_estimate=cost(5), name="plans_lead",
+    )(ss, hold_l)
+    send_l, hold_l, send_m, hold_m = fold(1, send_l, hold_l, send_m, hold_m, came_l, came_m, av, gram)
     for step in range(2, bits - 1):
         came_l = swap(send_l, 1 << order_a[step], n)
         came_m = swap(send_m, 1 << order_b[step], n)
-        send_l, hold_l, send_m, hold_m = fold(step, send_l, hold_l, send_m, hold_m, came_l, came_m, gram_other)
+        gram = gram + swap(gram, 1 << order_a[step], n)
+        send_l, hold_l, send_m, hold_m = fold(step, send_l, hold_l, send_m, hold_m, came_l, came_m, gram)
+    gram = gram + swap(gram, 1 << order_a[-1], n)
+    gram_other = swap(gram, 1, n)
     came_l, came_m = swap(send_l, 1 << order_a[-1], n), swap(send_m, 1 << order_b[-1], n)
     lead = pl.pallas_call(
         lambda *refs: lead_kernel(cl / ck, *refs),
         out_shape=shape(f32, 8, rank, rank),
-        in_specs=[vmem] * 3 + [anywhere], out_specs=vmem,
+        in_specs=[vmem] * 3, out_specs=vmem,
         scratch_shapes=[pair, pltpu.VMEM((2 * rank + 16, rank), f32)],
-        compiler_params=params(16), name="lead",
-    )(gram, gram_other, av, hold_l)
+        compiler_params=params(16), cost_estimate=cost(6), name="lead",
+    )(gram, gram_other, av)
     basis_cells, ltu, d = pl.pallas_call(
         lambda *refs: cells_kernel(float(n_cells) ** 0.5, *refs),
         out_shape=(shape(f32, cells_dev, 2 * rank), square, square),
         in_specs=[vmem] * 3, out_specs=(vmem,) * 3, scratch_shapes=[pair],
-        compiler_params=params(16), name="cells",
+        compiler_params=params(16), cost_estimate=cost(8), name="cells",
     )(lead, cell_factor, k)
     lt, sums_send, sums = pl.pallas_call(
         pair_kernel, out_shape=(shape(f32, blk, rank), square, square),
         in_specs=[vmem] * 4 + [anywhere], out_specs=(vmem,) * 3,
         scratch_shapes=[pltpu.VMEM((2 * rank, rank), f32)],
         compiler_params=params(16), name="pair",
-    )(hold_l, came_l, hold_m, came_m, d)
+    )(hold_l, came_l, hold_m, came_m, lead)
     sums = sums + swap(sums_send, 1, n)
-    for bit in range(1, bits):
+    for bit in range(1, bits - 1):
         sums = sums + swap(sums, 1 << bit, n)
+    sums = pl.pallas_call(
+        add_kernel, out_shape=square, in_specs=[vmem] * 2 + [anywhere], out_specs=vmem,
+        compiler_params=params(16), name="add",
+    )(sums, swap(sums, 1 << (bits - 1), n), d)
     sums_other = swap(sums, 1, n)
     own = lax.dynamic_slice_in_dim(sched_factor, me * blk, blk, 0)
     scale = rank / (float(n_cells) * float(n_sched)) ** 0.5

time: 114 us -> 107 us (0.939)
  starting transfers between devices: 21.2 us -> 17.2 us
  waiting for transfers between devices: 35.9 us -> 33.1 us
  local copies, waits for them, and re-layouts: 2.48 us -> 4.27 us
    ppermute x18, starting transfers between devices: 21.2 us -> 17.2 us  [swap(): return lax.ppermute(x, 'cell', [(i, i ^ mask) for i in range(n)])]
    ppermute x18, waiting for transfers between devices: 35.9 us -> 33.1 us  [swap(): return lax.ppermute(x, 'cell', [(i, i ^ mask) for i in range(n)])]
    pallas_call x1, Pallas kernels: 24.3 us -> 23.1 us  [local(): pl.pallas_call(lambda *refs: state_kernel(ck, cl, relative, slot_of, *ref...]
    unnamed x10 -> x12, local copies, waits for them, and re-layouts: 2.46 us -> 3.35 us
  transfers between devices with their start and end apart: 18 -> 18, of which waited for: 10 -> 9; matrix products, arithmetic and copies ran while one was open for 1% -> 2% of each run, Pallas kernels for 17% -> 18%
where the time goes in v2:
time: 107 us
  Pallas kernels  50.8 us (47%)
  waiting for transfers between devices  33.1 us (31%)
  starting transfers between devices  17.2 us (16%)
  local copies, waits for them, and re-layouts  4.27 us (4%)
    ppermute x18, waiting for transfers between devices, swap(): return lax.ppermute(x, 'cell', [(i, i ^ mask) for i in range(n)])  33.1 us
    pallas_call x1, Pallas kernels, local(): pl.pallas_call(lambda *refs: state_kernel(ck, cl, relative, slot_of, *ref...  23.1 us
    ppermute x18, starting transfers between devices, swap(): return lax.ppermute(x, 'cell', [(i, i ^ mask) for i in range(n)])  17.2 us
    pallas_call x1, Pallas kernels, local(): pl.pallas_call(lambda *refs: cells_kernel(float(n_cells) ** 0.5, *refs),...  7.63 us
    pallas_call x1, Pallas kernels, local(): pl.pallas_call(lambda *refs: plans_kernel(float(n_sched) ** 0.5, ck, cl,...  7 us
    pallas_call x1, Pallas kernels, local(): pl.pallas_call(lambda *refs: lead_kernel(cl / ck, *refs), out_shape=shape...  5.88 us
    pallas_call x1, Pallas kernels, local(): pl.pallas_call(plans_lead_kernel, out_shape=square, in_specs=[vmem, anywh...  5.16 us
    unnamed x12, local copies, waits for them, and re-layouts  3.35 us
  transfers between devices with their start and end apart: 18, of which 9 were waited for; matrix products, arithmetic and copies ran while one was open for 2% of the time, Pallas kernels for 18%

profile of v2, /device:TPU:0, one launch (start us, length us, event | category | flops | bytes accessed | tf_op | source)
XLA Modules:
  0.0 106.9 jit_solution(17871659879241982504)
XLA Ops:
  0.6 23.1 %state.1 = (f32[1024,128]{1,0:T(8,128)}, f32[136,128]{1,0:T(8,128)}, f32[136,128]{1,0:T(8,128)}, bf16[8,512,128]{2,1,0:T(8,128)(2,1)}, bf16[8,512,128]{2,1,0:T(8...) custom-call(bf16[1024,128]{1,0:T(8,128)(2,1)} %refs_1_.1, bf16[16,512,128]{2,1,0:T(8,128)(2,1)} %bitcast.5, ...), custom_call_target="tpu_custom_call" | custom-call | tf_op jit(solution)/shard_map/state/pallas_call | solution.py:357
  23.7 0.5 collective-permute-start
  24.3 0.4 collective-permute-start.2
  24.7 3.6 %collective-permute-done.2.gram_came = f32[136,128]{1,0:T(8,128)S(1)} collective-permute-done((f32[136,128]{1,0:T(8,128)}, f32[136,128]{1,0:T(8,128)S(1)}, u32[]{:S(2)}, u32[]{:S(2)}) %collective-permute-start.2) | collective-permute-done | bytes 69664 | tf_op jit(solution)/shard_map/ppermute | solution.py:26
  28.3 1.2 %copy-done = bf16[8,512,128]{2,1,0:T(8,128)(2,1)S(1)} copy-done((bf16[8,512,128]{2,1,0:T(8,128)(2,1)S(1)}, bf16[8,512,128]{2,1,0:T(8,128)(2,1)}, u32[]{:S(2)}) %copy-start) | copy-done | bytes 1048600
  29.6 1.2 %copy-done.1 = bf16[8,512,128]{2,1,0:T(8,128)(2,1)S(1)} copy-done((bf16[8,512,128]{2,1,0:T(8,128)(2,1)S(1)}, bf16[8,512,128]{2,1,0:T(8,128)(2,1)}, u32[]{:S(2)}) %copy-start.1) | copy-done | bytes 1048600
  30.8 0.9 copy-done.4
  31.7 0.8 first_fold.1
  32.4 3.0 %collective-permute-start.7 = (bf16[4,512,128]{2,1,0:T(8,128)(2,1)S(1)}, bf16[4,512,128]{2,1,0:T(8,128)(2,1)S(1)}, u32[]{:S(2)}, u32[]{:S(2)}) collective-permute-start(bf16[4,512,128]{2,1,0:T(8,128)(2,1)S(1)} %get-tuple-element.41), channel_id=1, source_target_pairs={{0,2},{1,3},{2,0},{3,1},{4,6},{5,7},{6,4},{7,5},{8,10},{9,11},{10,... | collective-permute-start | bytes 1572872 | tf_op jit(solution)/shard_map/ppermute | solution.py:26
  35.4 1.6 %collective-permute-start.8 = (bf16[4,512,128]{2,1,0:T(8,128)(2,1)S(1)}, bf16[4,512,128]{2,1,0:T(8,128)(2,1)S(1)}, u32[]{:S(2)}, u32[]{:S(2)}) collective-permute-start(bf16[4,512,128]{2,1,0:T(8,128)(2,1)S(1)} %get-tuple-element.43), channel_id=1, source_target_pairs={{0,4},{1,5},{2,6},{3,7},{4,0},{5,1},{6,2},{7,3},{8,12},{9,13},{10,... | collective-permute-start | bytes 1572872 | tf_op jit(solution)/shard_map/ppermute | solution.py:26
  37.0 0.5 collective-permute-start.3
  37.5 0.7 fusion.ss_ref
  38.2 5.2 %plans_lead.1.refs_2_.rest_0_ = f32[128,128]{1,0:T(8,128)S(1)} custom-call(f32[128,128]{1,0:T(8,128)S(1)} %fusion.ss_ref, bf16[4,512,128]{2,1,0:T(8,128)(2,1)S(1)} %get-tuple-element.38.after.keep_l), custom_call_target="tpu_custom_call" | custom-call | bytes 18000000 | tf_op jit(solution)/shard_map/plans_lead/pallas_call | solution.py:413
  43.4 5.7 %collective-permute-done.3 = f32[136,128]{1,0:T(8,128)S(1)} collective-permute-done((f32[136,128]{1,0:T(8,128)S(1)}, f32[136,128]{1,0:T(8,128)S(1)}, u32[]{:S(2)}, u32[]{:S(2)}) %collective-permute-start.3) | collective-permute-done | bytes 69664 | tf_op jit(solution)/shard_map/ppermute | solution.py:26
  49.4 1.8 %collective-permute-start.10 = (bf16[2,512,128]{2,1,0:T(8,128)(2,1)S(1)}, bf16[2,512,128]{2,1,0:T(8,128)(2,1)S(1)}, u32[]{:S(2)}, u32[]{:S(2)}) collective-permute-start(bf16[2,512,128]{2,1,0:T(8,128)(2,1)S(1)} %get-tuple-element.47), channel_id=1, source_target_pairs={{0,2},{1,3},{2,0},{3,1},{4,6},{5,7},{6,4},{7,5},{8,10},{9,11},{10,... | collective-permute-start | bytes 786440 | tf_op jit(solution)/shard_map/ppermute | solution.py:26
  51.2 1.6 %collective-permute-start.9 = (bf16[2,512,128]{2,1,0:T(8,128)(2,1)S(1)}, bf16[2,512,128]{2,1,0:T(8,128)(2,1)S(1)}, u32[]{:S(2)}, u32[]{:S(2)}) collective-permute-start(bf16[2,512,128]{2,1,0:T(8,128)(2,1)S(1)} %get-tuple-element.45), channel_id=1, source_target_pairs={{0,4},{1,5},{2,6},{3,7},{4,0},{5,1},{6,2},{7,3},{8,12},{9,13},{10,... | collective-permute-start | bytes 786440 | tf_op jit(solution)/shard_map/ppermute | solution.py:26
  52.8 0.4 collective-permute-start.4
  53.3 6.7 %collective-permute-done.4 = f32[136,128]{1,0:T(8,128)S(1)} collective-permute-done((f32[136,128]{1,0:T(8,128)S(1)}, f32[136,128]{1,0:T(8,128)S(1)}, u32[]{:S(2)}, u32[]{:S(2)}) %collective-permute-start.4) | collective-permute-done | bytes 69664 | tf_op jit(solution)/shard_map/ppermute | solution.py:26
  60.0 2.6 %collective-permute-start.5 = (f32[136,128]{1,0:T(8,128)S(1)}, f32[136,128]{1,0:T(8,128)S(1)}, u32[]{:S(2)}, u32[]{:S(2)}) collective-permute-start(f32[136,128]{1,0:T(8,128)S(1)} %add.23.rest_0_), channel_id=1, source_target_pairs={{0,8},{1,9},{2,10},{3,11},{4,12},{5,13},{6,14},{7,15},{8,0},{9,1},... | collective-permute-start | bytes 208904 | tf_op jit(solution)/shard_map/ppermute | solution.py:26
  63.2 2.6 %collective-permute-start.12 = (bf16[1,512,128]{2,1,0:T(8,128)(2,1)S(1)}, bf16[1,512,128]{2,1,0:T(8,128)(2,1)S(1)}, u32[]{:S(2)}, u32[]{:S(2)}) collective-permute-start(bf16[1,512,128]{2,1,0:T(8,128)(2,1)S(1)} %get-tuple-element.51), channel_id=1, source_target_pairs={{0,8},{1,9},{2,10},{3,11},{4,12},{5,13},{6,14},{7,15},{8,0},{9,1},... | collective-permute-start | bytes 393224 | tf_op jit(solution)/shard_map/ppermute | solution.py:26
  65.8 6.5 %collective-permute-done.5 = f32[136,128]{1,0:T(8,128)S(1)} collective-permute-done((f32[136,128]{1,0:T(8,128)S(1)}, f32[136,128]{1,0:T(8,128)S(1)}, u32[]{:S(2)}, u32[]{:S(2)}) %collective-permute-start.5) | collective-permute-done | bytes 69664 | tf_op jit(solution)/shard_map/ppermute | solution.py:26
  72.4 1.2 %collective-permute-done.6.refs_1_ = f32[136,128]{1,0:T(8,128)S(1)} collective-permute-done((f32[136,128]{1,0:T(8,128)S(1)}, f32[136,128]{1,0:T(8,128)S(1)}, u32[]{:S(2)}, u32[]{:S(2)}) %collective-permute-start.6) | collective-permute-done | bytes 69664 | tf_op jit(solution)/shard_map/ppermute | solution.py:26
  73.6 5.9 %lead.1.refs_0_.after.refs_2_ = f32[8,128,128]{2,1,0:T(8,128)S(1)} custom-call(f32[136,128]{1,0:T(8,128)S(1)} %add.24.refs_0_, f32[136,128]{1,0:T(8,128)S(1)} %collective-permute-done.6.refs_1_, f32[128,128]{1,0:T(8,128)S(1)} %plans_lead.1.refs_2_.rest_0_), custom_call_target="tpu_custom_call" | custom-call | bytes 21600000 | tf_op jit(solution)/shard_map/lead/pallas_call | solution.py:426
  79.5 0.9 pair.1
  80.6 1.1 %collective-permute-done.13 = f32[128,128]{1,0:T(8,128)S(1)} collective-permute-done((f32[128,128]{1,0:T(8,128)S(1)}, f32[128,128]{1,0:T(8,128)S(1)}, u32[]{:S(2)}, u32[]{:S(2)}) %collective-permute-start.13) | collective-permute-done | bytes 65568 | tf_op jit(solution)/shard_map/ppermute | solution.py:26
  81.7 0.7 collective-permute-start.14
  82.4 3.6 %collective-permute-done.14 = f32[128,128]{1,0:T(8,128)S(1)} collective-permute-done((f32[128,128]{1,0:T(8,128)S(1)}, f32[128,128]{1,0:T(8,128)S(1)}, u32[]{:S(2)}, u32[]{:S(2)}) %collective-permute-start.14) | collective-permute-done | bytes 65568 | tf_op jit(solution)/shard_map/ppermute | solution.py:26
  86.1 4.3 %collective-permute-done.15 = f32[128,128]{1,0:T(8,128)S(1)} collective-permute-done((f32[128,128]{1,0:T(8,128)S(1)}, f32[128,128]{1,0:T(8,128)S(1)}, u32[]{:S(2)}, u32[]{:S(2)}) %collective-permute-start.15) | collective-permute-done | bytes 65568 | tf_op jit(solution)/shard_map/ppermute | solution.py:26
  90.4 0.6 collective-permute-start.16
  91.0 7.6 %cells.1 = (f32[1024,256]{1,0:T(8,128)}, f32[128,128]{1,0:T(8,128)S(1)}, f32[128,128]{1,0:T(8,128)S(1)}) custom-call(f32[8,128,128]{2,1,0:T(8,128)S(1)} %lead.1.refs_0_.after.refs_2_, bf16[1024,128]{1,0:T(8,128)(2,1)S(1)} %copy-done.2, f32[1024,128]{1,0:T(8,128)S(1)} %copy-done.3), custom_call_target="tpu_custom_call" | custom-call | bytes 28800000 | tf_op jit(solution)/shard_map/cells/pallas_call | solution.py:433
  98.7 0.9 constant_dynamic-slice_fusion.refs_5_
  99.9 7.0 %plans.1 = (f32[512,256]{1,0:T(8,128)}, f32[256,256]{1,0:T(8,128)}) custom-call(f32[128,128]{1,0:T(8,128)S(1)} %add.29.refs_0_, f32[128,128]{1,0:T(8,128)S(1)} %collective-permute-done.17.refs_1_, f32[8,128,128]{2,1,0:T(8,128)S(1)} %lead.1.refs_0_.after.refs_2_, f32[128,128]{1,0:T(8,128)S(1)} %get-tuple-element.55.refs_3_, ...), custom_call_target="tpu_custom_call" | custom-call | tf_op jit(solution)/shard_map/plans/pallas_call | solution.py:455
  (34 shorter events, 1.7 us)
Async XLA Ops:
  23.7 4.6 %collective-permute-start = (bf16[8,512,128]{2,1,0:T(8,128)(2,1)}, bf16[8,512,128]{2,1,0:T(8,128)(2,1)S(1)}, u32[]{:S(2)}, u32[]{:S(2)}) collective-permute-start(bf16[8,512,128]{2,1,0:T(8,128)(2,1)} %get-tuple-element.32), channel_id=1, source_target_pairs={{0,1},{1,0},{2,3},{3,2},{4,5},{5,4},{6,7},{7,6},{8,9},{9,8},{10,11... | collective-permute-start | bytes 3145736 | tf_op jit(solution)/shard_map/ppermute | solution.py:26
  24.2 4.1 %collective-permute-start.1 = (bf16[8,512,128]{2,1,0:T(8,128)(2,1)}, bf16[8,512,128]{2,1,0:T(8,128)(2,1)S(1)}, u32[]{:S(2)}, u32[]{:S(2)}) collective-permute-start(bf16[8,512,128]{2,1,0:T(8,128)(2,1)} %get-tuple-element.34), channel_id=1, source_target_pairs={{0,1},{1,0},{2,3},{3,2},{4,5},{5,4},{6,7},{7,6},{8,9},{9,8},{10,11... | collective-permute-start | bytes 3145736 | tf_op jit(solution)/shard_map/ppermute | solution.py:26
  24.3 4.0 %collective-permute-start.2 = (f32[136,128]{1,0:T(8,128)}, f32[136,128]{1,0:T(8,128)S(1)}, u32[]{:S(2)}, u32[]{:S(2)}) collective-permute-start(f32[136,128]{1,0:T(8,128)} %get-tuple-element.36), channel_id=1, source_target_pairs={{0,1},{1,0},{2,3},{3,2},{4,5},{5,4},{6,7},{7,6},{8,9},{9,8},{10,11... | collective-permute-start | bytes 208904 | tf_op jit(solution)/shard_map/ppermute | solution.py:26
  28.3 1.2 %copy-start = (bf16[8,512,128]{2,1,0:T(8,128)(2,1)S(1)}, bf16[8,512,128]{2,1,0:T(8,128)(2,1)}, u32[]{:S(2)}) copy-start(bf16[8,512,128]{2,1,0:T(8,128)(2,1)} %get-tuple-element.31.keep_l0.keep_l1) | copy-start | bytes 3145732
  29.6 1.2 %copy-start.1 = (bf16[8,512,128]{2,1,0:T(8,128)(2,1)S(1)}, bf16[8,512,128]{2,1,0:T(8,128)(2,1)}, u32[]{:S(2)}) copy-start(bf16[8,512,128]{2,1,0:T(8,128)(2,1)} %get-tuple-element.33.keep_m0.keep_m1) | copy-start | bytes 3145732
  30.8 0.9 copy-start.4
  31.7 5.8 %copy-start.5 = (bf16[8192,128]{1,0:T(8,128)(2,1)S(1)}, bf16[8192,128]{1,0:T(8,128)(2,1)}, u32[]{:S(2)}) copy-start(bf16[8192,128]{1,0:T(8,128)(2,1)} %param.7) | copy-start | bytes 6291460
  32.4 16.7 %collective-permute-start.7 = (bf16[4,512,128]{2,1,0:T(8,128)(2,1)S(1)}, bf16[4,512,128]{2,1,0:T(8,128)(2,1)S(1)}, u32[]{:S(2)}, u32[]{:S(2)}) collective-permute-start(bf16[4,512,128]{2,1,0:T(8,128)(2,1)S(1)} %get-tuple-element.41), channel_id=1, source_target_pairs={{0,2},{1,3},{2,0},{3,1},{4,6},{5,7},{6,4},{7,5},{8,10},{9,11},{10,... | collective-permute-start | bytes 1572872 | tf_op jit(solution)/shard_map/ppermute | solution.py:26
  35.4 13.7 %collective-permute-start.8 = (bf16[4,512,128]{2,1,0:T(8,128)(2,1)S(1)}, bf16[4,512,128]{2,1,0:T(8,128)(2,1)S(1)}, u32[]{:S(2)}, u32[]{:S(2)}) collective-permute-start(bf16[4,512,128]{2,1,0:T(8,128)(2,1)S(1)} %get-tuple-element.43), channel_id=1, source_target_pairs={{0,4},{1,5},{2,6},{3,7},{4,0},{5,1},{6,2},{7,3},{8,12},{9,13},{10,... | collective-permute-start | bytes 1572872 | tf_op jit(solution)/shard_map/ppermute | solution.py:26
  37.0 12.1 %collective-permute-start.3 = (f32[136,128]{1,0:T(8,128)S(1)}, f32[136,128]{1,0:T(8,128)S(1)}, u32[]{:S(2)}, u32[]{:S(2)}) collective-permute-start(f32[136,128]{1,0:T(8,128)S(1)} %get-tuple-element.37), channel_id=1, source_target_pairs={{0,2},{1,3},{2,0},{3,1},{4,6},{5,7},{6,4},{7,5},{8,10},{9,11},{10,... | collective-permute-start | bytes 208904 | tf_op jit(solution)/shard_map/ppermute | solution.py:26
  49.4 41.6 %copy-start.2 = (bf16[1024,128]{1,0:T(8,128)(2,1)S(1)}, bf16[1024,128]{1,0:T(8,128)(2,1)}, u32[]{:S(2)}) copy-start(bf16[1024,128]{1,0:T(8,128)(2,1)} %refs_1_.1) | copy-start | bytes 786436
  49.4 41.6 %copy-start.3 = (f32[1024,128]{1,0:T(8,128)S(1)}, f32[1024,128]{1,0:T(8,128)}, u32[]{:S(2)}) copy-start(f32[1024,128]{1,0:T(8,128)} %get-tuple-element.39.refs_2_) | copy-start | bytes 1572868
  49.4 13.2 %collective-permute-start.10 = (bf16[2,512,128]{2,1,0:T(8,128)(2,1)S(1)}, bf16[2,512,128]{2,1,0:T(8,128)(2,1)S(1)}, u32[]{:S(2)}, u32[]{:S(2)}) collective-permute-start(bf16[2,512,128]{2,1,0:T(8,128)(2,1)S(1)} %get-tuple-element.47), channel_id=1, source_target_pairs={{0,2},{1,3},{2,0},{3,1},{4,6},{5,7},{6,4},{7,5},{8,10},{9,11},{10,... | collective-permute-start | bytes 786440 | tf_op jit(solution)/shard_map/ppermute | solution.py:26
  51.2 11.4 %collective-permute-start.9 = (bf16[2,512,128]{2,1,0:T(8,128)(2,1)S(1)}, bf16[2,512,128]{2,1,0:T(8,128)(2,1)S(1)}, u32[]{:S(2)}, u32[]{:S(2)}) collective-permute-start(bf16[2,512,128]{2,1,0:T(8,128)(2,1)S(1)} %get-tuple-element.45), channel_id=1, source_target_pairs={{0,4},{1,5},{2,6},{3,7},{4,0},{5,1},{6,2},{7,3},{8,12},{9,13},{10,... | collective-permute-start | bytes 786440 | tf_op jit(solution)/shard_map/ppermute | solution.py:26
  52.8 7.2 %collective-permute-start.4 = (f32[136,128]{1,0:T(8,128)S(1)}, f32[136,128]{1,0:T(8,128)S(1)}, u32[]{:S(2)}, u32[]{:S(2)}) collective-permute-start(f32[136,128]{1,0:T(8,128)S(1)} %add.22.rest_1_), channel_id=1, source_target_pairs={{0,4},{1,5},{2,6},{3,7},{4,0},{5,1},{6,2},{7,3},{8,12},{9,13},{10,... | collective-permute-start | bytes 208904 | tf_op jit(solution)/shard_map/ppermute | solution.py:26
  60.0 12.3 %collective-permute-start.5 = (f32[136,128]{1,0:T(8,128)S(1)}, f32[136,128]{1,0:T(8,128)S(1)}, u32[]{:S(2)}, u32[]{:S(2)}) collective-permute-start(f32[136,128]{1,0:T(8,128)S(1)} %add.23.rest_0_), channel_id=1, source_target_pairs={{0,8},{1,9},{2,10},{3,11},{4,12},{5,13},{6,14},{7,15},{8,0},{9,1},... | collective-permute-start | bytes 208904 | tf_op jit(solution)/shard_map/ppermute | solution.py:26
  62.8 16.7 %collective-permute-start.11 = (bf16[1,512,128]{2,1,0:T(8,128)(2,1)S(1)}, bf16[1,512,128]{2,1,0:T(8,128)(2,1)S(1)}, u32[]{:S(2)}, u32[]{:S(2)}) collective-permute-start(bf16[1,512,128]{2,1,0:T(8,128)(2,1)S(1)} %get-tuple-element.49), channel_id=1, source_target_pairs={{0,8},{1,9},{2,10},{3,11},{4,12},{5,13},{6,14},{7,15},{8,0},{9,1},... | collective-permute-start | bytes 393224 | tf_op jit(solution)/shard_map/ppermute | solution.py:26
  63.2 16.3 %collective-permute-start.12 = (bf16[1,512,128]{2,1,0:T(8,128)(2,1)S(1)}, bf16[1,512,128]{2,1,0:T(8,128)(2,1)S(1)}, u32[]{:S(2)}, u32[]{:S(2)}) collective-permute-start(bf16[1,512,128]{2,1,0:T(8,128)(2,1)S(1)} %get-tuple-element.51), channel_id=1, source_target_pairs={{0,8},{1,9},{2,10},{3,11},{4,12},{5,13},{6,14},{7,15},{8,0},{9,1},... | collective-permute-start | bytes 393224 | tf_op jit(solution)/shard_map/ppermute | solution.py:26
  72.3 1.3 %collective-permute-start.6 = (f32[136,128]{1,0:T(8,128)S(1)}, f32[136,128]{1,0:T(8,128)S(1)}, u32[]{:S(2)}, u32[]{:S(2)}) collective-permute-start(f32[136,128]{1,0:T(8,128)S(1)} %add.24.refs_0_), channel_id=1, source_target_pairs={{0,1},{1,0},{2,3},{3,2},{4,5},{5,4},{6,7},{7,6},{8,9},{9,8},{10,11... | collective-permute-start | bytes 208904 | tf_op jit(solution)/shard_map/ppermute | solution.py:26
  80.4 1.3 %collective-permute-start.13 = (f32[128,128]{1,0:T(8,128)S(1)}, f32[128,128]{1,0:T(8,128)S(1)}, u32[]{:S(2)}, u32[]{:S(2)}) collective-permute-start(f32[128,128]{1,0:T(8,128)S(1)} %get-tuple-element.53), channel_id=1, source_target_pairs={{0,1},{1,0},{2,3},{3,2},{4,5},{5,4},{6,7},{7,6},{8,9},{9,8},{10,11... | collective-permute-start | bytes 196616 | tf_op jit(solution)/shard_map/ppermute | solution.py:26
  81.7 4.3 %collective-permute-start.14 = (f32[128,128]{1,0:T(8,128)S(1)}, f32[128,128]{1,0:T(8,128)S(1)}, u32[]{:S(2)}, u32[]{:S(2)}) collective-permute-start(f32[128,128]{1,0:T(8,128)S(1)} %add.25), channel_id=1, source_target_pairs={{0,2},{1,3},{2,0},{3,1},{4,6},{5,7},{6,4},{7,5},{8,10},{9,11},{10,... | collective-permute-start | bytes 196616 | tf_op jit(solution)/shard_map/ppermute | solution.py:26
  86.1 4.3 %collective-permute-start.15 = (f32[128,128]{1,0:T(8,128)S(1)}, f32[128,128]{1,0:T(8,128)S(1)}, u32[]{:S(2)}, u32[]{:S(2)}) collective-permute-start(f32[128,128]{1,0:T(8,128)S(1)} %add.26), channel_id=1, source_target_pairs={{0,4},{1,5},{2,6},{3,7},{4,0},{5,1},{6,2},{7,3},{8,12},{9,13},{10,... | collective-permute-start | bytes 196616 | tf_op jit(solution)/shard_map/ppermute | solution.py:26
  90.4 8.2 %collective-permute-start.16 = (f32[128,128]{1,0:T(8,128)S(1)}, f32[128,128]{1,0:T(8,128)S(1)}, u32[]{:S(2)}, u32[]{:S(2)}) collective-permute-start(f32[128,128]{1,0:T(8,128)S(1)} %add.27.a_ref), channel_id=1, source_target_pairs={{0,8},{1,9},{2,10},{3,11},{4,12},{5,13},{6,14},{7,15},{8,0},{9,1},... | collective-permute-start | bytes 196616 | tf_op jit(solution)/shard_map/ppermute | solution.py:26
  98.6 1.3 %collective-permute-start.17 = (f32[128,128]{1,0:T(8,128)S(1)}, f32[128,128]{1,0:T(8,128)S(1)}, u32[]{:S(2)}, u32[]{:S(2)}) collective-permute-start(f32[128,128]{1,0:T(8,128)S(1)} %add.29.refs_0_), channel_id=1, source_target_pairs={{0,1},{1,0},{2,3},{3,2},{4,5},{5,4},{6,7},{7,6},{8,9},{9,8},{10,11... | collective-permute-start | bytes 196616 | tf_op jit(solution)/shard_map/ppermute | solution.py:26

commit v3 on v1

--- a/solution.py
+++ b/solution.py
@@ -26,28 +26,16 @@
     return lax.ppermute(x, "cell", [(i, i ^ mask) for i in range(n)])
 
 
-def diagonal(m):
-    return lax.broadcasted_iota(i32, (m, m), 0) - lax.broadcasted_iota(i32, (m, m), 1)
-
-
-def cut(rows_ref, send_ref, keep_ref):
-    half = send_ref.shape[0]
-    odd = lax.rem(lax.axis_index("cell"), 2)
-    send_ref[...] = rows_ref[pl.ds(pl.multiple_of((1 - odd) * half, 8), half), :]
-    keep_ref[...] = rows_ref[pl.ds(pl.multiple_of(odd * half, 8), half), :]
-
-
-def joined(rows_ref, mine_ref, other_ref):
-    half = mine_ref.shape[0]
-    odd = lax.rem(lax.axis_index("cell"), 2)
-    rows_ref[pl.ds(pl.multiple_of(odd * half, 8), half), :] = mine_ref[...]
-    rows_ref[pl.ds(pl.multiple_of((1 - odd) * half, 8), half), :] = other_ref[...]
+def all_sum(x, n):
+    parts = lax.all_to_all(x.reshape(n, x.shape[0] // n, x.shape[1]), "cell", 0, 0)
+    mine = jnp.sum(parts, axis=0)
+    return lax.all_to_all(jnp.broadcast_to(mine, parts.shape), "cell", 0, 0).reshape(x.shape)
 
 
 def state_kernel(ck, cl, relative, slot_of, c_hbm, s_hbm, core_hbm, table_hbm, well_hbm, prof_hbm,
-                 k_ref, gsend_ref, gkeep_ref, send_l, send_m, hold_l, hold_m,
+                 k_ref, gram_ref, send_l, send_m, hold_l, hold_m,
                  c_ref, s_ref, core_ref, table_ref, well_ref, prof_ref,
-                 g_ref, ft_ref, ps_ref, kt_ref, both_ref, inj_ref, l_ref, m_ref, gram_ref, sems, out_sems):
+                 g_ref, ft_ref, ps_ref, kt_ref, both_ref, inj_ref, l_ref, m_ref, sems, out_sems):
     n, blk, rank = s_ref.shape
     cells = c_ref.shape[0]
     half = n // 2
@@ -102,13 +90,9 @@
     inj_ref[profiles:, :] = a_lo
     cc = dot(ct, c, 1, 0)
     kk = dot(kt_hi, k_hi, 1, 0) + (dot(kt_hi, k_lo, 1, 0) + dot(kt_lo, k_hi, 1, 0))
-    below = diagonal(rank)
-    gram_ref[:rank, :] = dot(ct, k_hi, 1, 0) + dot(ct, k_lo, 1, 0)
-    gram_ref[rank : 2 * rank, :] = jnp.where(below > 0, cc, kk)
-    gram_ref[2 * rank :, :] = jnp.broadcast_to(
-        jnp.sum(jnp.where(below == 0, cc, 0.0), axis=0, keepdims=True), (16, rank)
-    )
-    cut(gram_ref, gsend_ref, gkeep_ref)
+    gram_ref[:rank, :] = cc
+    gram_ref[rank : 2 * rank, :] = dot(ct, k_hi, 1, 0) + dot(ct, k_lo, 1, 0)
+    gram_ref[2 * rank :, :] = kk
     me = lax.axis_index("cell")
 
     def outgoing(j, at, dst_l, dst_m):
@@ -131,7 +115,7 @@
                 copy.start()
             return carry
 
-        lax.fori_loop(0, half, body, 0)
+        lax.fori_loop(0, half, body, 0, unroll=2)
 
     def finish(first_slot, dst_l, dst_m):
         def body(at, carry):
@@ -159,7 +143,7 @@
             send[j] = (keep[half + j].astype(f32) + came[half + j].astype(f32)).astype(bf16)
 
 
-def first_fold_kernel(keep_l0, keep_l1, came_l0, came_l1, keep_m0, keep_m1, came_m0, came_m1, after,
+def first_fold_kernel(keep_l0, keep_l1, came_l0, came_l1, keep_m0, keep_m1, came_m0, came_m1,
                       send_l, hold_l, send_m, hold_m):
     for keep, came, out in (
         (keep_l0, came_l0, hold_l), (keep_l1, came_l1, send_l),
@@ -168,14 +152,13 @@
         out[...] = (keep[...].astype(f32) + came[...].astype(f32)).astype(bf16)
 
 
-def pair_kernel(keep_l, came_l, keep_m, came_m, after, l_ref, send_ref, keep_ref, sums_ref):
+def pair_kernel(keep_l, came_l, keep_m, came_m, after, l_ref, sums_ref):
     rank = l_ref.shape[1]
     l = keep_l[0].astype(f32) + came_l[0].astype(f32)
     m2 = keep_m[0].astype(f32) + came_m[0].astype(f32)
     l_ref[...] = l
     sums_ref[:rank, :] = dot(l, l, 0, 0, HI)
     sums_ref[rank:, :] = dot(m2, l, 0, 0, HI)
-    cut(sums_ref, send_ref, keep_ref)
 
 
 def spread(row, col, m):
@@ -247,17 +230,11 @@
     av_ref[...] = upper(w)[1]
 
 
-def lead_kernel(ratio, mine_ref, other_ref, av_ref, after, lead_ref, w, gram_ref):
+def lead_kernel(ratio, gram_ref, av_ref, lead_ref, w):
     m = av_ref.shape[0]
-    joined(gram_ref, mine_ref, other_ref)
-    below = diagonal(m)
-    mixed = gram_ref[m : 2 * m, :]
-    low = jnp.where(below > 0, mixed, 0.0)
-    high = jnp.where(below <= 0, mixed, 0.0)
-    strict = jnp.where(below < 0, mixed, 0.0)
-    load_gram(w, low + low.T + jnp.where(below == 0, gram_ref[2 * m : 2 * m + 1, :], 0.0))
+    load_gram(w, gram_ref[:m, :])
     av = av_ref[...]
-    ck = gram_ref[:m, :]
+    ck = gram_ref[m : 2 * m, :]
     l21v = dot(ck * ratio, av, 1, 1, HI)
     lead_ref[4] = av
     lead_ref[5] = l21v
@@ -269,7 +246,7 @@
     lead_ref[0] = a
     lead_ref[1] = l21u
     lead_ref[2] = dot(a, l21u, 0, 1, HI)
-    lead_ref[3] = high + strict.T - dot(l21u, l21u, 1, 1, HI)
+    lead_ref[3] = gram_ref[2 * m :, :] - dot(l21u, l21u, 1, 1, HI)
 
 
 def cells_kernel(root, lead_ref, c_ref, k_ref, basis_ref, lt_ref, inv_ref, w):
@@ -284,10 +261,9 @@
     basis_ref[:, m:] = dot(k_ref[...] - dot(c, lead_ref[2], 1, 0, HI), d, 1, 1, HI) * root
 
 
-def plans_kernel(root, ck, cl, scale, mine_ref, other_ref, lead_ref, ltu_ref, d_ref, s_ref, l_ref,
-                 basis_ref, core_ref, w, sums_ref):
+def plans_kernel(root, ck, cl, scale, sums_ref, lead_ref, ltu_ref, d_ref, s_ref, l_ref,
+                 basis_ref, core_ref, w):
     m = w.shape[0]
-    joined(sums_ref, mine_ref, other_ref)
     ll = sums_ref[:m, :]
     n22 = sums_ref[m:, :]
     load_gram(w, ll - lead_ref[7])
@@ -306,6 +282,10 @@
     core_ref[m:, m:] = dot(e, dv, 1, 1, HI) * scale
 
 
+def cost(units):
+    return pl.CostEstimate(flops=0, bytes_accessed=units * 3_600_000, transcendentals=0)
+
+
 def params(mib):
     return pltpu.CompilerParams(vmem_limit_bytes=mib << 20)
 
@@ -340,12 +320,11 @@
         return jax.ShapeDtypeStruct(dims, dtype)
 
     part = shape(bf16, half, blk, rank)
-    gram_half = shape(f32, rank + 8, rank)
-    k, gram_send, gram, send_l, send_m, hold_l, hold_m = pl.pallas_call(
+    k, gram, send_l, send_m, hold_l, hold_m = pl.pallas_call(
         lambda *refs: state_kernel(ck, cl, relative, slot_of, *refs),
-        out_shape=(shape(f32, cells_dev, rank), gram_half, gram_half, part, part, part, part),
+        out_shape=(shape(f32, cells_dev, rank), shape(f32, 3 * rank, rank), part, part, part, part),
         in_specs=[hbm] * 6,
-        out_specs=(vmem,) * 3 + (hbm,) * 4,
+        out_specs=(vmem,) * 2 + (hbm,) * 4,
         scratch_shapes=[
             pltpu.VMEM((cells_dev, rank), bf16),
             pltpu.VMEM((n, blk, rank), bf16),
@@ -361,7 +340,6 @@
             pltpu.VMEM((2 * profiles, 2 * rank), bf16),
             pltpu.VMEM((n, blk, rank), bf16),
             pltpu.VMEM((n, blk, rank), bf16),
-            pltpu.VMEM((2 * rank + 16, rank), f32),
             pltpu.SemaphoreType.DMA((6,)),
             pltpu.SemaphoreType.DMA((2, n)),
         ],
@@ -376,7 +354,6 @@
     square = shape(f32, rank, rank)
 
     came_l, came_m = swap(send_l, 1, n), swap(send_m, 1, n)
-    gram = gram + swap(gram_send, 1, n)
     quarter = half // 2
     block = (1, blk, rank)
     near = pl.BlockSpec(block, lambda j: (j, 0, 0))
@@ -384,8 +361,8 @@
     part = shape(bf16, quarter, blk, rank)
     send_l, hold_l, send_m, hold_m = pl.pallas_call(
         first_fold_kernel, grid=(quarter,), out_shape=(part,) * 4,
-        in_specs=[near, far] * 4 + [anywhere], out_specs=(near,) * 4, compiler_params=params(20), name="first_fold",
-    )(hold_l, hold_l, came_l, came_l, hold_m, hold_m, came_m, came_m, gram)
+        in_specs=[near, far] * 4, out_specs=(near,) * 4, compiler_params=params(20), name="first_fold",
+    )(hold_l, hold_l, came_l, came_l, hold_m, hold_m, came_m, came_m)
 
     def fold(step, send_l, hold_l, send_m, hold_m, came_l, came_m, after):
         part = shape(bf16, half >> (step + 1), blk, rank)
@@ -394,46 +371,36 @@
             compiler_params=params(16), name="fold",
         )(hold_l, came_l, hold_m, came_m, after)
 
-    gram = gram + swap(gram, 1 << order_a[1], n)
     came_l, came_m = swap(send_l, 1 << order_a[1], n), swap(send_m, 1 << order_b[1], n)
-    gram_came = swap(gram, 1 << order_a[2], n)
+    gram = all_sum(gram, n)
     av = pl.pallas_call(
         plans_lead_kernel, out_shape=square, in_specs=[vmem, anywhere], out_specs=vmem,
-        scratch_shapes=[pair], compiler_params=params(16), name="plans_lead",
-    )(ss, gram)
+        scratch_shapes=[pair], compiler_params=params(16), cost_estimate=cost(5), name="plans_lead",
+    )(ss, hold_l)
     send_l, hold_l, send_m, hold_m = fold(1, send_l, hold_l, send_m, hold_m, came_l, came_m, av)
-    gram = gram + gram_came
-    for bit in range(3, bits):
-        gram = gram + swap(gram, 1 << bit, n)
-    gram_other = swap(gram, 1, n)
     for step in range(2, bits - 1):
         came_l = swap(send_l, 1 << order_a[step], n)
         came_m = swap(send_m, 1 << order_b[step], n)
-        send_l, hold_l, send_m, hold_m = fold(step, send_l, hold_l, send_m, hold_m, came_l, came_m, gram_other)
+        send_l, hold_l, send_m, hold_m = fold(step, send_l, hold_l, send_m, hold_m, came_l, came_m, av)
     came_l, came_m = swap(send_l, 1 << order_a[-1], n), swap(send_m, 1 << order_b[-1], n)
     lead = pl.pallas_call(
         lambda *refs: lead_kernel(cl / ck, *refs),
         out_shape=shape(f32, 8, rank, rank),
-        in_specs=[vmem] * 3 + [anywhere], out_specs=vmem,
-        scratch_shapes=[pair, pltpu.VMEM((2 * rank + 16, rank), f32)],
-        compiler_params=params(16), name="lead",
-    )(gram, gram_other, av, hold_l)
+        in_specs=[vmem] * 2, out_specs=vmem, scratch_shapes=[pair],
+        compiler_params=params(16), cost_estimate=cost(6), name="lead",
+    )(gram, av)
     basis_cells, ltu, d = pl.pallas_call(
         lambda *refs: cells_kernel(float(n_cells) ** 0.5, *refs),
         out_shape=(shape(f32, cells_dev, 2 * rank), square, square),
         in_specs=[vmem] * 3, out_specs=(vmem,) * 3, scratch_shapes=[pair],
-        compiler_params=params(16), name="cells",
+        compiler_params=params(16), cost_estimate=cost(8), name="cells",
     )(lead, cell_factor, k)
-    lt, sums_send, sums = pl.pallas_call(
-        pair_kernel, out_shape=(shape(f32, blk, rank), square, square),
-        in_specs=[vmem] * 4 + [anywhere], out_specs=(vmem,) * 3,
-        scratch_shapes=[pltpu.VMEM((2 * rank, rank), f32)],
+    lt, sums = pl.pallas_call(
+        pair_kernel, out_shape=(shape(f32, blk, rank), shape(f32, 2 * rank, rank)),
+        in_specs=[vmem] * 4 + [anywhere], out_specs=(vmem,) * 2,
         compiler_params=params(16), name="pair",
-    )(hold_l, came_l, hold_m, came_m, d)
-    sums = sums + swap(sums_send, 1, n)
-    for bit in range(1, bits):
-        sums = sums + swap(sums, 1 << bit, n)
-    sums_other = swap(sums, 1, n)
+    )(hold_l, came_l, hold_m, came_m, av)
+    sums = all_sum(sums, n)
     own = lax.dynamic_slice_in_dim(sched_factor, me * blk, blk, 0)
     scale = rank / (float(n_cells) * float(n_sched)) ** 0.5
     basis_sched, core_out = pl.pallas_call(
@@ -442,10 +409,9 @@
             jax.ShapeDtypeStruct((blk, 2 * rank), f32),
             jax.ShapeDtypeStruct((2 * rank, 2 * rank), f32),
         ),
-        in_specs=[vmem] * 7, out_specs=(vmem,) * 2,
-        scratch_shapes=[pair, pltpu.VMEM((2 * rank, rank), f32)],
+        in_specs=[vmem] * 6, out_specs=(vmem,) * 2, scratch_shapes=[pair],
         compiler_params=params(16), name="plans",
-    )(sums, sums_other, lead, ltu, d, own, lt)
+    )(sums, lead, ltu, d, own, lt)
     return (basis_cells, basis_sched, core_out)
 
 

time: 114 us -> 127 us (1.11)
  waiting for transfers between devices: 35.9 us -> 43.3 us
  starting transfers between devices: 21.2 us -> 26.1 us
  local copies, waits for them, and re-layouts: 2.48 us -> 4.73 us
    all_to_all x0 -> x4, waiting for transfers between devices: none -> 16.8 us  [the longest x2 8.94 us: all_sum(): lax.all_to_all(jnp.broadcast_to(mine, parts.shape), 'cell', 0, 0)]
    all_to_all x0 -> x4, starting transfers between devices: none -> 15.9 us  [the longest x2 8.67 us: all_sum(): lax.all_to_all(x.reshape(n, x.shape[0] // n, x.shape[1]), 'cell', 0, 0)]
    ppermute x18 -> x8, starting transfers between devices: 21.2 us -> 10.2 us  [swap(): return lax.ppermute(x, 'cell', [(i, i ^ mask) for i in range(n)])]
    ppermute x18 -> x8, waiting for transfers between devices: 35.9 us -> 26.5 us  [swap(): return lax.ppermute(x, 'cell', [(i, i ^ mask) for i in range(n)])]
    broadcast_in_dim x0 -> x2, local copies, waits for them, and re-layouts: none -> 1.35 us  [all_sum(): jnp.broadcast_to(mine, parts.shape)]
  transfers between devices with their start and end apart: 18 -> 12, of which waited for: 10 -> 10; matrix products, arithmetic and copies ran while one was open for 1% -> 1% of each run, Pallas kernels for 17% -> 16%
where the time goes in v3:
time: 127 us
  Pallas kernels  51 us (40%)
  waiting for transfers between devices  43.3 us (34%)
  starting transfers between devices  26.1 us (21%)
  local copies, waits for them, and re-layouts  4.73 us (4%)
    ppermute x8, waiting for transfers between devices, swap(): return lax.ppermute(x, 'cell', [(i, i ^ mask) for i in range(n)])  26.5 us
    pallas_call x1, Pallas kernels, local(): pl.pallas_call(lambda *refs: state_kernel(ck, cl, relative, slot_of, *ref...  23.1 us
    ppermute x8, starting transfers between devices, swap(): return lax.ppermute(x, 'cell', [(i, i ^ mask) for i in range(n)])  10.2 us
    all_to_all x2, waiting for transfers between devices, all_sum(): lax.all_to_all(jnp.broadcast_to(mine, parts.shape), 'cell', 0, 0)  8.94 us
    all_to_all x2, starting transfers between devices, all_sum(): lax.all_to_all(x.reshape(n, x.shape[0] // n, x.shape[1]), 'cell', 0, 0)  8.67 us
    all_to_all x2, waiting for transfers between devices, all_sum(): lax.all_to_all(x.reshape(n, x.shape[0] // n, x.shape[1]), 'cell', 0, 0)  7.91 us
    pallas_call x1, Pallas kernels, local(): pl.pallas_call(lambda *refs: cells_kernel(float(n_cells) ** 0.5, *refs),...  7.63 us
    all_to_all x2, starting transfers between devices, all_sum(): lax.all_to_all(jnp.broadcast_to(mine, parts.shape), 'cell', 0, 0)  7.22 us
  transfers between devices with their start and end apart: 12, of which 10 were waited for; matrix products, arithmetic and copies ran while one was open for 1% of the time, Pallas kernels for 16%

profile of v3, /device:TPU:0, one launch (start us, length us, event | category | flops | bytes accessed | tf_op | source)
XLA Modules:
  0.0 126.8 jit_solution(13354914152902281326)
XLA Ops:
  0.6 23.1 %state.1 = (f32[1024,128]{1,0:T(8,128)}, f32[384,128]{1,0:T(8,128)}, bf16[8,512,128]{2,1,0:T(8,128)(2,1)}, bf16[8,512,128]{2,1,0:T(8,128)(2,1)}, bf16[8,512,128]...) custom-call(bf16[1024,128]{1,0:T(8,128)(2,1)} %refs_1_.1, bf16[16,512,128]{2,1,0:T(8,128)(2,1)} %bitcast.11, ...), custom_call_target="tpu_custom_call" | custom-call | tf_op jit(solution)/shard_map/state/pallas_call | solution.py:323
  23.7 0.5 collective-permute-start
  24.3 2.4 %collective-permute-done.came_l0.came_l1 = bf16[8,512,128]{2,1,0:T(8,128)(2,1)S(1)} collective-permute-done((bf16[8,512,128]{2,1,0:T(8,128)(2,1)}, bf16[8,512,128]{2,1,0:T(8,128)(2,1)S(1)}, u32[]{:S(2)}, u32[]{:S(2)}) %collective-permute-start) | collective-permute-done | bytes 1048608 | tf_op jit(solution)/shard_map/ppermute | solution.py:26
  26.7 1.5 %collective-permute-done.1.came_m0.came_m1 = bf16[8,512,128]{2,1,0:T(8,128)(2,1)S(1)} collective-permute-done((bf16[8,512,128]{2,1,0:T(8,128)(2,1)}, bf16[8,512,128]{2,1,0:T(8,128)(2,1)S(1)}, u32[]{:S(2)}, u32[]{:S(2)}) %collective-permute-start.1) | collective-permute-done | bytes 1048608 | tf_op jit(solution)/shard_map/ppermute | solution.py:26
  28.2 1.2 copy-done
  29.5 1.2 copy-done.1
  30.7 0.5 first_fold.1
  31.2 3.0 %collective-permute-start.2 = (bf16[4,512,128]{2,1,0:T(8,128)(2,1)S(1)}, bf16[4,512,128]{2,1,0:T(8,128)(2,1)S(1)}, u32[]{:S(2)}, u32[]{:S(2)}) collective-permute-start(bf16[4,512,128]{2,1,0:T(8,128)(2,1)S(1)} %get-tuple-element.36), channel_id=1, source_target_pairs={{0,2},{1,3},{2,0},{3,1},{4,6},{5,7},{6,4},{7,5},{8,10},{9,11},{10,... | collective-permute-start | bytes 1572872 | tf_op jit(solution)/shard_map/ppermute | solution.py:26
  34.2 1.6 %collective-permute-start.3 = (bf16[4,512,128]{2,1,0:T(8,128)(2,1)S(1)}, bf16[4,512,128]{2,1,0:T(8,128)(2,1)S(1)}, u32[]{:S(2)}, u32[]{:S(2)}) collective-permute-start(bf16[4,512,128]{2,1,0:T(8,128)(2,1)S(1)} %get-tuple-element.38), channel_id=1, source_target_pairs={{0,4},{1,5},{2,6},{3,7},{4,0},{5,1},{6,2},{7,3},{8,12},{9,13},{10,... | collective-permute-start | bytes 1572872 | tf_op jit(solution)/shard_map/ppermute | solution.py:26
  35.7 0.8 fusion.ss_ref
  36.5 5.2 %plans_lead.1.refs_1_.after = f32[128,128]{1,0:T(8,128)S(1)} custom-call(f32[128,128]{1,0:T(8,128)S(1)} %fusion.ss_ref, bf16[4,512,128]{2,1,0:T(8,128)(2,1)S(1)} %get-tuple-element.33.after.keep_l), custom_call_target="tpu_custom_call" | custom-call | bytes 18000000 | tf_op jit(solution)/shard_map/plans_lead/pallas_call | solution.py:376
  41.7 4.7 %collective-permute-done.2.came_l = bf16[4,512,128]{2,1,0:T(8,128)(2,1)S(1)} collective-permute-done((bf16[4,512,128]{2,1,0:T(8,128)(2,1)S(1)}, bf16[4,512,128]{2,1,0:T(8,128)(2,1)S(1)}, u32[]{:S(2)}, u32[]{:S(2)}) %collective-permute-start.2) | collective-permute-done | bytes 524320 | tf_op jit(solution)/shard_map/ppermute | solution.py:26
  46.4 1.5 %collective-permute-done.3.came_m = bf16[4,512,128]{2,1,0:T(8,128)(2,1)S(1)} collective-permute-done((bf16[4,512,128]{2,1,0:T(8,128)(2,1)S(1)}, bf16[4,512,128]{2,1,0:T(8,128)(2,1)S(1)}, u32[]{:S(2)}, u32[]{:S(2)}) %collective-permute-start.3) | collective-permute-done | bytes 524320 | tf_op jit(solution)/shard_map/ppermute | solution.py:26
  48.1 1.6 %collective-permute-start.4 = (bf16[2,512,128]{2,1,0:T(8,128)(2,1)S(1)}, bf16[2,512,128]{2,1,0:T(8,128)(2,1)S(1)}, u32[]{:S(2)}, u32[]{:S(2)}) collective-permute-start(bf16[2,512,128]{2,1,0:T(8,128)(2,1)S(1)} %get-tuple-element.40), channel_id=1, source_target_pairs={{0,4},{1,5},{2,6},{3,7},{4,0},{5,1},{6,2},{7,3},{8,12},{9,13},{10,... | collective-permute-start | bytes 786440 | tf_op jit(solution)/shard_map/ppermute | solution.py:26
  49.7 0.5 collective-permute-start.5
  50.2 4.9 %all-to-all-start = ((f32[16,24,128]{2,1,0:T(8,128)}), f32[16,24,128]{2,1,0:T(8,128)S(1)}, u32[]{:S(2)}, u32[]{:S(2)}) async-start(f32[16,24,128]{2,1,0:T(8,128)} %bitcast.3), calls=%async_computation | async-start | bytes 393216 | tf_op jit(solution)/shard_map/all_to_all | solution.py:30
  55.4 1.3 %collective-permute-done.5.came_m = bf16[2,512,128]{2,1,0:T(8,128)(2,1)S(1)} collective-permute-done((bf16[2,512,128]{2,1,0:T(8,128)(2,1)S(1)}, bf16[2,512,128]{2,1,0:T(8,128)(2,1)S(1)}, u32[]{:S(2)}, u32[]{:S(2)}) %collective-permute-start.5) | collective-permute-done | bytes 262176 | tf_op jit(solution)/shard_map/ppermute | solution.py:26
  56.8 2.7 %collective-permute-start.6 = (bf16[1,512,128]{2,1,0:T(8,128)(2,1)S(1)}, bf16[1,512,128]{2,1,0:T(8,128)(2,1)S(1)}, u32[]{:S(2)}, u32[]{:S(2)}) collective-permute-start(bf16[1,512,128]{2,1,0:T(8,128)(2,1)S(1)} %get-tuple-element.44), channel_id=1, source_target_pairs={{0,8},{1,9},{2,10},{3,11},{4,12},{5,13},{6,14},{7,15},{8,0},{9,1},... | collective-permute-start | bytes 393224 | tf_op jit(solution)/shard_map/ppermute | solution.py:26
  59.8 12.5 %collective-permute-done.6.came_l = bf16[1,512,128]{2,1,0:T(8,128)(2,1)S(1)} collective-permute-done((bf16[1,512,128]{2,1,0:T(8,128)(2,1)S(1)}, bf16[1,512,128]{2,1,0:T(8,128)(2,1)S(1)}, u32[]{:S(2)}, u32[]{:S(2)}) %collective-permute-start.6) | collective-permute-done | bytes 131104 | tf_op jit(solution)/shard_map/ppermute | solution.py:26
  72.3 2.3 %collective-permute-done.7.came_m = bf16[1,512,128]{2,1,0:T(8,128)(2,1)S(1)} collective-permute-done((bf16[1,512,128]{2,1,0:T(8,128)(2,1)S(1)}, bf16[1,512,128]{2,1,0:T(8,128)(2,1)S(1)}, u32[]{:S(2)}, u32[]{:S(2)}) %collective-permute-start.7) | collective-permute-done | bytes 131104 | tf_op jit(solution)/shard_map/ppermute | solution.py:26
  74.7 1.3 %pair.1 = (f32[512,128]{1,0:T(8,128)S(1)}, f32[256,128]{1,0:T(8,128)}) custom-call(bf16[1,512,128]{2,1,0:T(8,128)(2,1)S(1)} %get-tuple-element.43.keep_l, bf16[1,512,128]{2,1,0:T(8,128)(2,1)S(1)} %collective-permute-done.6.came_l, bf16[1,512,128]{2,1,0:T(8,128)(2,1)S(1)} %get-tuple-element.45.keep_m, bf16[1,512,128]{2,1,0:T(8,128)(2,1)S(1)} %collective-permute-done.7.came_m, ...), custom_call_target="tpu_custom_call" | custom-call | tf_op jit(solution)/shard_map/pair/pallas_call | solution.py:398
  76.0 3.7 %all-to-all-start.2 = ((f32[16,16,128]{2,1,0:T(8,128)}), f32[16,16,128]{2,1,0:T(8,128)S(1)}, u32[]{:S(2)}, u32[]{:S(2)}) async-start(f32[16,16,128]{2,1,0:T(8,128)} %bitcast.5), calls=%async_computation.2 | async-start | bytes 262144 | tf_op jit(solution)/shard_map/all_to_all | solution.py:30
  79.7 7.9 %all-to-all-done.2 = f32[16,16,128]{2,1,0:T(8,128)S(1)} async-done(((f32[16,16,128]{2,1,0:T(8,128)}), f32[16,16,128]{2,1,0:T(8,128)S(1)}, u32[]{:S(2)}, u32[]{:S(2)}) %all-to-all-start.2) | async-done | bytes 131104 | tf_op jit(solution)/shard_map/all_to_all | solution.py:30
  87.6 0.7 broadcast_in_dim.6
  88.3 3.5 %all-to-all-start.1 = ((f32[16,24,128]{2,1,0:T(8,128)}), f32[16,24,128]{2,1,0:T(8,128)S(1)}, u32[]{:S(2)}, u32[]{:S(2)}) async-start(f32[16,24,128]{2,1,0:T(8,128)} %broadcast_in_dim.6), calls=%async_computation.1 | async-start | bytes 393216 | tf_op jit(solution)/shard_map/all_to_all | solution.py:32
  91.9 8.9 %all-to-all-done.1 = f32[16,24,128]{2,1,0:T(8,128)S(1)} async-done(((f32[16,24,128]{2,1,0:T(8,128)}), f32[16,24,128]{2,1,0:T(8,128)S(1)}, u32[]{:S(2)}, u32[]{:S(2)}) %all-to-all-start.1) | async-done | bytes 196640 | tf_op jit(solution)/shard_map/all_to_all | solution.py:32
  100.8 0.7 broadcast_in_dim.7
  101.5 3.7 %all-to-all-start.3 = ((f32[16,16,128]{2,1,0:T(8,128)}), f32[16,16,128]{2,1,0:T(8,128)S(1)}, u32[]{:S(2)}, u32[]{:S(2)}) async-start(f32[16,16,128]{2,1,0:T(8,128)} %broadcast_in_dim.7), calls=%async_computation.3 | async-start | bytes 262144 | tf_op jit(solution)/shard_map/all_to_all | solution.py:32
  105.2 0.9 constant_dynamic-slice_fusion.refs_4_
  106.1 5.8 %lead.1.refs_0_.refs_1_ = f32[8,128,128]{2,1,0:T(8,128)S(1)} custom-call(f32[384,128]{1,0:T(8,128)S(1)} %bitcast.9, f32[128,128]{1,0:T(8,128)S(1)} %plans_lead.1.refs_1_.after), custom_call_target="tpu_custom_call" | custom-call | bytes 21600000 | tf_op jit(solution)/shard_map/lead/pallas_call | solution.py:386
  111.9 7.6 %cells.1 = (f32[1024,256]{1,0:T(8,128)}, f32[128,128]{1,0:T(8,128)S(1)}, f32[128,128]{1,0:T(8,128)S(1)}) custom-call(f32[8,128,128]{2,1,0:T(8,128)S(1)} %lead.1.refs_0_.refs_1_, bf16[1024,128]{1,0:T(8,128)(2,1)S(1)} %copy-done.2, f32[1024,128]{1,0:T(8,128)S(1)} %copy-done.3), custom_call_target="tpu_custom_call" | custom-call | bytes 28800000 | tf_op jit(solution)/shard_map/cells/pallas_call | solution.py:392
  119.6 7.2 %plans.1 = (f32[512,256]{1,0:T(8,128)}, f32[256,256]{1,0:T(8,128)}) custom-call(f32[256,128]{1,0:T(8,128)S(1)} %bitcast.10, f32[8,128,128]{2,1,0:T(8,128)S(1)} %lead.1.refs_0_.refs_1_, f32[128,128]{1,0:T(8,128)S(1)} %get-tuple-element.48.refs_2_, f32[128,128]{1,0:T(8,128)S(1)} %get-tuple-element.49.refs_3_, ...), custom_call_target="tpu_custom_call" | custom-call | tf_op jit(solution)/shard_map/plans/pallas_call | solution.py:406
  (17 shorter events, 1.0 us)
Async XLA Ops:
  23.7 3.0 %collective-permute-start = (bf16[8,512,128]{2,1,0:T(8,128)(2,1)}, bf16[8,512,128]{2,1,0:T(8,128)(2,1)S(1)}, u32[]{:S(2)}, u32[]{:S(2)}) collective-permute-start(bf16[8,512,128]{2,1,0:T(8,128)(2,1)} %get-tuple-element.30), channel_id=1, source_target_pairs={{0,1},{1,0},{2,3},{3,2},{4,5},{5,4},{6,7},{7,6},{8,9},{9,8},{10,11... | collective-permute-start | bytes 3145736 | tf_op jit(solution)/shard_map/ppermute | solution.py:26
  24.2 4.0 %collective-permute-start.1 = (bf16[8,512,128]{2,1,0:T(8,128)(2,1)}, bf16[8,512,128]{2,1,0:T(8,128)(2,1)S(1)}, u32[]{:S(2)}, u32[]{:S(2)}) collective-permute-start(bf16[8,512,128]{2,1,0:T(8,128)(2,1)} %get-tuple-element.32), channel_id=1, source_target_pairs={{0,1},{1,0},{2,3},{3,2},{4,5},{5,4},{6,7},{7,6},{8,9},{9,8},{10,11... | collective-permute-start | bytes 3145736 | tf_op jit(solution)/shard_map/ppermute | solution.py:26
  28.2 1.2 copy-start
  29.5 1.2 copy-start.1
  30.7 5.1 %copy-start.4 = (bf16[8192,128]{1,0:T(8,128)(2,1)S(1)}, bf16[8192,128]{1,0:T(8,128)(2,1)}, u32[]{:S(2)}) copy-start(bf16[8192,128]{1,0:T(8,128)(2,1)} %param.7) | copy-start | bytes 6291460
  31.2 15.2 %collective-permute-start.2 = (bf16[4,512,128]{2,1,0:T(8,128)(2,1)S(1)}, bf16[4,512,128]{2,1,0:T(8,128)(2,1)S(1)}, u32[]{:S(2)}, u32[]{:S(2)}) collective-permute-start(bf16[4,512,128]{2,1,0:T(8,128)(2,1)S(1)} %get-tuple-element.36), channel_id=1, source_target_pairs={{0,2},{1,3},{2,0},{3,1},{4,6},{5,7},{6,4},{7,5},{8,10},{9,11},{10,... | collective-permute-start | bytes 1572872 | tf_op jit(solution)/shard_map/ppermute | solution.py:26
  34.2 13.7 %collective-permute-start.3 = (bf16[4,512,128]{2,1,0:T(8,128)(2,1)S(1)}, bf16[4,512,128]{2,1,0:T(8,128)(2,1)S(1)}, u32[]{:S(2)}, u32[]{:S(2)}) collective-permute-start(bf16[4,512,128]{2,1,0:T(8,128)(2,1)S(1)} %get-tuple-element.38), channel_id=1, source_target_pairs={{0,4},{1,5},{2,6},{3,7},{4,0},{5,1},{6,2},{7,3},{8,12},{9,13},{10,... | collective-permute-start | bytes 1572872 | tf_op jit(solution)/shard_map/ppermute | solution.py:26
  48.1 7.3 %collective-permute-start.4 = (bf16[2,512,128]{2,1,0:T(8,128)(2,1)S(1)}, bf16[2,512,128]{2,1,0:T(8,128)(2,1)S(1)}, u32[]{:S(2)}, u32[]{:S(2)}) collective-permute-start(bf16[2,512,128]{2,1,0:T(8,128)(2,1)S(1)} %get-tuple-element.40), channel_id=1, source_target_pairs={{0,4},{1,5},{2,6},{3,7},{4,0},{5,1},{6,2},{7,3},{8,12},{9,13},{10,... | collective-permute-start | bytes 786440 | tf_op jit(solution)/shard_map/ppermute | solution.py:26
  49.7 6.9 %collective-permute-start.5 = (bf16[2,512,128]{2,1,0:T(8,128)(2,1)S(1)}, bf16[2,512,128]{2,1,0:T(8,128)(2,1)S(1)}, u32[]{:S(2)}, u32[]{:S(2)}) collective-permute-start(bf16[2,512,128]{2,1,0:T(8,128)(2,1)S(1)} %get-tuple-element.42), channel_id=1, source_target_pairs={{0,2},{1,3},{2,0},{3,1},{4,6},{5,7},{6,4},{7,5},{8,10},{9,11},{10,... | collective-permute-start | bytes 786440 | tf_op jit(solution)/shard_map/ppermute | solution.py:26
  50.2 25.7 %all-to-all-start = ((f32[16,24,128]{2,1,0:T(8,128)}), f32[16,24,128]{2,1,0:T(8,128)S(1)}, u32[]{:S(2)}, u32[]{:S(2)}) async-start(f32[16,24,128]{2,1,0:T(8,128)} %bitcast.3), calls=%async_computation | async-start | bytes 393216 | tf_op jit(solution)/shard_map/all_to_all | solution.py:30
  56.7 55.3 %copy-start.2 = (bf16[1024,128]{1,0:T(8,128)(2,1)S(1)}, bf16[1024,128]{1,0:T(8,128)(2,1)}, u32[]{:S(2)}) copy-start(bf16[1024,128]{1,0:T(8,128)(2,1)} %refs_1_.1) | copy-start | bytes 786436
  56.7 55.3 %copy-start.3 = (f32[1024,128]{1,0:T(8,128)S(1)}, f32[1024,128]{1,0:T(8,128)}, u32[]{:S(2)}) copy-start(f32[1024,128]{1,0:T(8,128)} %get-tuple-element.34.refs_2_) | copy-start | bytes 1572868
  56.8 15.5 %collective-permute-start.6 = (bf16[1,512,128]{2,1,0:T(8,128)(2,1)S(1)}, bf16[1,512,128]{2,1,0:T(8,128)(2,1)S(1)}, u32[]{:S(2)}, u32[]{:S(2)}) collective-permute-start(bf16[1,512,128]{2,1,0:T(8,128)(2,1)S(1)} %get-tuple-element.44), channel_id=1, source_target_pairs={{0,8},{1,9},{2,10},{3,11},{4,12},{5,13},{6,14},{7,15},{8,0},{9,1},... | collective-permute-start | bytes 393224 | tf_op jit(solution)/shard_map/ppermute | solution.py:26
  59.4 15.2 %collective-permute-start.7 = (bf16[1,512,128]{2,1,0:T(8,128)(2,1)S(1)}, bf16[1,512,128]{2,1,0:T(8,128)(2,1)S(1)}, u32[]{:S(2)}, u32[]{:S(2)}) collective-permute-start(bf16[1,512,128]{2,1,0:T(8,128)(2,1)S(1)} %get-tuple-element.46), channel_id=1, source_target_pairs={{0,8},{1,9},{2,10},{3,11},{4,12},{5,13},{6,14},{7,15},{8,0},{9,1},... | collective-permute-start | bytes 393224 | tf_op jit(solution)/shard_map/ppermute | solution.py:26
  76.0 11.7 %all-to-all-start.2 = ((f32[16,16,128]{2,1,0:T(8,128)}), f32[16,16,128]{2,1,0:T(8,128)S(1)}, u32[]{:S(2)}, u32[]{:S(2)}) async-start(f32[16,16,128]{2,1,0:T(8,128)} %bitcast.5), calls=%async_computation.2 | async-start | bytes 262144 | tf_op jit(solution)/shard_map/all_to_all | solution.py:30
  88.3 12.5 %all-to-all-start.1 = ((f32[16,24,128]{2,1,0:T(8,128)}), f32[16,24,128]{2,1,0:T(8,128)S(1)}, u32[]{:S(2)}, u32[]{:S(2)}) async-start(f32[16,24,128]{2,1,0:T(8,128)} %broadcast_in_dim.6), calls=%async_computation.1 | async-start | bytes 393216 | tf_op jit(solution)/shard_map/all_to_all | solution.py:32
  101.5 18.1 %all-to-all-start.3 = ((f32[16,16,128]{2,1,0:T(8,128)}), f32[16,16,128]{2,1,0:T(8,128)S(1)}, u32[]{:S(2)}, u32[]{:S(2)}) async-start(f32[16,16,128]{2,1,0:T(8,128)} %broadcast_in_dim.7), calls=%async_computation.3 | async-start | bytes 262144 | tf_op jit(solution)/shard_map/all_to_all | solution.py:32

commit v4 on v1

--- a/solution.py
+++ b/solution.py
@@ -20,6 +20,17 @@
 def split(x):
     hi = x.astype(bf16)
     return hi, (x - hi.astype(f32)).astype(bf16)
+
+
+def dot3(a, b, ca, cb):
+    a_hi, a_lo = split(a)
+    b_hi, b_lo = split(b)
+    return dot(a_hi, b_hi, ca, cb) + (dot(a_hi, b_lo, ca, cb) + dot(a_lo, b_hi, ca, cb))
+
+
+def against(rows, inv, cross):
+    hi, lo = split(jnp.concatenate([inv.T, cross], axis=1))
+    return dot(rows, hi, 1, 0) + dot(rows, lo, 1, 0)
 
 
 def swap(x, mask, n):
@@ -131,7 +142,7 @@
                 copy.start()
             return carry
 
-        lax.fori_loop(0, half, body, 0)
+        lax.fori_loop(0, half, body, 0, unroll=2)
 
     def finish(first_slot, dst_l, dst_m):
         def body(at, carry):
@@ -159,7 +170,7 @@
             send[j] = (keep[half + j].astype(f32) + came[half + j].astype(f32)).astype(bf16)
 
 
-def first_fold_kernel(keep_l0, keep_l1, came_l0, came_l1, keep_m0, keep_m1, came_m0, came_m1, after,
+def first_fold_kernel(keep_l0, keep_l1, came_l0, came_l1, keep_m0, keep_m1, came_m0, came_m1,
                       send_l, hold_l, send_m, hold_m):
     for keep, came, out in (
         (keep_l0, came_l0, hold_l), (keep_l1, came_l1, send_l),
@@ -176,6 +187,10 @@
     sums_ref[:rank, :] = dot(l, l, 0, 0, HI)
     sums_ref[rank:, :] = dot(m2, l, 0, 0, HI)
     cut(sums_ref, send_ref, keep_ref)
+
+
+def add_kernel(a_ref, b_ref, after, out_ref):
+    out_ref[...] = a_ref[...] + b_ref[...]
 
 
 def spread(row, col, m):
@@ -247,7 +262,7 @@
     av_ref[...] = upper(w)[1]
 
 
-def lead_kernel(ratio, mine_ref, other_ref, av_ref, after, lead_ref, w, gram_ref):
+def lead_kernel(ratio, mine_ref, other_ref, av_ref, lead_ref, w, gram_ref):
     m = av_ref.shape[0]
     joined(gram_ref, mine_ref, other_ref)
     below = diagonal(m)
@@ -275,13 +290,14 @@
 def cells_kernel(root, lead_ref, c_ref, k_ref, basis_ref, lt_ref, inv_ref, w):
     m = w.shape[0]
     load_gram(w, lead_ref[3])
+    both = against(c_ref[...], lead_ref[0], lead_ref[2])
+    basis_ref[:, :m] = both[:, :m] * root
+    basis_ref[:, m:] = k_ref[...] - both[:, m:]
     eliminate([w])
     lt, d = upper(w)
     lt_ref[...] = lt
     inv_ref[...] = d
-    c = c_ref[...].astype(f32)
-    basis_ref[:, :m] = dot(c, lead_ref[0], 1, 1, HI) * root
-    basis_ref[:, m:] = dot(k_ref[...] - dot(c, lead_ref[2], 1, 0, HI), d, 1, 1, HI) * root
+    basis_ref[:, m:] = dot3(basis_ref[:, m:], d * root, 1, 1)
 
 
 def plans_kernel(root, ck, cl, scale, mine_ref, other_ref, lead_ref, ltu_ref, d_ref, s_ref, l_ref,
@@ -291,19 +307,27 @@
     ll = sums_ref[:m, :]
     n22 = sums_ref[m:, :]
     load_gram(w, ll - lead_ref[7])
+    a, l21u, av, l21v, xv = (lead_ref[i] for i in (0, 1, 4, 5, 6))
+    d = d_ref[...]
+    both = against(s_ref[...], av, xv)
+    basis_ref[:, :m] = both[:, :m] * root
+    basis_ref[:, m:] = l_ref[...] - both[:, m:]
+    b = -dot(dot(d, l21u, 1, 0, HI), a, 1, 0, HI)
+    core_ref[m:, m:] = (
+        dot(b, ll, 1, 0, HI) * (1.0 / cl) + dot(d, n22, 1, 0, HI)
+        - dot(ltu_ref[...], xv, 1, 0, HI) * (1.0 / ck)
+    )
+    core_ref[:m, :m] = dot(a, l21v, 1, 0, HI) * (scale / cl)
+    core_ref[m:, :m] = dot(ltu_ref[...], av, 1, 1, HI) * (scale / ck)
     eliminate([w])
     ltv, dv = upper(w)
-    a, l21u, av, l21v, xv = (lead_ref[i] for i in (0, 1, 4, 5, 6))
-    d = d_ref[...]
-    own = s_ref[...].astype(f32)
-    basis_ref[:, :m] = dot(own, av, 1, 1, HI) * root
-    basis_ref[:, m:] = dot(l_ref[...] - dot(own, xv, 1, 0, HI), dv, 1, 1, HI) * root
-    b = -dot(dot(d, l21u, 1, 0, HI), a, 1, 0, HI)
-    e = dot(b, ll, 1, 0, HI) * (1.0 / cl) + dot(d, n22, 1, 0, HI) - dot(ltu_ref[...], xv, 1, 0, HI) * (1.0 / ck)
-    core_ref[:m, :m] = dot(a, l21v, 1, 0, HI) * (scale / cl)
+    basis_ref[:, m:] = dot3(basis_ref[:, m:], dv * root, 1, 1)
     core_ref[:m, m:] = dot(a, ltv, 1, 1, HI) * (scale / cl)
-    core_ref[m:, :m] = dot(ltu_ref[...], av, 1, 1, HI) * (scale / ck)
-    core_ref[m:, m:] = dot(e, dv, 1, 1, HI) * scale
+    core_ref[m:, m:] = dot(core_ref[m:, m:], dv, 1, 1, HI) * scale
+
+
+def cost(units):
+    return pl.CostEstimate(flops=0, bytes_accessed=units * 3_600_000, transcendentals=0)
 
 
 def params(mib):
@@ -384,8 +408,8 @@
     part = shape(bf16, quarter, blk, rank)
     send_l, hold_l, send_m, hold_m = pl.pallas_call(
         first_fold_kernel, grid=(quarter,), out_shape=(part,) * 4,
-        in_specs=[near, far] * 4 + [anywhere], out_specs=(near,) * 4, compiler_params=params(20), name="first_fold",
-    )(hold_l, hold_l, came_l, came_l, hold_m, hold_m, came_m, came_m, gram)
+        in_specs=[near, far] * 4, out_specs=(near,) * 4, compiler_params=params(20), name="first_fold",
+    )(hold_l, hold_l, came_l, came_l, hold_m, hold_m, came_m, came_m)
 
     def fold(step, send_l, hold_l, send_m, hold_m, came_l, came_m, after):
         part = shape(bf16, half >> (step + 1), blk, rank)
@@ -394,45 +418,46 @@
             compiler_params=params(16), name="fold",
         )(hold_l, came_l, hold_m, came_m, after)
 
-    gram = gram + swap(gram, 1 << order_a[1], n)
     came_l, came_m = swap(send_l, 1 << order_a[1], n), swap(send_m, 1 << order_b[1], n)
-    gram_came = swap(gram, 1 << order_a[2], n)
+    for bit in range(1, bits):
+        gram = gram + swap(gram, 1 << bit, n)
+    gram_other = swap(gram, 1, n)
     av = pl.pallas_call(
         plans_lead_kernel, out_shape=square, in_specs=[vmem, anywhere], out_specs=vmem,
-        scratch_shapes=[pair], compiler_params=params(16), name="plans_lead",
-    )(ss, gram)
+        scratch_shapes=[pair], compiler_params=params(16), cost_estimate=cost(5), name="plans_lead",
+    )(ss, hold_l)
     send_l, hold_l, send_m, hold_m = fold(1, send_l, hold_l, send_m, hold_m, came_l, came_m, av)
-    gram = gram + gram_came
-    for bit in range(3, bits):
-        gram = gram + swap(gram, 1 << bit, n)
-    gram_other = swap(gram, 1, n)
     for step in range(2, bits - 1):
         came_l = swap(send_l, 1 << order_a[step], n)
         came_m = swap(send_m, 1 << order_b[step], n)
-        send_l, hold_l, send_m, hold_m = fold(step, send_l, hold_l, send_m, hold_m, came_l, came_m, gram_other)
+        send_l, hold_l, send_m, hold_m = fold(step, send_l, hold_l, send_m, hold_m, came_l, came_m, av)
     came_l, came_m = swap(send_l, 1 << order_a[-1], n), swap(send_m, 1 << order_b[-1], n)
     lead = pl.pallas_call(
         lambda *refs: lead_kernel(cl / ck, *refs),
         out_shape=shape(f32, 8, rank, rank),
-        in_specs=[vmem] * 3 + [anywhere], out_specs=vmem,
+        in_specs=[vmem] * 3, out_specs=vmem,
         scratch_shapes=[pair, pltpu.VMEM((2 * rank + 16, rank), f32)],
-        compiler_params=params(16), name="lead",
-    )(gram, gram_other, av, hold_l)
+        compiler_params=params(16), cost_estimate=cost(6), name="lead",
+    )(gram, gram_other, av)
     basis_cells, ltu, d = pl.pallas_call(
         lambda *refs: cells_kernel(float(n_cells) ** 0.5, *refs),
         out_shape=(shape(f32, cells_dev, 2 * rank), square, square),
         in_specs=[vmem] * 3, out_specs=(vmem,) * 3, scratch_shapes=[pair],
-        compiler_params=params(16), name="cells",
+        compiler_params=params(16), cost_estimate=cost(8), name="cells",
     )(lead, cell_factor, k)
     lt, sums_send, sums = pl.pallas_call(
         pair_kernel, out_shape=(shape(f32, blk, rank), square, square),
         in_specs=[vmem] * 4 + [anywhere], out_specs=(vmem,) * 3,
         scratch_shapes=[pltpu.VMEM((2 * rank, rank), f32)],
         compiler_params=params(16), name="pair",
-    )(hold_l, came_l, hold_m, came_m, d)
+    )(hold_l, came_l, hold_m, came_m, av)
     sums = sums + swap(sums_send, 1, n)
-    for bit in range(1, bits):
-        sums = sums + swap(sums, 1 << bit, n)
+    dues = [lead] * (bits - 2) + [d]
+    for bit, due in zip(range(1, bits), dues):
+        sums = pl.pallas_call(
+            add_kernel, out_shape=square, in_specs=[vmem] * 2 + [anywhere], out_specs=vmem,
+            compiler_params=params(16), name="add",
+        )(sums, swap(sums, 1 << bit, n), due)
     sums_other = swap(sums, 1, n)
     own = lax.dynamic_slice_in_dim(sched_factor, me * blk, blk, 0)
     scale = rank / (float(n_cells) * float(n_sched)) ** 0.5

time: 114 us -> 101 us (0.89)
  waiting for transfers between devices: 35.9 us -> 24.8 us
  Pallas kernels: 51.9 us -> 49.1 us
    ppermute x18, waiting for transfers between devices: 35.9 us -> 24.8 us  [swap(): return lax.ppermute(x, 'cell', [(i, i ^ mask) for i in range(n)])]
    pallas_call x1, Pallas kernels: 7.85 us -> 6.42 us  [local(): pl.pallas_call(lambda *refs: cells_kernel(float(n_cells) ** 0.5, *refs),...]
    pallas_call x1, Pallas kernels: 24.3 us -> 23.1 us  [local(): pl.pallas_call(lambda *refs: state_kernel(ck, cl, relative, slot_of, *ref...]
    unnamed x10 -> x14, local copies, waits for them, and re-layouts: 2.46 us -> 2.47 us
  transfers between devices with their start and end apart: 18 -> 18, of which waited for: 10 -> 12; matrix products, arithmetic and copies ran while one was open for 1% -> 2% of each run, Pallas kernels for 17% -> 18%
where the time goes in v4:
time: 101 us
  Pallas kernels  49.1 us (49%)
  waiting for transfers between devices  24.8 us (25%)
  starting transfers between devices  22.1 us (22%)
  local copies, waits for them, and re-layouts  3.39 us (3%)
    ppermute x18, waiting for transfers between devices, swap(): return lax.ppermute(x, 'cell', [(i, i ^ mask) for i in range(n)])  24.8 us
    pallas_call x1, Pallas kernels, local(): pl.pallas_call(lambda *refs: state_kernel(ck, cl, relative, slot_of, *ref...  23.1 us
    ppermute x18, starting transfers between devices, swap(): return lax.ppermute(x, 'cell', [(i, i ^ mask) for i in range(n)])  22.1 us
    pallas_call x1, Pallas kernels, local(): pl.pallas_call(lambda *refs: plans_kernel(float(n_sched) ** 0.5, ck, cl,...  6.54 us
    pallas_call x1, Pallas kernels, local(): pl.pallas_call(lambda *refs: cells_kernel(float(n_cells) ** 0.5, *refs),...  6.42 us
    pallas_call x1, Pallas kernels, local(): pl.pallas_call(lambda *refs: lead_kernel(cl / ck, *refs), out_shape=shape...  6.09 us
    pallas_call x1, Pallas kernels, local(): pl.pallas_call(plans_lead_kernel, out_shape=square, in_specs=[vmem, anywh...  5.16 us
    unnamed x14, local copies, waits for them, and re-layouts  2.47 us
  transfers between devices with their start and end apart: 18, of which 12 were waited for; matrix products, arithmetic and copies ran while one was open for 2% of the time, Pallas kernels for 18%

profile of v4, /device:TPU:0, one launch (start us, length us, event | category | flops | bytes accessed | tf_op | source)
XLA Modules:
  0.0 101.0 jit_solution(2567704981141475114)
XLA Ops:
  0.6 23.1 %state.1 = (f32[1024,128]{1,0:T(8,128)}, f32[136,128]{1,0:T(8,128)}, f32[136,128]{1,0:T(8,128)}, bf16[8,512,128]{2,1,0:T(8,128)(2,1)}, bf16[8,512,128]{2,1,0:T(8...) custom-call(bf16[1024,128]{1,0:T(8,128)(2,1)} %refs_1_.1, bf16[16,512,128]{2,1,0:T(8,128)(2,1)} %bitcast.5, ...), custom_call_target="tpu_custom_call" | custom-call | tf_op jit(solution)/shard_map/state/pallas_call | solution.py:368
  24.3 2.4 %collective-permute-done.5.came_l0.came_l1 = bf16[8,512,128]{2,1,0:T(8,128)(2,1)S(1)} collective-permute-done((bf16[8,512,128]{2,1,0:T(8,128)(2,1)}, bf16[8,512,128]{2,1,0:T(8,128)(2,1)S(1)}, u32[]{:S(2)}, u32[]{:S(2)}) %collective-permute-start.5) | collective-permute-done | bytes 1048608 | tf_op jit(solution)/shard_map/ppermute | solution.py:37
  26.7 1.5 %collective-permute-done.6.came_m0.came_m1 = bf16[8,512,128]{2,1,0:T(8,128)(2,1)S(1)} collective-permute-done((bf16[8,512,128]{2,1,0:T(8,128)(2,1)}, bf16[8,512,128]{2,1,0:T(8,128)(2,1)S(1)}, u32[]{:S(2)}, u32[]{:S(2)}) %collective-permute-start.6) | collective-permute-done | bytes 1048608 | tf_op jit(solution)/shard_map/ppermute | solution.py:37
  28.2 1.2 %copy-done = bf16[8,512,128]{2,1,0:T(8,128)(2,1)S(1)} copy-done((bf16[8,512,128]{2,1,0:T(8,128)(2,1)S(1)}, bf16[8,512,128]{2,1,0:T(8,128)(2,1)}, u32[]{:S(2)}) %copy-start) | copy-done | bytes 1048600
  29.5 1.2 %copy-done.1 = bf16[8,512,128]{2,1,0:T(8,128)(2,1)S(1)} copy-done((bf16[8,512,128]{2,1,0:T(8,128)(2,1)S(1)}, bf16[8,512,128]{2,1,0:T(8,128)(2,1)}, u32[]{:S(2)}) %copy-start.1) | copy-done | bytes 1048600
  30.7 0.7 first_fold.1
  31.4 3.0 %collective-permute-start.7 = (bf16[4,512,128]{2,1,0:T(8,128)(2,1)S(1)}, bf16[4,512,128]{2,1,0:T(8,128)(2,1)S(1)}, u32[]{:S(2)}, u32[]{:S(2)}) collective-permute-start(bf16[4,512,128]{2,1,0:T(8,128)(2,1)S(1)} %get-tuple-element.39), channel_id=1, source_target_pairs={{0,2},{1,3},{2,0},{3,1},{4,6},{5,7},{6,4},{7,5},{8,10},{9,11},{10,... | collective-permute-start | bytes 1572872 | tf_op jit(solution)/shard_map/ppermute | solution.py:37
  34.4 1.6 %collective-permute-start.8 = (bf16[4,512,128]{2,1,0:T(8,128)(2,1)S(1)}, bf16[4,512,128]{2,1,0:T(8,128)(2,1)S(1)}, u32[]{:S(2)}, u32[]{:S(2)}) collective-permute-start(bf16[4,512,128]{2,1,0:T(8,128)(2,1)S(1)} %get-tuple-element.41), channel_id=1, source_target_pairs={{0,4},{1,5},{2,6},{3,7},{4,0},{5,1},{6,2},{7,3},{8,12},{9,13},{10,... | collective-permute-start | bytes 1572872 | tf_op jit(solution)/shard_map/ppermute | solution.py:37
  35.9 0.7 fusion.ss_ref
  36.7 5.2 %plans_lead.1.refs_2_.after = f32[128,128]{1,0:T(8,128)S(1)} custom-call(f32[128,128]{1,0:T(8,128)S(1)} %fusion.ss_ref, bf16[4,512,128]{2,1,0:T(8,128)(2,1)S(1)} %get-tuple-element.36.after.keep_l), custom_call_target="tpu_custom_call" | custom-call | bytes 18000000 | tf_op jit(solution)/shard_map/plans_lead/pallas_call | solution.py:425
  41.9 4.7 %collective-permute-done.7.came_l = bf16[4,512,128]{2,1,0:T(8,128)(2,1)S(1)} collective-permute-done((bf16[4,512,128]{2,1,0:T(8,128)(2,1)S(1)}, bf16[4,512,128]{2,1,0:T(8,128)(2,1)S(1)}, u32[]{:S(2)}, u32[]{:S(2)}) %collective-permute-start.7) | collective-permute-done | bytes 524320 | tf_op jit(solution)/shard_map/ppermute | solution.py:37
  46.6 1.5 %collective-permute-done.8.came_m = bf16[4,512,128]{2,1,0:T(8,128)(2,1)S(1)} collective-permute-done((bf16[4,512,128]{2,1,0:T(8,128)(2,1)S(1)}, bf16[4,512,128]{2,1,0:T(8,128)(2,1)S(1)}, u32[]{:S(2)}, u32[]{:S(2)}) %collective-permute-start.8) | collective-permute-done | bytes 524320 | tf_op jit(solution)/shard_map/ppermute | solution.py:37
  48.7 1.7 %collective-permute-start.9 = (bf16[2,512,128]{2,1,0:T(8,128)(2,1)S(1)}, bf16[2,512,128]{2,1,0:T(8,128)(2,1)S(1)}, u32[]{:S(2)}, u32[]{:S(2)}) collective-permute-start(bf16[2,512,128]{2,1,0:T(8,128)(2,1)S(1)} %get-tuple-element.43), channel_id=1, source_target_pairs={{0,4},{1,5},{2,6},{3,7},{4,0},{5,1},{6,2},{7,3},{8,12},{9,13},{10,... | collective-permute-start | bytes 786440 | tf_op jit(solution)/shard_map/ppermute | solution.py:37
  50.4 1.3 %collective-permute-done = f32[136,128]{1,0:T(8,128)S(1)} collective-permute-done((f32[136,128]{1,0:T(8,128)S(1)}, f32[136,128]{1,0:T(8,128)S(1)}, u32[]{:S(2)}, u32[]{:S(2)}) %collective-permute-start) | collective-permute-done | bytes 69664 | tf_op jit(solution)/shard_map/ppermute | solution.py:37
  51.7 1.6 %collective-permute-start.1 = (f32[136,128]{1,0:T(8,128)S(1)}, f32[136,128]{1,0:T(8,128)S(1)}, u32[]{:S(2)}, u32[]{:S(2)}) collective-permute-start(f32[136,128]{1,0:T(8,128)S(1)} %add.21), channel_id=1, source_target_pairs={{0,2},{1,3},{2,0},{3,1},{4,6},{5,7},{6,4},{7,5},{8,10},{9,11},{10,... | collective-permute-start | bytes 208904 | tf_op jit(solution)/shard_map/ppermute | solution.py:37
  53.3 3.0 %collective-permute-done.10.came_m = bf16[2,512,128]{2,1,0:T(8,128)(2,1)S(1)} collective-permute-done((bf16[2,512,128]{2,1,0:T(8,128)(2,1)S(1)}, bf16[2,512,128]{2,1,0:T(8,128)(2,1)S(1)}, u32[]{:S(2)}, u32[]{:S(2)}) %collective-permute-start.10) | collective-permute-done | bytes 262176 | tf_op jit(solution)/shard_map/ppermute | solution.py:37
  56.4 2.6 %collective-permute-start.11 = (bf16[1,512,128]{2,1,0:T(8,128)(2,1)S(1)}, bf16[1,512,128]{2,1,0:T(8,128)(2,1)S(1)}, u32[]{:S(2)}, u32[]{:S(2)}) collective-permute-start(bf16[1,512,128]{2,1,0:T(8,128)(2,1)S(1)} %get-tuple-element.47), channel_id=1, source_target_pairs={{0,8},{1,9},{2,10},{3,11},{4,12},{5,13},{6,14},{7,15},{8,0},{9,1},... | collective-permute-start | bytes 393224 | tf_op jit(solution)/shard_map/ppermute | solution.py:37
  59.4 1.6 %collective-permute-start.2 = (f32[136,128]{1,0:T(8,128)S(1)}, f32[136,128]{1,0:T(8,128)S(1)}, u32[]{:S(2)}, u32[]{:S(2)}) collective-permute-start(f32[136,128]{1,0:T(8,128)S(1)} %add.22), channel_id=1, source_target_pairs={{0,4},{1,5},{2,6},{3,7},{4,0},{5,1},{6,2},{7,3},{8,12},{9,13},{10,... | collective-permute-start | bytes 208904 | tf_op jit(solution)/shard_map/ppermute | solution.py:37
  61.1 3.2 %collective-permute-done.2 = f32[136,128]{1,0:T(8,128)S(1)} collective-permute-done((f32[136,128]{1,0:T(8,128)S(1)}, f32[136,128]{1,0:T(8,128)S(1)}, u32[]{:S(2)}, u32[]{:S(2)}) %collective-permute-start.2) | collective-permute-done | bytes 69664 | tf_op jit(solution)/shard_map/ppermute | solution.py:37
  64.3 3.8 %collective-permute-start.3 = (f32[136,128]{1,0:T(8,128)S(1)}, f32[136,128]{1,0:T(8,128)S(1)}, u32[]{:S(2)}, u32[]{:S(2)}) collective-permute-start(f32[136,128]{1,0:T(8,128)S(1)} %add.23), channel_id=1, source_target_pairs={{0,8},{1,9},{2,10},{3,11},{4,12},{5,13},{6,14},{7,15},{8,0},{9,1},... | collective-permute-start | bytes 208904 | tf_op jit(solution)/shard_map/ppermute | solution.py:37
  68.1 0.6 collective-permute-done.11.came_l
  68.7 2.5 %collective-permute-done.12.came_m = bf16[1,512,128]{2,1,0:T(8,128)(2,1)S(1)} collective-permute-done((bf16[1,512,128]{2,1,0:T(8,128)(2,1)S(1)}, bf16[1,512,128]{2,1,0:T(8,128)(2,1)S(1)}, u32[]{:S(2)}, u32[]{:S(2)}) %collective-permute-start.12) | collective-permute-done | bytes 131104 | tf_op jit(solution)/shard_map/ppermute | solution.py:37
  71.2 0.7 pair.1
  72.0 0.5 collective-permute-start.4
  72.5 0.7 collective-permute-done.13
  73.6 6.1 %lead.1.refs_0_.after.refs_2_ = f32[8,128,128]{2,1,0:T(8,128)S(1)} custom-call(f32[136,128]{1,0:T(8,128)S(1)} %add.24.refs_0_, f32[136,128]{1,0:T(8,128)S(1)} %collective-permute-done.4.refs_1_, f32[128,128]{1,0:T(8,128)S(1)} %plans_lead.1.refs_2_.after), custom_call_target="tpu_custom_call" | custom-call | bytes 21600000 | tf_op jit(solution)/shard_map/lead/pallas_call | solution.py:435
  79.7 1.1 %collective-permute-start.15 = (f32[128,128]{1,0:T(8,128)S(1)}, f32[128,128]{1,0:T(8,128)S(1)}, u32[]{:S(2)}, u32[]{:S(2)}) collective-permute-start(f32[128,128]{1,0:T(8,128)S(1)} %add.27.a_ref), channel_id=1, source_target_pairs={{0,4},{1,5},{2,6},{3,7},{4,0},{5,1},{6,2},{7,3},{8,12},{9,13},{10,... | collective-permute-start | bytes 196616 | tf_op jit(solution)/shard_map/ppermute | solution.py:37
  80.8 3.2 %collective-permute-done.15.b_ref = f32[128,128]{1,0:T(8,128)S(1)} collective-permute-done((f32[128,128]{1,0:T(8,128)S(1)}, f32[128,128]{1,0:T(8,128)S(1)}, u32[]{:S(2)}, u32[]{:S(2)}) %collective-permute-start.15) | collective-permute-done | bytes 65568 | tf_op jit(solution)/shard_map/ppermute | solution.py:37
  84.0 2.6 %collective-permute-start.16 = (f32[128,128]{1,0:T(8,128)S(1)}, f32[128,128]{1,0:T(8,128)S(1)}, u32[]{:S(2)}, u32[]{:S(2)}) collective-permute-start(f32[128,128]{1,0:T(8,128)S(1)} %add.28.a_ref), channel_id=1, source_target_pairs={{0,8},{1,9},{2,10},{3,11},{4,12},{5,13},{6,14},{7,15},{8,0},{9,1},... | collective-permute-start | bytes 196616 | tf_op jit(solution)/shard_map/ppermute | solution.py:37
  86.7 6.4 %cells.1 = (f32[1024,256]{1,0:T(8,128)}, f32[128,128]{1,0:T(8,128)S(1)}, f32[128,128]{1,0:T(8,128)S(1)}) custom-call(f32[8,128,128]{2,1,0:T(8,128)S(1)} %lead.1.refs_0_.after.refs_2_, bf16[1024,128]{1,0:T(8,128)(2,1)S(1)} %copy-done.2, f32[1024,128]{1,0:T(8,128)S(1)} %copy-done.3), custom_call_target="tpu_custom_call" | custom-call | bytes 28800000 | tf_op jit(solution)/shard_map/cells/pallas_call | solution.py:442
  93.2 0.9 constant_dynamic-slice_fusion.refs_5_
  94.4 6.5 %plans.1 = (f32[512,256]{1,0:T(8,128)}, f32[256,256]{1,0:T(8,128)}) custom-call(f32[128,128]{1,0:T(8,128)S(1)} %add.29.refs_0_, f32[128,128]{1,0:T(8,128)S(1)} %collective-permute-done.17.refs_1_, f32[8,128,128]{2,1,0:T(8,128)S(1)} %lead.1.refs_0_.after.refs_2_, f32[128,128]{1,0:T(8,128)S(1)} %get-tuple-element.53.refs_3_, ...), custom_call_target="tpu_custom_call" | custom-call | tf_op jit(solution)/shard_map/plans/pallas_call | solution.py:464
  (37 shorter events, 2.6 us)
Async XLA Ops:
  23.7 3.0 %collective-permute-start.5 = (bf16[8,512,128]{2,1,0:T(8,128)(2,1)}, bf16[8,512,128]{2,1,0:T(8,128)(2,1)S(1)}, u32[]{:S(2)}, u32[]{:S(2)}) collective-permute-start(bf16[8,512,128]{2,1,0:T(8,128)(2,1)} %get-tuple-element.33), channel_id=1, source_target_pairs={{0,1},{1,0},{2,3},{3,2},{4,5},{5,4},{6,7},{7,6},{8,9},{9,8},{10,11... | collective-permute-start | bytes 3145736 | tf_op jit(solution)/shard_map/ppermute | solution.py:37
  24.2 4.0 %collective-permute-start.6 = (bf16[8,512,128]{2,1,0:T(8,128)(2,1)}, bf16[8,512,128]{2,1,0:T(8,128)(2,1)S(1)}, u32[]{:S(2)}, u32[]{:S(2)}) collective-permute-start(bf16[8,512,128]{2,1,0:T(8,128)(2,1)} %get-tuple-element.35), channel_id=1, source_target_pairs={{0,1},{1,0},{2,3},{3,2},{4,5},{5,4},{6,7},{7,6},{8,9},{9,8},{10,11... | collective-permute-start | bytes 3145736 | tf_op jit(solution)/shard_map/ppermute | solution.py:37
  28.2 1.2 %copy-start = (bf16[8,512,128]{2,1,0:T(8,128)(2,1)S(1)}, bf16[8,512,128]{2,1,0:T(8,128)(2,1)}, u32[]{:S(2)}) copy-start(bf16[8,512,128]{2,1,0:T(8,128)(2,1)} %get-tuple-element.32.keep_l0.keep_l1) | copy-start | bytes 3145732
  29.5 1.2 %copy-start.1 = (bf16[8,512,128]{2,1,0:T(8,128)(2,1)S(1)}, bf16[8,512,128]{2,1,0:T(8,128)(2,1)}, u32[]{:S(2)}) copy-start(bf16[8,512,128]{2,1,0:T(8,128)(2,1)} %get-tuple-element.34.keep_m0.keep_m1) | copy-start | bytes 3145732
  30.7 5.3 %copy-start.4 = (bf16[8192,128]{1,0:T(8,128)(2,1)S(1)}, bf16[8192,128]{1,0:T(8,128)(2,1)}, u32[]{:S(2)}) copy-start(bf16[8192,128]{1,0:T(8,128)(2,1)} %param.7) | copy-start | bytes 6291460
  31.4 15.2 %collective-permute-start.7 = (bf16[4,512,128]{2,1,0:T(8,128)(2,1)S(1)}, bf16[4,512,128]{2,1,0:T(8,128)(2,1)S(1)}, u32[]{:S(2)}, u32[]{:S(2)}) collective-permute-start(bf16[4,512,128]{2,1,0:T(8,128)(2,1)S(1)} %get-tuple-element.39), channel_id=1, source_target_pairs={{0,2},{1,3},{2,0},{3,1},{4,6},{5,7},{6,4},{7,5},{8,10},{9,11},{10,... | collective-permute-start | bytes 1572872 | tf_op jit(solution)/shard_map/ppermute | solution.py:37
  34.4 13.7 %collective-permute-start.8 = (bf16[4,512,128]{2,1,0:T(8,128)(2,1)S(1)}, bf16[4,512,128]{2,1,0:T(8,128)(2,1)S(1)}, u32[]{:S(2)}, u32[]{:S(2)}) collective-permute-start(bf16[4,512,128]{2,1,0:T(8,128)(2,1)S(1)} %get-tuple-element.41), channel_id=1, source_target_pairs={{0,4},{1,5},{2,6},{3,7},{4,0},{5,1},{6,2},{7,3},{8,12},{9,13},{10,... | collective-permute-start | bytes 1572872 | tf_op jit(solution)/shard_map/ppermute | solution.py:37
  36.7 13.7 %copy-start.6 = (f32[136,128]{1,0:T(8,128)S(1)}, f32[136,128]{1,0:T(8,128)}, u32[]{:S(2)}) copy-start(f32[136,128]{1,0:T(8,128)} %get-tuple-element.31) | copy-start | bytes 208900
  36.7 15.0 %copy-start.5 = (f32[136,128]{1,0:T(8,128)S(1)}, f32[136,128]{1,0:T(8,128)}, u32[]{:S(2)}) copy-start(f32[136,128]{1,0:T(8,128)} %get-tuple-element.30) | copy-start | bytes 208900
  48.3 8.0 %collective-permute-start.10 = (bf16[2,512,128]{2,1,0:T(8,128)(2,1)S(1)}, bf16[2,512,128]{2,1,0:T(8,128)(2,1)S(1)}, u32[]{:S(2)}, u32[]{:S(2)}) collective-permute-start(bf16[2,512,128]{2,1,0:T(8,128)(2,1)S(1)} %get-tuple-element.45), channel_id=1, source_target_pairs={{0,2},{1,3},{2,0},{3,1},{4,6},{5,7},{6,4},{7,5},{8,10},{9,11},{10,... | collective-permute-start | bytes 786440 | tf_op jit(solution)/shard_map/ppermute | solution.py:37
  48.7 7.6 %collective-permute-start.9 = (bf16[2,512,128]{2,1,0:T(8,128)(2,1)S(1)}, bf16[2,512,128]{2,1,0:T(8,128)(2,1)S(1)}, u32[]{:S(2)}, u32[]{:S(2)}) collective-permute-start(bf16[2,512,128]{2,1,0:T(8,128)(2,1)S(1)} %get-tuple-element.43), channel_id=1, source_target_pairs={{0,4},{1,5},{2,6},{3,7},{4,0},{5,1},{6,2},{7,3},{8,12},{9,13},{10,... | collective-permute-start | bytes 786440 | tf_op jit(solution)/shard_map/ppermute | solution.py:37
  50.4 1.3 %collective-permute-start = (f32[136,128]{1,0:T(8,128)S(1)}, f32[136,128]{1,0:T(8,128)S(1)}, u32[]{:S(2)}, u32[]{:S(2)}) collective-permute-start(f32[136,128]{1,0:T(8,128)S(1)} %copy-done.6), channel_id=1, source_target_pairs={{0,1},{1,0},{2,3},{3,2},{4,5},{5,4},{6,7},{7,6},{8,9},{9,8},{10,11... | collective-permute-start | bytes 208904 | tf_op jit(solution)/shard_map/ppermute | solution.py:37
  51.7 7.7 %collective-permute-start.1 = (f32[136,128]{1,0:T(8,128)S(1)}, f32[136,128]{1,0:T(8,128)S(1)}, u32[]{:S(2)}, u32[]{:S(2)}) collective-permute-start(f32[136,128]{1,0:T(8,128)S(1)} %add.21), channel_id=1, source_target_pairs={{0,2},{1,3},{2,0},{3,1},{4,6},{5,7},{6,4},{7,5},{8,10},{9,11},{10,... | collective-permute-start | bytes 208904 | tf_op jit(solution)/shard_map/ppermute | solution.py:37
  56.3 30.4 %copy-start.2 = (bf16[1024,128]{1,0:T(8,128)(2,1)S(1)}, bf16[1024,128]{1,0:T(8,128)(2,1)}, u32[]{:S(2)}) copy-start(bf16[1024,128]{1,0:T(8,128)(2,1)} %refs_1_.1) | copy-start | bytes 786436
  56.3 30.4 %copy-start.3 = (f32[1024,128]{1,0:T(8,128)S(1)}, f32[1024,128]{1,0:T(8,128)}, u32[]{:S(2)}) copy-start(f32[1024,128]{1,0:T(8,128)} %get-tuple-element.37.refs_2_) | copy-start | bytes 1572868
  56.4 12.3 %collective-permute-start.11 = (bf16[1,512,128]{2,1,0:T(8,128)(2,1)S(1)}, bf16[1,512,128]{2,1,0:T(8,128)(2,1)S(1)}, u32[]{:S(2)}, u32[]{:S(2)}) collective-permute-start(bf16[1,512,128]{2,1,0:T(8,128)(2,1)S(1)} %get-tuple-element.47), channel_id=1, source_target_pairs={{0,8},{1,9},{2,10},{3,11},{4,12},{5,13},{6,14},{7,15},{8,0},{9,1},... | collective-permute-start | bytes 393224 | tf_op jit(solution)/shard_map/ppermute | solution.py:37
  59.1 12.1 %collective-permute-start.12 = (bf16[1,512,128]{2,1,0:T(8,128)(2,1)S(1)}, bf16[1,512,128]{2,1,0:T(8,128)(2,1)S(1)}, u32[]{:S(2)}, u32[]{:S(2)}) collective-permute-start(bf16[1,512,128]{2,1,0:T(8,128)(2,1)S(1)} %get-tuple-element.49), channel_id=1, source_target_pairs={{0,8},{1,9},{2,10},{3,11},{4,12},{5,13},{6,14},{7,15},{8,0},{9,1},... | collective-permute-start | bytes 393224 | tf_op jit(solution)/shard_map/ppermute | solution.py:37
  59.4 4.8 %collective-permute-start.2 = (f32[136,128]{1,0:T(8,128)S(1)}, f32[136,128]{1,0:T(8,128)S(1)}, u32[]{:S(2)}, u32[]{:S(2)}) collective-permute-start(f32[136,128]{1,0:T(8,128)S(1)} %add.22), channel_id=1, source_target_pairs={{0,4},{1,5},{2,6},{3,7},{4,0},{5,1},{6,2},{7,3},{8,12},{9,13},{10,... | collective-permute-start | bytes 208904 | tf_op jit(solution)/shard_map/ppermute | solution.py:37
  64.3 7.7 %collective-permute-start.3 = (f32[136,128]{1,0:T(8,128)S(1)}, f32[136,128]{1,0:T(8,128)S(1)}, u32[]{:S(2)}, u32[]{:S(2)}) collective-permute-start(f32[136,128]{1,0:T(8,128)S(1)} %add.23), channel_id=1, source_target_pairs={{0,8},{1,9},{2,10},{3,11},{4,12},{5,13},{6,14},{7,15},{8,0},{9,1},... | collective-permute-start | bytes 208904 | tf_op jit(solution)/shard_map/ppermute | solution.py:37
  71.9 1.3 %collective-permute-start.13 = (f32[128,128]{1,0:T(8,128)S(1)}, f32[128,128]{1,0:T(8,128)S(1)}, u32[]{:S(2)}, u32[]{:S(2)}) collective-permute-start(f32[128,128]{1,0:T(8,128)S(1)} %get-tuple-element.51), channel_id=1, source_target_pairs={{0,1},{1,0},{2,3},{3,2},{4,5},{5,4},{6,7},{7,6},{8,9},{9,8},{10,11... | collective-permute-start | bytes 196616 | tf_op jit(solution)/shard_map/ppermute | solution.py:37
  72.0 1.6 %collective-permute-start.4 = (f32[136,128]{1,0:T(8,128)S(1)}, f32[136,128]{1,0:T(8,128)S(1)}, u32[]{:S(2)}, u32[]{:S(2)}) collective-permute-start(f32[136,128]{1,0:T(8,128)S(1)} %add.24.refs_0_), channel_id=1, source_target_pairs={{0,1},{1,0},{2,3},{3,2},{4,5},{5,4},{6,7},{7,6},{8,9},{9,8},{10,11... | collective-permute-start | bytes 208904 | tf_op jit(solution)/shard_map/ppermute | solution.py:37
  73.2 6.5 %collective-permute-start.14 = (f32[128,128]{1,0:T(8,128)S(1)}, f32[128,128]{1,0:T(8,128)S(1)}, u32[]{:S(2)}, u32[]{:S(2)}) collective-permute-start(f32[128,128]{1,0:T(8,128)S(1)} %add.25.a_ref), channel_id=1, source_target_pairs={{0,2},{1,3},{2,0},{3,1},{4,6},{5,7},{6,4},{7,5},{8,10},{9,11},{10,... | collective-permute-start | bytes 196616 | tf_op jit(solution)/shard_map/ppermute | solution.py:37
  79.7 4.3 %collective-permute-start.15 = (f32[128,128]{1,0:T(8,128)S(1)}, f32[128,128]{1,0:T(8,128)S(1)}, u32[]{:S(2)}, u32[]{:S(2)}) collective-permute-start(f32[128,128]{1,0:T(8,128)S(1)} %add.27.a_ref), channel_id=1, source_target_pairs={{0,4},{1,5},{2,6},{3,7},{4,0},{5,1},{6,2},{7,3},{8,12},{9,13},{10,... | collective-permute-start | bytes 196616 | tf_op jit(solution)/shard_map/ppermute | solution.py:37
  84.0 9.1 %collective-permute-start.16 = (f32[128,128]{1,0:T(8,128)S(1)}, f32[128,128]{1,0:T(8,128)S(1)}, u32[]{:S(2)}, u32[]{:S(2)}) collective-permute-start(f32[128,128]{1,0:T(8,128)S(1)} %add.28.a_ref), channel_id=1, source_target_pairs={{0,8},{1,9},{2,10},{3,11},{4,12},{5,13},{6,14},{7,15},{8,0},{9,1},... | collective-permute-start | bytes 196616 | tf_op jit(solution)/shard_map/ppermute | solution.py:37
  93.1 1.3 %collective-permute-start.17 = (f32[128,128]{1,0:T(8,128)S(1)}, f32[128,128]{1,0:T(8,128)S(1)}, u32[]{:S(2)}, u32[]{:S(2)}) collective-permute-start(f32[128,128]{1,0:T(8,128)S(1)} %add.29.refs_0_), channel_id=1, source_target_pairs={{0,1},{1,0},{2,3},{3,2},{4,5},{5,4},{6,7},{7,6},{8,9},{9,8},{10,11... | collective-permute-start | bytes 196616 | tf_op jit(solution)/shard_map/ppermute | solution.py:37

commit v5 on v4

--- a/solution.py
+++ b/solution.py
@@ -93,7 +93,7 @@
         ps_ref[...] += dot(onehot(prof_ref[b], profiles, blk), s, 1, 0)
         return carry
 
-    lax.fori_loop(0, n, first, 0, unroll=2)
+    lax.fori_loop(0, n, first, 0, unroll=4)
 
     table = table_ref[...]
     wt = onehot(well_ref[...], wells, cells)
@@ -142,7 +142,7 @@
                 copy.start()
             return carry
 
-        lax.fori_loop(0, half, body, 0, unroll=2)
+        lax.fori_loop(0, half, body, 0, unroll=4)
 
     def finish(first_slot, dst_l, dst_m):
         def body(at, carry):

time: 101 us -> 99.8 us (0.988)
  Pallas kernels: 49.1 us -> 47.7 us
    pallas_call x1, Pallas kernels: 23.1 us -> 21.7 us  [local(): pl.pallas_call(lambda *refs: state_kernel(ck, cl, relative, slot_of, *ref...]
  transfers between devices with their start and end apart: 18 -> 18, of which waited for: 12 -> 12; matrix products, arithmetic and copies ran while one was open for 2% -> 2% of each run, Pallas kernels for 18% -> 19%
where the time goes in v5:
time: 99.8 us; the launch traced here: 99.6 us
  Pallas kernels  47.7 us (48%)
  waiting for transfers between devices  24.9 us (25%)
  starting transfers between devices  22.1 us (22%)
  local copies, waits for them, and re-layouts  3.39 us (3%)
    ppermute x18, waiting for transfers between devices, swap(): return lax.ppermute(x, 'cell', [(i, i ^ mask) for i in range(n)])  24.9 us
    ppermute x18, starting transfers between devices, swap(): return lax.ppermute(x, 'cell', [(i, i ^ mask) for i in range(n)])  22.1 us
    pallas_call x1, Pallas kernels, local(): pl.pallas_call(lambda *refs: state_kernel(ck, cl, relative, slot_of, *ref...  21.7 us
    pallas_call x1, Pallas kernels, local(): pl.pallas_call(lambda *refs: plans_kernel(float(n_sched) ** 0.5, ck, cl,...  6.54 us
    pallas_call x1, Pallas kernels, local(): pl.pallas_call(lambda *refs: cells_kernel(float(n_cells) ** 0.5, *refs),...  6.42 us
    pallas_call x1, Pallas kernels, local(): pl.pallas_call(lambda *refs: lead_kernel(cl / ck, *refs), out_shape=shape...  6.1 us
    pallas_call x1, Pallas kernels, local(): pl.pallas_call(plans_lead_kernel, out_shape=square, in_specs=[vmem, anywh...  5.16 us
    unnamed x14, local copies, waits for them, and re-layouts  2.47 us
  transfers between devices with their start and end apart: 18, of which 12 were waited for; matrix products, arithmetic and copies ran while one was open for 2% of the time, Pallas kernels for 19%

profile of v5, /device:TPU:0, one launch (start us, length us, event | category | flops | bytes accessed | tf_op | source)
XLA Modules:
  0.0 99.6 jit_solution(11634152405023134217)
XLA Ops:
  0.6 21.7 %state.1 = (f32[1024,128]{1,0:T(8,128)}, f32[136,128]{1,0:T(8,128)}, f32[136,128]{1,0:T(8,128)}, bf16[8,512,128]{2,1,0:T(8,128)(2,1)}, bf16[8,512,128]{2,1,0:T(8...) custom-call(bf16[1024,128]{1,0:T(8,128)(2,1)} %refs_1_.1, bf16[16,512,128]{2,1,0:T(8,128)(2,1)} %bitcast.5, ...), custom_call_target="tpu_custom_call" | custom-call | tf_op jit(solution)/shard_map/state/pallas_call | solution.py:368
  22.9 2.4 %collective-permute-done.5.came_l0.came_l1 = bf16[8,512,128]{2,1,0:T(8,128)(2,1)S(1)} collective-permute-done((bf16[8,512,128]{2,1,0:T(8,128)(2,1)}, bf16[8,512,128]{2,1,0:T(8,128)(2,1)S(1)}, u32[]{:S(2)}, u32[]{:S(2)}) %collective-permute-start.5) | collective-permute-done | bytes 1048608 | tf_op jit(solution)/shard_map/ppermute | solution.py:37
  25.3 1.5 %collective-permute-done.6.came_m0.came_m1 = bf16[8,512,128]{2,1,0:T(8,128)(2,1)S(1)} collective-permute-done((bf16[8,512,128]{2,1,0:T(8,128)(2,1)}, bf16[8,512,128]{2,1,0:T(8,128)(2,1)S(1)}, u32[]{:S(2)}, u32[]{:S(2)}) %collective-permute-start.6) | collective-permute-done | bytes 1048608 | tf_op jit(solution)/shard_map/ppermute | solution.py:37
  26.8 1.2 %copy-done = bf16[8,512,128]{2,1,0:T(8,128)(2,1)S(1)} copy-done((bf16[8,512,128]{2,1,0:T(8,128)(2,1)S(1)}, bf16[8,512,128]{2,1,0:T(8,128)(2,1)}, u32[]{:S(2)}) %copy-start) | copy-done | bytes 1048600
  28.1 1.2 %copy-done.1 = bf16[8,512,128]{2,1,0:T(8,128)(2,1)S(1)} copy-done((bf16[8,512,128]{2,1,0:T(8,128)(2,1)S(1)}, bf16[8,512,128]{2,1,0:T(8,128)(2,1)}, u32[]{:S(2)}) %copy-start.1) | copy-done | bytes 1048600
  29.3 0.7 first_fold.1
  30.0 3.0 %collective-permute-start.7 = (bf16[4,512,128]{2,1,0:T(8,128)(2,1)S(1)}, bf16[4,512,128]{2,1,0:T(8,128)(2,1)S(1)}, u32[]{:S(2)}, u32[]{:S(2)}) collective-permute-start(bf16[4,512,128]{2,1,0:T(8,128)(2,1)S(1)} %get-tuple-element.39), channel_id=1, source_target_pairs={{0,2},{1,3},{2,0},{3,1},{4,6},{5,7},{6,4},{7,5},{8,10},{9,11},{10,... | collective-permute-start | bytes 1572872 | tf_op jit(solution)/shard_map/ppermute | solution.py:37
  33.0 1.6 %collective-permute-start.8 = (bf16[4,512,128]{2,1,0:T(8,128)(2,1)S(1)}, bf16[4,512,128]{2,1,0:T(8,128)(2,1)S(1)}, u32[]{:S(2)}, u32[]{:S(2)}) collective-permute-start(bf16[4,512,128]{2,1,0:T(8,128)(2,1)S(1)} %get-tuple-element.41), channel_id=1, source_target_pairs={{0,4},{1,5},{2,6},{3,7},{4,0},{5,1},{6,2},{7,3},{8,12},{9,13},{10,... | collective-permute-start | bytes 1572872 | tf_op jit(solution)/shard_map/ppermute | solution.py:37
  34.5 0.7 fusion.ss_ref
  35.3 5.2 %plans_lead.1.refs_2_.after = f32[128,128]{1,0:T(8,128)S(1)} custom-call(f32[128,128]{1,0:T(8,128)S(1)} %fusion.ss_ref, bf16[4,512,128]{2,1,0:T(8,128)(2,1)S(1)} %get-tuple-element.36.after.keep_l), custom_call_target="tpu_custom_call" | custom-call | bytes 18000000 | tf_op jit(solution)/shard_map/plans_lead/pallas_call | solution.py:425
  40.5 4.7 %collective-permute-done.7.came_l = bf16[4,512,128]{2,1,0:T(8,128)(2,1)S(1)} collective-permute-done((bf16[4,512,128]{2,1,0:T(8,128)(2,1)S(1)}, bf16[4,512,128]{2,1,0:T(8,128)(2,1)S(1)}, u32[]{:S(2)}, u32[]{:S(2)}) %collective-permute-start.7) | collective-permute-done | bytes 524320 | tf_op jit(solution)/shard_map/ppermute | solution.py:37
  45.2 1.5 %collective-permute-done.8.came_m = bf16[4,512,128]{2,1,0:T(8,128)(2,1)S(1)} collective-permute-done((bf16[4,512,128]{2,1,0:T(8,128)(2,1)S(1)}, bf16[4,512,128]{2,1,0:T(8,128)(2,1)S(1)}, u32[]{:S(2)}, u32[]{:S(2)}) %collective-permute-start.8) | collective-permute-done | bytes 524320 | tf_op jit(solution)/shard_map/ppermute | solution.py:37
  47.3 1.7 %collective-permute-start.9 = (bf16[2,512,128]{2,1,0:T(8,128)(2,1)S(1)}, bf16[2,512,128]{2,1,0:T(8,128)(2,1)S(1)}, u32[]{:S(2)}, u32[]{:S(2)}) collective-permute-start(bf16[2,512,128]{2,1,0:T(8,128)(2,1)S(1)} %get-tuple-element.43), channel_id=1, source_target_pairs={{0,4},{1,5},{2,6},{3,7},{4,0},{5,1},{6,2},{7,3},{8,12},{9,13},{10,... | collective-permute-start | bytes 786440 | tf_op jit(solution)/shard_map/ppermute | solution.py:37
  49.0 1.3 %collective-permute-done = f32[136,128]{1,0:T(8,128)S(1)} collective-permute-done((f32[136,128]{1,0:T(8,128)S(1)}, f32[136,128]{1,0:T(8,128)S(1)}, u32[]{:S(2)}, u32[]{:S(2)}) %collective-permute-start) | collective-permute-done | bytes 69664 | tf_op jit(solution)/shard_map/ppermute | solution.py:37
  50.3 1.6 %collective-permute-start.1 = (f32[136,128]{1,0:T(8,128)S(1)}, f32[136,128]{1,0:T(8,128)S(1)}, u32[]{:S(2)}, u32[]{:S(2)}) collective-permute-start(f32[136,128]{1,0:T(8,128)S(1)} %add.21), channel_id=1, source_target_pairs={{0,2},{1,3},{2,0},{3,1},{4,6},{5,7},{6,4},{7,5},{8,10},{9,11},{10,... | collective-permute-start | bytes 208904 | tf_op jit(solution)/shard_map/ppermute | solution.py:37
  51.9 3.0 %collective-permute-done.10.came_m = bf16[2,512,128]{2,1,0:T(8,128)(2,1)S(1)} collective-permute-done((bf16[2,512,128]{2,1,0:T(8,128)(2,1)S(1)}, bf16[2,512,128]{2,1,0:T(8,128)(2,1)S(1)}, u32[]{:S(2)}, u32[]{:S(2)}) %collective-permute-start.10) | collective-permute-done | bytes 262176 | tf_op jit(solution)/shard_map/ppermute | solution.py:37
  55.0 2.6 %collective-permute-start.11 = (bf16[1,512,128]{2,1,0:T(8,128)(2,1)S(1)}, bf16[1,512,128]{2,1,0:T(8,128)(2,1)S(1)}, u32[]{:S(2)}, u32[]{:S(2)}) collective-permute-start(bf16[1,512,128]{2,1,0:T(8,128)(2,1)S(1)} %get-tuple-element.47), channel_id=1, source_target_pairs={{0,8},{1,9},{2,10},{3,11},{4,12},{5,13},{6,14},{7,15},{8,0},{9,1},... | collective-permute-start | bytes 393224 | tf_op jit(solution)/shard_map/ppermute | solution.py:37
  58.0 1.6 %collective-permute-start.2 = (f32[136,128]{1,0:T(8,128)S(1)}, f32[136,128]{1,0:T(8,128)S(1)}, u32[]{:S(2)}, u32[]{:S(2)}) collective-permute-start(f32[136,128]{1,0:T(8,128)S(1)} %add.22), channel_id=1, source_target_pairs={{0,4},{1,5},{2,6},{3,7},{4,0},{5,1},{6,2},{7,3},{8,12},{9,13},{10,... | collective-permute-start | bytes 208904 | tf_op jit(solution)/shard_map/ppermute | solution.py:37
  59.7 3.2 %collective-permute-done.2 = f32[136,128]{1,0:T(8,128)S(1)} collective-permute-done((f32[136,128]{1,0:T(8,128)S(1)}, f32[136,128]{1,0:T(8,128)S(1)}, u32[]{:S(2)}, u32[]{:S(2)}) %collective-permute-start.2) | collective-permute-done | bytes 69664 | tf_op jit(solution)/shard_map/ppermute | solution.py:37
  62.8 3.8 %collective-permute-start.3 = (f32[136,128]{1,0:T(8,128)S(1)}, f32[136,128]{1,0:T(8,128)S(1)}, u32[]{:S(2)}, u32[]{:S(2)}) collective-permute-start(f32[136,128]{1,0:T(8,128)S(1)} %add.23), channel_id=1, source_target_pairs={{0,8},{1,9},{2,10},{3,11},{4,12},{5,13},{6,14},{7,15},{8,0},{9,1},... | collective-permute-start | bytes 208904 | tf_op jit(solution)/shard_map/ppermute | solution.py:37
  66.7 0.6 collective-permute-done.11.came_l
  67.3 2.5 %collective-permute-done.12.came_m = bf16[1,512,128]{2,1,0:T(8,128)(2,1)S(1)} collective-permute-done((bf16[1,512,128]{2,1,0:T(8,128)(2,1)S(1)}, bf16[1,512,128]{2,1,0:T(8,128)(2,1)S(1)}, u32[]{:S(2)}, u32[]{:S(2)}) %collective-permute-start.12) | collective-permute-done | bytes 131104 | tf_op jit(solution)/shard_map/ppermute | solution.py:37
  69.8 0.7 pair.1
  70.6 0.5 collective-permute-start.4
  71.1 0.7 collective-permute-done.13
  72.1 6.1 %lead.1.refs_0_.after.refs_2_ = f32[8,128,128]{2,1,0:T(8,128)S(1)} custom-call(f32[136,128]{1,0:T(8,128)S(1)} %add.24.refs_0_, f32[136,128]{1,0:T(8,128)S(1)} %collective-permute-done.4.refs_1_, f32[128,128]{1,0:T(8,128)S(1)} %plans_lead.1.refs_2_.after), custom_call_target="tpu_custom_call" | custom-call | bytes 21600000 | tf_op jit(solution)/shard_map/lead/pallas_call | solution.py:435
  78.3 1.1 %collective-permute-start.15 = (f32[128,128]{1,0:T(8,128)S(1)}, f32[128,128]{1,0:T(8,128)S(1)}, u32[]{:S(2)}, u32[]{:S(2)}) collective-permute-start(f32[128,128]{1,0:T(8,128)S(1)} %add.27.a_ref), channel_id=1, source_target_pairs={{0,4},{1,5},{2,6},{3,7},{4,0},{5,1},{6,2},{7,3},{8,12},{9,13},{10,... | collective-permute-start | bytes 196616 | tf_op jit(solution)/shard_map/ppermute | solution.py:37
  79.4 3.2 %collective-permute-done.15.b_ref = f32[128,128]{1,0:T(8,128)S(1)} collective-permute-done((f32[128,128]{1,0:T(8,128)S(1)}, f32[128,128]{1,0:T(8,128)S(1)}, u32[]{:S(2)}, u32[]{:S(2)}) %collective-permute-start.15) | collective-permute-done | bytes 65568 | tf_op jit(solution)/shard_map/ppermute | solution.py:37
  82.6 2.6 %collective-permute-start.16 = (f32[128,128]{1,0:T(8,128)S(1)}, f32[128,128]{1,0:T(8,128)S(1)}, u32[]{:S(2)}, u32[]{:S(2)}) collective-permute-start(f32[128,128]{1,0:T(8,128)S(1)} %add.28.a_ref), channel_id=1, source_target_pairs={{0,8},{1,9},{2,10},{3,11},{4,12},{5,13},{6,14},{7,15},{8,0},{9,1},... | collective-permute-start | bytes 196616 | tf_op jit(solution)/shard_map/ppermute | solution.py:37
  85.2 6.4 %cells.1 = (f32[1024,256]{1,0:T(8,128)}, f32[128,128]{1,0:T(8,128)S(1)}, f32[128,128]{1,0:T(8,128)S(1)}) custom-call(f32[8,128,128]{2,1,0:T(8,128)S(1)} %lead.1.refs_0_.after.refs_2_, bf16[1024,128]{1,0:T(8,128)(2,1)S(1)} %copy-done.2, f32[1024,128]{1,0:T(8,128)S(1)} %copy-done.3), custom_call_target="tpu_custom_call" | custom-call | bytes 28800000 | tf_op jit(solution)/shard_map/cells/pallas_call | solution.py:442
  91.8 0.9 constant_dynamic-slice_fusion.refs_5_
  93.0 6.5 %plans.1 = (f32[512,256]{1,0:T(8,128)}, f32[256,256]{1,0:T(8,128)}) custom-call(f32[128,128]{1,0:T(8,128)S(1)} %add.29.refs_0_, f32[128,128]{1,0:T(8,128)S(1)} %collective-permute-done.17.refs_1_, f32[8,128,128]{2,1,0:T(8,128)S(1)} %lead.1.refs_0_.after.refs_2_, f32[128,128]{1,0:T(8,128)S(1)} %get-tuple-element.53.refs_3_, ...), custom_call_target="tpu_custom_call" | custom-call | tf_op jit(solution)/shard_map/plans/pallas_call | solution.py:464
  (37 shorter events, 2.7 us)
Async XLA Ops:
  22.3 3.0 %collective-permute-start.5 = (bf16[8,512,128]{2,1,0:T(8,128)(2,1)}, bf16[8,512,128]{2,1,0:T(8,128)(2,1)S(1)}, u32[]{:S(2)}, u32[]{:S(2)}) collective-permute-start(bf16[8,512,128]{2,1,0:T(8,128)(2,1)} %get-tuple-element.33), channel_id=1, source_target_pairs={{0,1},{1,0},{2,3},{3,2},{4,5},{5,4},{6,7},{7,6},{8,9},{9,8},{10,11... | collective-permute-start | bytes 3145736 | tf_op jit(solution)/shard_map/ppermute | solution.py:37
  22.8 4.0 %collective-permute-start.6 = (bf16[8,512,128]{2,1,0:T(8,128)(2,1)}, bf16[8,512,128]{2,1,0:T(8,128)(2,1)S(1)}, u32[]{:S(2)}, u32[]{:S(2)}) collective-permute-start(bf16[8,512,128]{2,1,0:T(8,128)(2,1)} %get-tuple-element.35), channel_id=1, source_target_pairs={{0,1},{1,0},{2,3},{3,2},{4,5},{5,4},{6,7},{7,6},{8,9},{9,8},{10,11... | collective-permute-start | bytes 3145736 | tf_op jit(solution)/shard_map/ppermute | solution.py:37
  26.8 1.2 %copy-start = (bf16[8,512,128]{2,1,0:T(8,128)(2,1)S(1)}, bf16[8,512,128]{2,1,0:T(8,128)(2,1)}, u32[]{:S(2)}) copy-start(bf16[8,512,128]{2,1,0:T(8,128)(2,1)} %get-tuple-element.32.keep_l0.keep_l1) | copy-start | bytes 3145732
  28.1 1.2 %copy-start.1 = (bf16[8,512,128]{2,1,0:T(8,128)(2,1)S(1)}, bf16[8,512,128]{2,1,0:T(8,128)(2,1)}, u32[]{:S(2)}) copy-start(bf16[8,512,128]{2,1,0:T(8,128)(2,1)} %get-tuple-element.34.keep_m0.keep_m1) | copy-start | bytes 3145732
  29.3 5.3 %copy-start.4 = (bf16[8192,128]{1,0:T(8,128)(2,1)S(1)}, bf16[8192,128]{1,0:T(8,128)(2,1)}, u32[]{:S(2)}) copy-start(bf16[8192,128]{1,0:T(8,128)(2,1)} %param.7) | copy-start | bytes 6291460
  30.0 15.2 %collective-permute-start.7 = (bf16[4,512,128]{2,1,0:T(8,128)(2,1)S(1)}, bf16[4,512,128]{2,1,0:T(8,128)(2,1)S(1)}, u32[]{:S(2)}, u32[]{:S(2)}) collective-permute-start(bf16[4,512,128]{2,1,0:T(8,128)(2,1)S(1)} %get-tuple-element.39), channel_id=1, source_target_pairs={{0,2},{1,3},{2,0},{3,1},{4,6},{5,7},{6,4},{7,5},{8,10},{9,11},{10,... | collective-permute-start | bytes 1572872 | tf_op jit(solution)/shard_map/ppermute | solution.py:37
  33.0 13.7 %collective-permute-start.8 = (bf16[4,512,128]{2,1,0:T(8,128)(2,1)S(1)}, bf16[4,512,128]{2,1,0:T(8,128)(2,1)S(1)}, u32[]{:S(2)}, u32[]{:S(2)}) collective-permute-start(bf16[4,512,128]{2,1,0:T(8,128)(2,1)S(1)} %get-tuple-element.41), channel_id=1, source_target_pairs={{0,4},{1,5},{2,6},{3,7},{4,0},{5,1},{6,2},{7,3},{8,12},{9,13},{10,... | collective-permute-start | bytes 1572872 | tf_op jit(solution)/shard_map/ppermute | solution.py:37
  35.3 13.7 %copy-start.6 = (f32[136,128]{1,0:T(8,128)S(1)}, f32[136,128]{1,0:T(8,128)}, u32[]{:S(2)}) copy-start(f32[136,128]{1,0:T(8,128)} %get-tuple-element.31) | copy-start | bytes 208900
  35.3 15.0 %copy-start.5 = (f32[136,128]{1,0:T(8,128)S(1)}, f32[136,128]{1,0:T(8,128)}, u32[]{:S(2)}) copy-start(f32[136,128]{1,0:T(8,128)} %get-tuple-element.30) | copy-start | bytes 208900
  46.9 8.0 %collective-permute-start.10 = (bf16[2,512,128]{2,1,0:T(8,128)(2,1)S(1)}, bf16[2,512,128]{2,1,0:T(8,128)(2,1)S(1)}, u32[]{:S(2)}, u32[]{:S(2)}) collective-permute-start(bf16[2,512,128]{2,1,0:T(8,128)(2,1)S(1)} %get-tuple-element.45), channel_id=1, source_target_pairs={{0,2},{1,3},{2,0},{3,1},{4,6},{5,7},{6,4},{7,5},{8,10},{9,11},{10,... | collective-permute-start | bytes 786440 | tf_op jit(solution)/shard_map/ppermute | solution.py:37
  47.3 7.6 %collective-permute-start.9 = (bf16[2,512,128]{2,1,0:T(8,128)(2,1)S(1)}, bf16[2,512,128]{2,1,0:T(8,128)(2,1)S(1)}, u32[]{:S(2)}, u32[]{:S(2)}) collective-permute-start(bf16[2,512,128]{2,1,0:T(8,128)(2,1)S(1)} %get-tuple-element.43), channel_id=1, source_target_pairs={{0,4},{1,5},{2,6},{3,7},{4,0},{5,1},{6,2},{7,3},{8,12},{9,13},{10,... | collective-permute-start | bytes 786440 | tf_op jit(solution)/shard_map/ppermute | solution.py:37
  49.0 1.3 %collective-permute-start = (f32[136,128]{1,0:T(8,128)S(1)}, f32[136,128]{1,0:T(8,128)S(1)}, u32[]{:S(2)}, u32[]{:S(2)}) collective-permute-start(f32[136,128]{1,0:T(8,128)S(1)} %copy-done.6), channel_id=1, source_target_pairs={{0,1},{1,0},{2,3},{3,2},{4,5},{5,4},{6,7},{7,6},{8,9},{9,8},{10,11... | collective-permute-start | bytes 208904 | tf_op jit(solution)/shard_map/ppermute | solution.py:37
  50.3 7.7 %collective-permute-start.1 = (f32[136,128]{1,0:T(8,128)S(1)}, f32[136,128]{1,0:T(8,128)S(1)}, u32[]{:S(2)}, u32[]{:S(2)}) collective-permute-start(f32[136,128]{1,0:T(8,128)S(1)} %add.21), channel_id=1, source_target_pairs={{0,2},{1,3},{2,0},{3,1},{4,6},{5,7},{6,4},{7,5},{8,10},{9,11},{10,... | collective-permute-start | bytes 208904 | tf_op jit(solution)/shard_map/ppermute | solution.py:37
  54.9 30.4 %copy-start.2 = (bf16[1024,128]{1,0:T(8,128)(2,1)S(1)}, bf16[1024,128]{1,0:T(8,128)(2,1)}, u32[]{:S(2)}) copy-start(bf16[1024,128]{1,0:T(8,128)(2,1)} %refs_1_.1) | copy-start | bytes 786436
  54.9 30.4 %copy-start.3 = (f32[1024,128]{1,0:T(8,128)S(1)}, f32[1024,128]{1,0:T(8,128)}, u32[]{:S(2)}) copy-start(f32[1024,128]{1,0:T(8,128)} %get-tuple-element.37.refs_2_) | copy-start | bytes 1572868
  55.0 12.3 %collective-permute-start.11 = (bf16[1,512,128]{2,1,0:T(8,128)(2,1)S(1)}, bf16[1,512,128]{2,1,0:T(8,128)(2,1)S(1)}, u32[]{:S(2)}, u32[]{:S(2)}) collective-permute-start(bf16[1,512,128]{2,1,0:T(8,128)(2,1)S(1)} %get-tuple-element.47), channel_id=1, source_target_pairs={{0,8},{1,9},{2,10},{3,11},{4,12},{5,13},{6,14},{7,15},{8,0},{9,1},... | collective-permute-start | bytes 393224 | tf_op jit(solution)/shard_map/ppermute | solution.py:37
  57.7 12.1 %collective-permute-start.12 = (bf16[1,512,128]{2,1,0:T(8,128)(2,1)S(1)}, bf16[1,512,128]{2,1,0:T(8,128)(2,1)S(1)}, u32[]{:S(2)}, u32[]{:S(2)}) collective-permute-start(bf16[1,512,128]{2,1,0:T(8,128)(2,1)S(1)} %get-tuple-element.49), channel_id=1, source_target_pairs={{0,8},{1,9},{2,10},{3,11},{4,12},{5,13},{6,14},{7,15},{8,0},{9,1},... | collective-permute-start | bytes 393224 | tf_op jit(solution)/shard_map/ppermute | solution.py:37
  58.0 4.8 %collective-permute-start.2 = (f32[136,128]{1,0:T(8,128)S(1)}, f32[136,128]{1,0:T(8,128)S(1)}, u32[]{:S(2)}, u32[]{:S(2)}) collective-permute-start(f32[136,128]{1,0:T(8,128)S(1)} %add.22), channel_id=1, source_target_pairs={{0,4},{1,5},{2,6},{3,7},{4,0},{5,1},{6,2},{7,3},{8,12},{9,13},{10,... | collective-permute-start | bytes 208904 | tf_op jit(solution)/shard_map/ppermute | solution.py:37
  62.8 7.7 %collective-permute-start.3 = (f32[136,128]{1,0:T(8,128)S(1)}, f32[136,128]{1,0:T(8,128)S(1)}, u32[]{:S(2)}, u32[]{:S(2)}) collective-permute-start(f32[136,128]{1,0:T(8,128)S(1)} %add.23), channel_id=1, source_target_pairs={{0,8},{1,9},{2,10},{3,11},{4,12},{5,13},{6,14},{7,15},{8,0},{9,1},... | collective-permute-start | bytes 208904 | tf_op jit(solution)/shard_map/ppermute | solution.py:37
  70.5 1.3 %collective-permute-start.13 = (f32[128,128]{1,0:T(8,128)S(1)}, f32[128,128]{1,0:T(8,128)S(1)}, u32[]{:S(2)}, u32[]{:S(2)}) collective-permute-start(f32[128,128]{1,0:T(8,128)S(1)} %get-tuple-element.51), channel_id=1, source_target_pairs={{0,1},{1,0},{2,3},{3,2},{4,5},{5,4},{6,7},{7,6},{8,9},{9,8},{10,11... | collective-permute-start | bytes 196616 | tf_op jit(solution)/shard_map/ppermute | solution.py:37
  70.6 1.6 %collective-permute-start.4 = (f32[136,128]{1,0:T(8,128)S(1)}, f32[136,128]{1,0:T(8,128)S(1)}, u32[]{:S(2)}, u32[]{:S(2)}) collective-permute-start(f32[136,128]{1,0:T(8,128)S(1)} %add.24.refs_0_), channel_id=1, source_target_pairs={{0,1},{1,0},{2,3},{3,2},{4,5},{5,4},{6,7},{7,6},{8,9},{9,8},{10,11... | collective-permute-start | bytes 208904 | tf_op jit(solution)/shard_map/ppermute | solution.py:37
  71.8 6.5 %collective-permute-start.14 = (f32[128,128]{1,0:T(8,128)S(1)}, f32[128,128]{1,0:T(8,128)S(1)}, u32[]{:S(2)}, u32[]{:S(2)}) collective-permute-start(f32[128,128]{1,0:T(8,128)S(1)} %add.25.a_ref), channel_id=1, source_target_pairs={{0,2},{1,3},{2,0},{3,1},{4,6},{5,7},{6,4},{7,5},{8,10},{9,11},{10,... | collective-permute-start | bytes 196616 | tf_op jit(solution)/shard_map/ppermute | solution.py:37
  78.3 4.3 %collective-permute-start.15 = (f32[128,128]{1,0:T(8,128)S(1)}, f32[128,128]{1,0:T(8,128)S(1)}, u32[]{:S(2)}, u32[]{:S(2)}) collective-permute-start(f32[128,128]{1,0:T(8,128)S(1)} %add.27.a_ref), channel_id=1, source_target_pairs={{0,4},{1,5},{2,6},{3,7},{4,0},{5,1},{6,2},{7,3},{8,12},{9,13},{10,... | collective-permute-start | bytes 196616 | tf_op jit(solution)/shard_map/ppermute | solution.py:37
  82.6 9.1 %collective-permute-start.16 = (f32[128,128]{1,0:T(8,128)S(1)}, f32[128,128]{1,0:T(8,128)S(1)}, u32[]{:S(2)}, u32[]{:S(2)}) collective-permute-start(f32[128,128]{1,0:T(8,128)S(1)} %add.28.a_ref), channel_id=1, source_target_pairs={{0,8},{1,9},{2,10},{3,11},{4,12},{5,13},{6,14},{7,15},{8,0},{9,1},... | collective-permute-start | bytes 196616 | tf_op jit(solution)/shard_map/ppermute | solution.py:37
  91.7 1.3 %collective-permute-start.17 = (f32[128,128]{1,0:T(8,128)S(1)}, f32[128,128]{1,0:T(8,128)S(1)}, u32[]{:S(2)}, u32[]{:S(2)}) collective-permute-start(f32[128,128]{1,0:T(8,128)S(1)} %add.29.refs_0_), channel_id=1, source_target_pairs={{0,1},{1,0},{2,3},{3,2},{4,5},{5,4},{6,7},{7,6},{8,9},{9,8},{10,11... | collective-permute-start | bytes 196616 | tf_op jit(solution)/shard_map/ppermute | solution.py:37
